TPU v7x, 32 devices: a whole 2x2x4 slice. The times are simulated.
32 devices in a mesh: ctx: 16 (over z, y, x), panel: 2 (over core).
Axes of the slice: x: 2, y: 2, z: 4, core: 2. Of those that a mesh axis runs over, the one named last changes fastest.
Arguments:
- se_streams: bfloat16 [3, 2304, 4096], P(None, 'ctx', 'panel'), may hold values from -6 to 6
- se_short: float32 [3, 3, 4096], P(None, None, 'panel'), may hold values from -2 to 2
- se_filter: float32 [7, 4096], P(None, 'panel'), may hold values from -2 to 2
- medium_projected_streams: bfloat16 [3, 2304, 4096], P(None, 'ctx', 'panel'), may hold values from -6 to 6
- mr_short: float32 [3, 3, 4096], P(None, None, 'panel'), may hold values from -2 to 2
- medium_filter_raw: float32 [128, 4096], P(None, 'panel'), may hold values from -0.9 to 0.9
- mr_decay: float32 [4096], P('panel'), may hold values from 0.003 to 0.1
- queries: bfloat16 [2304, 4096], P('ctx', 'panel'), may hold values from -180 to 180
- keys: bfloat16 [2304, 4096], P('ctx', 'panel'), may hold values from -6 to 6
- values: bfloat16 [2304, 4096], P('ctx', 'panel'), may hold values from -6 to 6
Outputs:
- se_out: bfloat16 [2304, 4096], P('ctx', 'panel')
- mr_out: bfloat16 [2304, 4096], P('ctx', 'panel')
- attn_out: bfloat16 [2304, 4096], P('ctx', 'panel')
All inputs are finite; a program needn't handle non-finite values.
Results may differ from a plain program's by a relative error of at most 0.008.
Values may be sent and summed in bfloat16 or wider, within the bound.
No kernel may reach another device: no remote copies, remote signals or barrier semaphores. Data moves between devices by JAX's collectives and lax.ppermute only.
A program may use at most 64 MiB of HBM per device.

v0:
```python
import math

import jax
import jax.numpy as jnp
from jax import lax
from jax.sharding import PartitionSpec as P

CHANNEL_SHARD = 4096
HD = 128
FEATURIZER_TAPS = 3
LSE = 7
MEDIUM_TAPS = 128


def from_behind(value, axis, steps):
    count = lax.axis_size(axis)
    first, last = (max(0, -steps), min(count, count - steps))
    return lax.ppermute(value, axis, [(source, source + steps) for source in range(first, last)])


def featurize(ext, short):
    taps = short.shape[1]
    count = ext.shape[1]
    total = short[:, 0][:, None, :] * ext[:, taps - 1 : count, :].astype(jnp.float32)
    for j in range(1, taps):
        total = total + short[:, j][:, None, :] * ext[:, taps - 1 - j : count - j, :].astype(
            jnp.float32
        )
    return total


def long_conv(product, filt):
    channels = filt.shape[1]
    reversed_taps = filt[::-1][:, None, :]
    signal = product.astype(jnp.float32)[None]
    result = lax.conv_general_dilated(
        signal,
        reversed_taps,
        (1,),
        "VALID",
        dimension_numbers=("NWC", "WIO", "NWC"),
        feature_group_count=channels,
        precision=lax.Precision.HIGHEST,
    )
    return result[0]


def attend(qblk, kblk, value_block, qpos, kpos):
    heads = qblk.shape[1] // HD
    q3 = qblk.reshape(-1, heads, HD)
    k3 = kblk.reshape(-1, heads, HD)
    v3 = value_block.reshape(-1, heads, HD)
    scores = jnp.einsum("qhd,khd->hqk", q3, k3, preferred_element_type=jnp.float32) * (
        1.0 / math.sqrt(HD)
    )
    valid = (kpos[None, :] >= 0) & (kpos[None, :] <= qpos[:, None])
    masked = jnp.where(valid[None], scores, -1e30)
    top = jnp.max(masked, axis=-1, keepdims=True)
    raw = jnp.exp(masked - top)
    total = jnp.sum(raw, axis=-1)
    probs = raw.astype(jnp.bfloat16)
    out = jnp.einsum("hqk,khd->qhd", probs, v3, preferred_element_type=jnp.float32)
    out = out / total.T[:, :, None]
    return out.reshape(qblk.shape[0], -1)


def body(
    se_streams,
    se_short,
    se_filter,
    medium_projected_streams,
    mr_short,
    medium_filter_raw,
    mr_decay,
    queries,
    keys,
    values,
):
    token_rows = se_streams.shape[1]
    step_index = jnp.arange(MEDIUM_TAPS, dtype=jnp.float32)
    mr_taps = medium_filter_raw * jnp.exp(-mr_decay[None, :] * step_index[:, None])
    se_rim, mr_rim = from_behind(
        (
            se_streams[:, token_rows - (FEATURIZER_TAPS - 1) :, :],
            medium_projected_streams[:, token_rows - (FEATURIZER_TAPS - 1) :, :],
        ),
        "ctx",
        1,
    )
    se_feats = featurize(jnp.concatenate([se_rim, se_streams], axis=1), se_short)
    mr_feats = featurize(jnp.concatenate([mr_rim, medium_projected_streams], axis=1), mr_short)
    se_own = (se_feats[1] * se_feats[2]).astype(jnp.bfloat16)
    mr_own = (mr_feats[1] * mr_feats[2]).astype(jnp.bfloat16)
    se_back, mr_back = from_behind(
        (se_own[token_rows - (LSE - 1) :], mr_own[token_rows - (MEDIUM_TAPS - 1) :]), "ctx", 1
    )
    se_prod = jnp.concatenate([se_back, se_own], axis=0)
    mr_prod = jnp.concatenate([mr_back, mr_own], axis=0)
    se_mix = se_feats[0] * long_conv(se_prod, se_filter)
    mr_mix = mr_feats[0] * long_conv(mr_prod, mr_taps)
    key_prev, value_prev = from_behind((keys, values), "ctx", 1)
    start_offset = lax.axis_index("ctx") * token_rows
    local = jnp.arange(token_rows, dtype=jnp.int32)
    wide = jnp.arange(2 * token_rows, dtype=jnp.int32)
    attn_mix = attend(
        queries,
        jnp.concatenate([key_prev, keys], axis=0),
        jnp.concatenate([value_prev, values], axis=0),
        start_offset + local,
        start_offset - token_rows + wide,
    )
    sums = lax.psum(
        (
            jnp.sum(se_mix * se_mix, axis=-1),
            jnp.sum(mr_mix * mr_mix, axis=-1),
            jnp.sum(attn_mix * attn_mix, axis=-1),
        ),
        "panel",
    )
    outputs = []
    for mixed, square in zip((se_mix, mr_mix, attn_mix), sums):
        scale = lax.rsqrt(square / CHANNEL_SHARD + 1e-06)
        outputs.append((mixed * scale[:, None]).astype(jnp.bfloat16))
    return (outputs[0], outputs[1], outputs[2])


def solution(mesh):
    placed = (
        P(None, "ctx", "panel"),
        P(None, None, "panel"),
        P(None, "panel"),
        P(None, "ctx", "panel"),
        P(None, None, "panel"),
        P(None, "panel"),
        P("panel"),
        P("ctx", "panel"),
        P("ctx", "panel"),
        P("ctx", "panel"),
    )
    return jax.shard_map(
        body,
        mesh=mesh,
        in_specs=placed,
        out_specs=(P("ctx", "panel"), P("ctx", "panel"), P("ctx", "panel")),
        check_vma=False,
    )
```

profile of v0, /device:TPU:9, one launch (start us, length us, event | category | flops | bytes accessed | tf_op | source)
XLA Modules:
  0.0 103.1 jit_solution(12158412768205350920)
XLA Ops:
  0.6 1.6 %slice.68 = bf16[3,2,2048]{2,1,0:T(2,128)(2,1)} slice(bf16[3,144,2048]{2,1,0:T(8,128)(2,1)} %param.10), slice={[0:3], [142:144], [0:2048]} | slice | bytes 49152 | tf_op jit(solution)/shard_map/slice | solution.py:84
  2.2 3.1 %collective-permute-start = (bf16[3,2,2048]{2,1,0:T(2,128)(2,1)}, bf16[3,2,2048]{2,1,0:T(2,128)(2,1)}, u32[]{:S(2)}, u32[]{:S(2)}) collective-permute-start(bf16[3,2,2048]{2,1,0:T(2,128)(2,1)} %slice.68), channel_id=1, source_target_pairs={{0,2},{2,4},{4,6},{6,8},{8,10},{10,12},{12,14},{14,16},{16,18},{18... | collective-permute-start | bytes 73736 | tf_op jit(solution)/shard_map/ppermute | solution.py:18
  6.9 3.1 %collective-permute-start.2 = (bf16[3,2,2048]{2,0,1:T(4,128)(2,1)}, bf16[3,2,2048]{2,0,1:T(4,128)(2,1)}, u32[]{:S(2)}, u32[]{:S(2)}) collective-permute-start(bf16[3,2,2048]{2,0,1:T(4,128)(2,1)} %copy.107), channel_id=1, source_target_pairs={{0,2},{2,4},{4,6},{6,8},{8,10},{10,12},{12,14},{14,16},{16,18},{18... | collective-permute-start | bytes 73736 | tf_op jit(solution)/shard_map/ppermute | solution.py:18
  10.0 3.1 %collective-permute-start.5 = (bf16[144,2048]{1,0:T(8,128)(2,1)}, bf16[144,2048]{1,0:T(8,128)(2,1)}, u32[]{:S(2)}, u32[]{:S(2)}) collective-permute-start(bf16[144,2048]{1,0:T(8,128)(2,1)} %param.18), channel_id=1, source_target_pairs={{0,2},{2,4},{4,6},{6,8},{8,10},{10,12},{12,14},{14,16},{16,18},{18... | collective-permute-start | bytes 1769480 | tf_op jit(solution)/shard_map/ppermute | solution.py:18
  13.2 3.1 %collective-permute-start.4 = (bf16[144,2048]{1,0:T(8,128)(2,1)}, bf16[144,2048]{1,0:T(8,128)(2,1)}, u32[]{:S(2)}, u32[]{:S(2)}) collective-permute-start(bf16[144,2048]{1,0:T(8,128)(2,1)} %param.19), channel_id=1, source_target_pairs={{0,2},{2,4},{4,6},{6,8},{8,10},{10,12},{12,14},{14,16},{16,18},{18... | collective-permute-start | bytes 1769480 | tf_op jit(solution)/shard_map/ppermute | solution.py:18
  17.6 1.1 %fusion.53 = (f32[3,1,2048]{2,1,0:T(1,128)S(1)}, f32[3,1,2048]{2,1,0:T(1,128)S(1)}, f32[3,1,2048]{2,1,0:T(1,128)S(1)}) fusion(f32[3,3,2048]{2,1,0:T(4,128)} %param.11), kind=kLoop, calls=%fused_computation.83 | loop fusion | bytes 147456 | tf_op jit(solution)/shard_map/slice | solution.py:24
  18.7 1.7 %fusion.52 = (f32[3,1,2048]{2,1,0:T(1,128)}, f32[3,1,2048]{2,1,0:T(1,128)S(1)}, f32[3,1,2048]{2,1,0:T(1,128)S(1)}) fusion(f32[3,3,2048]{2,1,0:T(4,128)} %param.14), kind=kLoop, calls=%fused_computation.82 | loop fusion | bytes 147456 | tf_op jit(solution)/shard_map/slice | solution.py:24
  21.1 1.5 %exponential_multiply_fusion = f32[128,2048]{1,0:T(8,128)S(1)} fusion(f32[128,2048]{1,0:T(8,128)} %param.15, f32[2048]{0:T(1024)S(1)} %neg.4), kind=kLoop, calls=%fused_computation.47 | loop fusion | flops 524288 | bytes 2105344 | tf_op jit(solution)/shard_map/mul | solution.py:81
  22.7 7.7 %rev.6 = f32[7,2048]{1,0:T(8,128)} reverse(f32[7,2048]{1,0:T(8,128)} %param.12), dimensions={0} | reverse | bytes 114688 | tf_op jit(solution)/shard_map/rev | solution.py:34
  31.0 1.4 %copy.116 = f32[3,1,2048]{2,0,1:T(4,128)} copy(f32[3,1,2048]{2,1,0:T(1,128)} %get-tuple-element.6) | data formatting | bytes 49152
  32.4 5.3 %rev.7 = f32[128,2048]{1,0:T(8,128)} reverse(f32[128,2048]{1,0:T(8,128)S(1)} %exponential_multiply_fusion), dimensions={0} | reverse | bytes 2097152 | tf_op jit(solution)/shard_map/rev | solution.py:34
  38.5 1.7 %constant_dynamic-update-slice_fusion = bf16[3,146,2048]{2,0,1:T(4,128)(2,1)S(1)} fusion(bf16[3,146,2048]{2,0,1:T(4,128)(2,1)S(1)} %constant_dynamic-update-slice_fusion.1, bf16[3,144,2048]{2,1,0:T(8,128)(2,1)S(1)} %copy-done.3), kind=kLoop, calls=%fused_computation.69 | loop fusion | bytes 4128768 | tf_op jit(solution)/shard_map/concatenate | solution.py:91
  40.2 3.0 %multiply_add_fusion = f32[3,144,2048]{2,0,1:T(4,128)S(1)} fusion(bf16[3,146,2048]{2,0,1:T(4,128)(2,1)S(1)} %constant_dynamic-update-slice_fusion, f32[3,2048]{1,0:T(4,128)S(1)} %copy-done.8, f32[3,2048]{1,0:T(4,128)S(1)} %copy-done.9, f32[3,2048]{1,0:T(4,128)S(1)} %bitcast.105, bf16[3,144,2048]{2,1,0:T(8,128)(2,1)S(1)} %copy-done.3), kind=kLoop, calls=%fused_computation | loop fusion | flops 7077888 | bytes 8921088 | tf_op jit(solution)/shard_map/add | solution.py:26
  43.3 1.8 %fusion.22 = bf16[1,144,2048]{2,0,1:T(2,128)(2,1)S(1)} fusion(f32[3,144,2048]{2,0,1:T(4,128)S(1)} %multiply_add_fusion), kind=kLoop, calls=%fused_computation.30 | loop fusion | flops 589824 | bytes 2949120 | tf_op jit(solution)/shard_map/convert_element_type | solution.py:93
  45.1 0.9 copy-done.5
  46.1 2.1 %multiply_add_fusion.1 = f32[3,144,2048]{2,1,0:T(8,128)S(1)} fusion(bf16[3,144,2048]{2,1,0:T(8,128)(2,1)S(1)} %copy-done.5, bf16[3,2,2048]{2,1,0:T(2,128)(2,1)} %collective-permute-done, f32[3,2048]{1,0:T(4,128)S(1)} %get-tuple-element.16, f32[3,2048]{1,0:T(4,128)S(1)} %get-tuple-element.17, f32[3,2048]{1,0:T(4,128)S(1)} %bitcast.104), kind=kLoop, calls=%fused_computation.3 | loop fusion | flops 12386304 | bytes 5406720 | tf_op jit(solution)/shard_map/add | solution.py:26
  48.4 3.1 %collective-permute-start.1 = (bf16[6,2048]{1,0:T(8,128)(2,1)S(1)}, bf16[6,2048]{1,0:T(8,128)(2,1)S(1)}, u32[]{:S(2)}, u32[]{:S(2)}) collective-permute-start(bf16[6,2048]{1,0:T(8,128)(2,1)S(1)} %slice_bitcast_fusion), channel_id=1, source_target_pairs={{0,2},{2,4},{4,6},{6,8},{8,10},{10,12},{12,14},{14,16},{16,18},{18... | collective-permute-start | bytes 73736 | tf_op jit(solution)/shard_map/ppermute | solution.py:18
  51.7 1.2 %copy.114 = bf16[1,144,2048]{2,1,0:T(8,128)(2,1)} copy(bf16[1,144,2048]{2,0,1:T(2,128)(2,1)S(1)} %fusion.22) | data formatting | bytes 1179648
  52.8 1.1 %slice.104 = bf16[1,127,2048]{2,0,1:T(2,128)(2,1)S(1)} slice(bf16[1,144,2048]{2,0,1:T(2,128)(2,1)S(1)} %fusion.22), slice={[0:1], [17:144], [0:2048]} | slice | bytes 1040384 | tf_op jit(solution)/shard_map/slice | solution.py:95
  53.9 1.1 %copy.115 = bf16[1,127,2048]{2,1,0:T(8,128)(2,1)} copy(bf16[1,127,2048]{2,0,1:T(2,128)(2,1)S(1)} %slice.104) | data formatting | bytes 1040384
  55.0 3.3 %collective-permute-start.3 = (bf16[127,2048]{1,0:T(8,128)(2,1)}, bf16[127,2048]{1,0:T(8,128)(2,1)}, u32[]{:S(2)}, u32[]{:S(2)}) collective-permute-start(bf16[127,2048]{1,0:T(8,128)(2,1)} %bitcast.99), channel_id=1, source_target_pairs={{0,2},{2,4},{4,6},{6,8},{8,10},{10,12},{12,14},{14,16},{16,18},{18... | collective-permute-start | bytes 1560584 | tf_op jit(solution)/shard_map/ppermute | solution.py:18
  61.0 1.7 %multiply_reduce_fusion.1 = f32[144]{0:T(256)S(1)} fusion(f32[1,152,2048]{2,1,0:T(8,128)S(1)} %reshape.97, f32[3,144,2048]{2,1,0:T(8,128)} %copy-done.1), kind=kLoop, calls=%fused_computation.44 | loop fusion | flops 884592 | bytes 2359872 | tf_op jit(solution)/shard_map/reduce_sum | solution.py:114
  62.6 7.7 %collective-permute-done.3 = bf16[127,2048]{1,0:T(8,128)(2,1)} collective-permute-done((bf16[127,2048]{1,0:T(8,128)(2,1)}, bf16[127,2048]{1,0:T(8,128)(2,1)}, u32[]{:S(2)}, u32[]{:S(2)}) %collective-permute-start.3) | collective-permute-done | bytes 520224 | tf_op jit(solution)/shard_map/ppermute | solution.py:18
  70.3 1.2 %maximum_bitcast_fusion.2 = bf16[1,271,2048]{2,1,0:T(8,128)(2,1)S(1)} fusion(bf16[144,2048]{1,0:T(8,128)(2,1)S(1)} %bitcast.102, bf16[127,2048]{1,0:T(8,128)(2,1)} %collective-permute-done.3), kind=kLoop, calls=%fused_computation.45 | loop fusion | flops 2220032 | bytes 2220032 | tf_op jit(solution)/shard_map/broadcast_in_dim | solution.py:35
  71.6 14.3 %slice_multiply_fusion.1 = f32[1,144,2048]{2,0,1:T(1,128)S(1)} fusion(f32[3,144,2048]{2,0,1:T(4,128)} %copy-done.2, f32[128,1,2048]{2,0,1:T(8,128)S(1)} %bitcast.103, bf16[1,271,2048]{2,1,0:T(8,128)(2,1)S(1)} %maximum_bitcast_fusion.2), kind=kOutput, calls=%fused_computation.31 | convolution fusion | flops 453279744 | bytes 4517888 | tf_op jit(solution)/shard_map/conv_general_dilated | solution.py:36
  86.3 2.1 %fusion.2 = (f32[16,144]{1,0:T(8,128)S(1)}, f32[16,288,144]{1,2,0:T(8,128)S(1)}) fusion(pred[144,288]{1,0:T(8,128)(4,1)S(1)} %compare_and_fusion, bf16[144,2048]{1,0:T(8,128)(2,1)S(1)} %copy-done.14, bf16[144,2048]{1,0:T(8,128)(2,1)} %collective-permute-done.5, bf16[144,2048]{1,0:T(8,128)(2,1)S(1)} %copy-done), kind=kOutput, calls=%fused_computation.6 | convolution fusion | flops 174216960 | bytes 4474368 | tf_op jit(solution)/shard_map/qhd,khd->hqk/dot_general | solution.py:53
  88.4 1.5 %fusion = f32[16,144]{1,0:T(8,128)S(1)} fusion(f32[16,288,144]{1,2,0:T(8,128)S(1)} %get-tuple-element.13, f32[16,144]{1,0:T(8,128)S(1)} %get-tuple-element.12, pred[144,288]{1,0:T(8,128)(4,1)S(1)} %compare_and_fusion), kind=kLoop, calls=%fused_computation.4 | loop fusion | flops 2651904 | bytes 2714112 | tf_op jit(solution)/shard_map/reduce_sum | solution.py:60
  89.9 3.6 %multiply_reduce_fusion = (f32[144]{0:T(256)S(1)}, f32[144,16,128]{2,0,1:T(8,128)}) fusion(f32[144,16]{0,1:T(8,128)S(1)} %bitcast.107, f32[16,288,144]{1,2,0:T(8,128)S(1)} %get-tuple-element.13, f32[16,144]{1,0:T(8,128)S(1)} %get-tuple-element.12, pred[144,288]{1,0:T(8,128)(4,1)S(1)} %compare_and_fusion, bf16[144,2048]{1,0:T(8,128)(2,1)S(1)} %copy-done.15, ...), kind=kOutput, calls=%fused_computation.42 | convolution fusion | flops 175767408 | bytes 5073984 | tf_op jit(solution)/shard_map/hqk,khd->qhd/dot_general | solution.py:62
  93.5 5.1 %all-reduce = (f32[144]{0:T(256)S(1)}, f32[144]{0:T(256)S(1)}, f32[144]{0:T(256)S(1)}) all-reduce(f32[144]{0:T(256)S(1)} %multiply_reduce_fusion.1, f32[144]{0:T(256)S(1)} %fusion.25, f32[144]{0:T(256)S(1)} %get-tuple-element.14), channel_id=1, replica_groups=mesh['ctx'=16,'panel'=2] {'panel'}, use_global_device_ids=true, to_apply=%region_1.2 | all-reduce | flops 432 | bytes 3456 | tf_op jit(solution)/shard_map/psum | solution.py:112
  98.6 2.4 %multiply_convert_fusion = bf16[144,2048]{1,0:T(8,128)(2,1)} fusion(f32[144]{0:T(256)S(1)} %add_rsqrt_fusion.2, f32[1,152,2048]{2,1,0:T(8,128)S(1)} %reshape.97, f32[3,144,2048]{2,1,0:T(8,128)} %copy-done.1), kind=kLoop, calls=%fused_computation.43 | loop fusion | flops 884736 | bytes 2949696 | tf_op jit(solution)/shard_map/convert_element_type | solution.py:123
  101.0 1.2 %fusion.26 = bf16[144,2048]{1,0:T(8,128)(2,1)} fusion(f32[1,144,2048]{2,0,1:T(1,128)S(1)} %slice_multiply_fusion.1, f32[144]{0:T(256)S(1)} %add_rsqrt_fusion.1), kind=kLoop, calls=%fused_computation.41 | loop fusion | flops 589824 | bytes 1770048 | tf_op jit(solution)/shard_map/convert_element_type | solution.py:123
  102.2 0.9 fusion.16
  (64 shorter events, 8.3 us)
Async XLA Ops:
  0.6 85.6 %copy-start = (bf16[144,2048]{1,0:T(8,128)(2,1)S(1)}, bf16[144,2048]{1,0:T(8,128)(2,1)}, u32[]{:S(2)}) copy-start(bf16[144,2048]{1,0:T(8,128)(2,1)} %param.17) | copy-start | bytes 1769476
  2.2 42.9 %collective-permute-start = (bf16[3,2,2048]{2,1,0:T(2,128)(2,1)}, bf16[3,2,2048]{2,1,0:T(2,128)(2,1)}, u32[]{:S(2)}, u32[]{:S(2)}) collective-permute-start(bf16[3,2,2048]{2,1,0:T(2,128)(2,1)} %slice.68), channel_id=1, source_target_pairs={{0,2},{2,4},{4,6},{6,8},{8,10},{10,12},{12,14},{14,16},{16,18},{18... | collective-permute-start | bytes 73736 | tf_op jit(solution)/shard_map/ppermute | solution.py:18
  6.9 30.8 %collective-permute-start.2 = (bf16[3,2,2048]{2,0,1:T(4,128)(2,1)}, bf16[3,2,2048]{2,0,1:T(4,128)(2,1)}, u32[]{:S(2)}, u32[]{:S(2)}) collective-permute-start(bf16[3,2,2048]{2,0,1:T(4,128)(2,1)} %copy.107), channel_id=1, source_target_pairs={{0,2},{2,4},{4,6},{6,8},{8,10},{10,12},{12,14},{14,16},{16,18},{18... | collective-permute-start | bytes 73736 | tf_op jit(solution)/shard_map/ppermute | solution.py:18
  10.0 76.3 %collective-permute-start.5 = (bf16[144,2048]{1,0:T(8,128)(2,1)}, bf16[144,2048]{1,0:T(8,128)(2,1)}, u32[]{:S(2)}, u32[]{:S(2)}) collective-permute-start(bf16[144,2048]{1,0:T(8,128)(2,1)} %param.18), channel_id=1, source_target_pairs={{0,2},{2,4},{4,6},{6,8},{8,10},{10,12},{12,14},{14,16},{16,18},{18... | collective-permute-start | bytes 1769480 | tf_op jit(solution)/shard_map/ppermute | solution.py:18
  13.2 76.7 %collective-permute-start.4 = (bf16[144,2048]{1,0:T(8,128)(2,1)}, bf16[144,2048]{1,0:T(8,128)(2,1)}, u32[]{:S(2)}, u32[]{:S(2)}) collective-permute-start(bf16[144,2048]{1,0:T(8,128)(2,1)} %param.19), channel_id=1, source_target_pairs={{0,2},{2,4},{4,6},{6,8},{8,10},{10,12},{12,14},{14,16},{16,18},{18... | collective-permute-start | bytes 1769480 | tf_op jit(solution)/shard_map/ppermute | solution.py:18
  16.9 5.8 %copy-start.13 = (s32[144]{0:T(256)S(1)}, s32[144]{0:T(256)}, u32[]{:S(2)}) copy-start(s32[144]{0:T(256)} %iota_add_fusion.1) | copy-start | bytes 1732
  21.1 17.4 %copy-start.3 = (bf16[3,144,2048]{2,1,0:T(8,128)(2,1)S(1)}, bf16[3,144,2048]{2,1,0:T(8,128)(2,1)}, u32[]{:S(2)}) copy-start(bf16[3,144,2048]{2,1,0:T(8,128)(2,1)} %param.13) | copy-start | bytes 5308420
  38.5 1.7 %copy-start.8 = (f32[3,2048]{1,0:T(4,128)S(1)}, f32[3,2048]{1,0:T(4,128)}, u32[]{:S(2)}) copy-start(f32[3,2048]{1,0:T(4,128)} %get-tuple-element.18) | copy-start | bytes 73732
  38.5 1.7 %copy-start.9 = (f32[3,2048]{1,0:T(4,128)S(1)}, f32[3,2048]{1,0:T(4,128)}, u32[]{:S(2)}) copy-start(f32[3,2048]{1,0:T(4,128)} %get-tuple-element.19) | copy-start | bytes 73732
  38.5 1.7 %copy-start.11 = (f32[3,1,2048]{2,0,1:T(4,128)S(1)}, f32[3,1,2048]{2,0,1:T(4,128)}, u32[]{:S(2)}) copy-start(f32[3,1,2048]{2,0,1:T(4,128)} %copy.116) | copy-start | bytes 73732
  43.3 5.1 %copy-start.2 = (f32[3,144,2048]{2,0,1:T(4,128)}, f32[3,144,2048]{2,0,1:T(4,128)S(1)}, u32[]{:S(2)}) copy-start(f32[3,144,2048]{2,0,1:T(4,128)S(1)} %multiply_add_fusion) | copy-start | bytes 10616836
  43.3 2.8 %copy-start.5 = (bf16[3,144,2048]{2,1,0:T(8,128)(2,1)S(1)}, bf16[3,144,2048]{2,1,0:T(8,128)(2,1)}, u32[]{:S(2)}) copy-start(bf16[3,144,2048]{2,1,0:T(8,128)(2,1)} %param.10) | copy-start | bytes 5308420
  43.3 2.8 %copy-start.10 = (f32[3,1,2048]{2,0,1:T(4,128)S(1)}, f32[3,1,2048]{2,0,1:T(4,128)}, u32[]{:S(2)}) copy-start(f32[3,1,2048]{2,0,1:T(4,128)} %copy.117) | copy-start | bytes 73732
  48.2 3.4 %copy-start.1 = (f32[3,144,2048]{2,1,0:T(8,128)}, f32[3,144,2048]{2,1,0:T(8,128)S(1)}, u32[]{:S(2)}) copy-start(f32[3,144,2048]{2,1,0:T(8,128)S(1)} %multiply_add_fusion.1) | copy-start | bytes 10616836
  48.4 9.9 %collective-permute-start.1 = (bf16[6,2048]{1,0:T(8,128)(2,1)S(1)}, bf16[6,2048]{1,0:T(8,128)(2,1)S(1)}, u32[]{:S(2)}, u32[]{:S(2)}) collective-permute-start(bf16[6,2048]{1,0:T(8,128)(2,1)S(1)} %slice_bitcast_fusion), channel_id=1, source_target_pairs={{0,2},{2,4},{4,6},{6,8},{8,10},{10,12},{12,14},{14,16},{16,18},{18... | collective-permute-start | bytes 73736 | tf_op jit(solution)/shard_map/ppermute | solution.py:18
  55.0 15.3 %collective-permute-start.3 = (bf16[127,2048]{1,0:T(8,128)(2,1)}, bf16[127,2048]{1,0:T(8,128)(2,1)}, u32[]{:S(2)}, u32[]{:S(2)}) collective-permute-start(bf16[127,2048]{1,0:T(8,128)(2,1)} %bitcast.99), channel_id=1, source_target_pairs={{0,2},{2,4},{4,6},{6,8},{8,10},{10,12},{12,14},{14,16},{16,18},{18... | collective-permute-start | bytes 1560584 | tf_op jit(solution)/shard_map/ppermute | solution.py:18
  58.5 0.8 copy-start.12
  58.5 0.8 copy-start.16
  60.9 9.4 %copy-start.4 = (bf16[1,144,2048]{2,1,0:T(8,128)(2,1)S(1)}, bf16[1,144,2048]{2,1,0:T(8,128)(2,1)}, u32[]{:S(2)}) copy-start(bf16[1,144,2048]{2,1,0:T(8,128)(2,1)} %copy.114) | copy-start | bytes 1769476
  61.0 10.6 %copy-start.7 = (f32[128,2048]{1,0:T(8,128)S(1)}, f32[128,2048]{1,0:T(8,128)}, u32[]{:S(2)}) copy-start(f32[128,2048]{1,0:T(8,128)} %rev.7) | copy-start | bytes 3145732
  71.6 14.7 %copy-start.14 = (bf16[144,2048]{1,0:T(8,128)(2,1)S(1)}, bf16[144,2048]{1,0:T(8,128)(2,1)}, u32[]{:S(2)}) copy-start(bf16[144,2048]{1,0:T(8,128)(2,1)} %param.18) | copy-start | bytes 1769476
  88.4 1.5 %copy-start.15 = (bf16[144,2048]{1,0:T(8,128)(2,1)S(1)}, bf16[144,2048]{1,0:T(8,128)(2,1)}, u32[]{:S(2)}) copy-start(bf16[144,2048]{1,0:T(8,128)(2,1)} %param.19) | copy-start | bytes 1769476
  98.6 3.6 %copy-start.6 = (f32[144,16,128]{2,0,1:T(8,128)S(1)}, f32[144,16,128]{2,0,1:T(8,128)}, u32[]{:S(2)}) copy-start(f32[144,16,128]{2,0,1:T(8,128)} %get-tuple-element.15) | copy-start | bytes 3538948
where the time goes:
time: 104 us; the launch traced here: 103 us
  local copies, waits for them, and re-layouts  30.1 us (29%)
  matrix products  20.6 us (20%)
  other arithmetic  19.6 us (19%)
  starting transfers between devices  18.9 us (18%)
  waiting for transfers between devices  7.71 us (7%)
  blocking collectives  5.11 us (5%)
  between operations  1.07 us (1%)
    ppermute x6, starting transfers between devices, from_behind(): lax.ppermute(value, axis, [(source, source + steps) for source in range(f...  18.9 us
    conv_general_dilated x2, matrix products, long_conv(): lax.conv_general_dilated(signal, reversed_taps, (1,), 'VALID', dimension_...  15 us
    rev x2, local copies, waits for them, and re-layouts, long_conv(): reversed_taps = filt[::-1][:, None, :]  13 us
    ppermute x6, waiting for transfers between devices, from_behind(): lax.ppermute(value, axis, [(source, source + steps) for source in range(f...  7.71 us
    unnamed x42, local copies, waits for them, and re-layouts  7.51 us
    add x2, other arithmetic, featurize(): total + short[:, j][:, None, :] * ext[:, taps - 1 - j:count - j, :].astyp...  5.18 us
    psum x1, blocking collectives, body(): lax.psum((jnp.sum(se_mix * se_mix, axis=-1), jnp.sum(mr_mix * mr_mix, axi...  5.11 us
    convert_element_type x3, other arithmetic, body(): outputs.append((mixed * scale[:, None]).astype(jnp.bfloat16))  4.52 us
  transfers between devices with their start and end apart: 6, of which 1 were waited for; matrix products, arithmetic and copies ran while one was open for 58% of the time, Pallas kernels for 0%

commit v1 on v0

v1 whole, which is shorter than its diff:
```python
import functools
import math

import jax
import jax.numpy as jnp
from jax import lax
from jax.experimental import pallas as pl
from jax.experimental.pallas import tpu as pltpu
from jax.sharding import PartitionSpec as P

CHANNELS = 4096
HD = 128
LSE = 7
MEDIUM_TAPS = 128
LANES = 128
F32 = jnp.float32
BF16 = jnp.bfloat16


def params():
    return pltpu.CompilerParams(
        dimension_semantics=("arbitrary",), vmem_limit_bytes=40 * 1024 * 1024
    )


def cost(flops, nbytes, trans=0):
    return pl.CostEstimate(flops=int(flops), bytes_accessed=int(nbytes), transcendentals=int(trans))


def roll(value, shift):
    shift = shift % value.shape[0]
    return pltpu.roll(value, shift, 0) if shift else value


def row_is(rows, at):
    return lax.broadcasted_iota(jnp.int32, (rows, LANES), 0) == at


def features(u, front, taps):
    ext = jnp.concatenate([front, u], axis=0)
    total = taps[0] * ext
    for j in range(1, len(taps)):
        total = total + taps[j] * roll(ext, j)
    return total[8:]


def tap_rows(ref, stream, lanes):
    return [ref[stream, j : j + 1, lanes] for j in range(ref.shape[1])]


def lane_block(k):
    return pl.ds(pl.multiple_of(k * LANES, LANES), LANES)


def write_taps(taps_ref, raw_ref, decay_ref, lanes):
    steps = lax.broadcasted_iota(jnp.int32, (MEDIUM_TAPS, LANES), 0).astype(F32)
    taps = raw_ref[:, lanes] * jnp.exp(-decay_ref[0:1, lanes] * steps)
    taps_ref[...] = taps
    return taps


def tap_tile(taps_ref, j):
    return jnp.broadcast_to(taps_ref[j : j + 1, :], (8, LANES))


def pack_kernel(per, m1_ref, m2_ref, m0t_ref, s0t_ref, s1t_ref, s2t_ref, mw_ref, sw_ref, out_ref, last_ref):
    step = pl.program_id(0)
    rows = m1_ref.shape[1]
    chunk = MEDIUM_TAPS + 16
    nothing = jnp.zeros((8, LANES), F32)

    @pl.when(step == 0)
    def _():
        last_ref[...] = jnp.zeros_like(last_ref)

    @pl.loop(0, per)
    def _(k):
        lanes = lane_block(k)
        block = step * per + k
        m1 = m1_ref[0, :, lanes].astype(F32)
        m2 = m2_ref[0, :, lanes].astype(F32)
        z1 = features(m1, nothing, tap_rows(mw_ref, 1, lanes))
        z2 = features(m2, nothing, tap_rows(mw_ref, 2, lanes))
        product = (z1 * z2)[rows - MEDIUM_TAPS :]
        tail_m0 = m0t_ref[0, :, lanes].astype(F32)[8:]
        tail_m1, tail_m2 = m1[rows - 8 :], m2[rows - 8 :]
        head = jnp.where(row_is(8, 0), roll(tail_m2, 2), product[:8])
        product = jnp.concatenate([head, product[8:]], axis=0)
        s0 = s0t_ref[0, :, lanes].astype(F32)[8:]
        s1 = s1t_ref[0, :, lanes].astype(F32)
        s2 = s2t_ref[0, :, lanes].astype(F32)
        y1 = features(s1, nothing, tap_rows(sw_ref, 1, lanes))[8:]
        y2 = features(s2, nothing, tap_rows(sw_ref, 2, lanes))[8:]
        at = lax.broadcasted_iota(jnp.int32, (8, LANES), 0)
        x1 = jnp.where(at < 2, roll(s0, 2), y1 * y2)
        x2 = jnp.where(
            at < 2,
            roll(s1[8:], 2),
            jnp.where(at < 4, roll(s2[8:], 4), jnp.where(at < 6, roll(tail_m0, 6), tail_m1)),
        )
        start = pl.multiple_of(block * chunk, 16)
        out_ref[pl.ds(start, MEDIUM_TAPS), :] = product.astype(BF16)
        out_ref[pl.ds(start + MEDIUM_TAPS, 16), :] = jnp.concatenate([x1, x2], axis=0).astype(BF16)
        last_ref[pl.ds(block, 1), :] = tail_m2[7:8]

    out_ref[out_ref.shape[0] - 16 :, :] = last_ref[...].astype(BF16)


def pack(se, mr, se_short, mr_short, per):
    _, rows, channels = se.shape
    blocks = channels // LANES
    total = blocks * (MEDIUM_TAPS + 16) + 16
    width = per * LANES
    whole = lambda s: pl.BlockSpec((1, rows, width), lambda i: (s, 0, i))
    tail = lambda s: pl.BlockSpec((1, 16, width), lambda i: (s, rows // 16 - 1, i))
    short = pl.BlockSpec((3, 3, width), lambda i: (0, 0, i))
    return pl.pallas_call(
        functools.partial(pack_kernel, per),
        grid=(blocks // per,),
        out_shape=jax.ShapeDtypeStruct((total, LANES), BF16),
        in_specs=[whole(1), whole(2), tail(0), tail(0), tail(1), tail(2), short, short],
        out_specs=pl.BlockSpec((total, LANES), lambda i: (0, 0)),
        scratch_shapes=[pltpu.VMEM((16, LANES), F32)],
        compiler_params=params(),
        cost_estimate=cost(20 * rows * channels, 6 * rows * channels),
        name="pack",
    )(mr, mr, mr, se, se, se, mr_short, se_short)


def own_kernel(per, m1_ref, m2_ref, mw_ref, raw_ref, decay_ref, out_ref, taps_ref):
    rows = m1_ref.shape[1]
    tiles = rows // 8
    nothing = jnp.zeros((8, LANES), F32)

    @pl.loop(0, per)
    def _(k):
        lanes = lane_block(k)
        write_taps(taps_ref, raw_ref, decay_ref, lanes)
        z1 = features(m1_ref[0, :, lanes].astype(F32), nothing, tap_rows(mw_ref, 1, lanes))
        z2 = features(m2_ref[0, :, lanes].astype(F32), nothing, tap_rows(mw_ref, 2, lanes))
        product = (z1 * z2).astype(BF16).astype(F32)
        at = lax.broadcasted_iota(jnp.int32, (8, LANES), 0)
        head = jnp.where(at < 2, 0.0, product[:8])
        ext = jnp.concatenate([nothing, head, product[8:]], axis=0)
        total = [None] * tiles
        for r in range(8):
            shifted = roll(ext, r)
            tap = [tap_tile(taps_ref, 8 * a + r) for a in range(MEDIUM_TAPS // 8)]
            for i in range(tiles):
                for a in range(min(i + 1, MEDIUM_TAPS // 8)):
                    at_tile = 8 * (i - a + 1)
                    term = tap[a] * shifted[at_tile : at_tile + 8]
                    total[i] = term if total[i] is None else total[i] + term
        out_ref[:, lanes] = jnp.concatenate(total, axis=0)


def own_convolution(mr, mr_short, raw, decay, per):
    _, rows, channels = mr.shape
    width = per * LANES
    whole = lambda s: pl.BlockSpec((1, rows, width), lambda i: (s, 0, i))
    flat = lambda n: pl.BlockSpec((n, width), lambda i: (0, i))
    return pl.pallas_call(
        functools.partial(own_kernel, per),
        grid=(channels // width,),
        out_shape=jax.ShapeDtypeStruct((rows, channels), F32),
        in_specs=[
            whole(1),
            whole(2),
            pl.BlockSpec((3, 3, width), lambda i: (0, 0, i)),
            flat(MEDIUM_TAPS),
            flat(1),
        ],
        out_specs=flat(rows),
        scratch_shapes=[pltpu.VMEM((MEDIUM_TAPS, LANES), F32)],
        compiler_params=params(),
        cost_estimate=cost(150 * rows * channels, 12 * rows * channels),
        name="own_convolution",
    )(mr, mr, mr_short, raw, decay)


def mix_kernel(
    per,
    packet_ref,
    own_ref,
    m_ref,
    s_ref,
    mw_ref,
    sw_ref,
    raw_ref,
    decay_ref,
    filter_ref,
    se_ref,
    mr_ref,
    square_ref,
    taps_ref,
    last_ref,
):
    step = pl.program_id(0)
    rows = m_ref.shape[1]
    tiles = rows // 8
    chunk = MEDIUM_TAPS + 16
    nothing = jnp.zeros((8, LANES), F32)
    last_ref[...] = packet_ref[packet_ref.shape[0] - 16 :, :].astype(F32)

    @pl.when(step == 0)
    def _():
        square_ref[...] = jnp.zeros_like(square_ref)

    @pl.loop(0, per)
    def _(k):
        lanes = lane_block(k)
        block = step * per + k
        start = pl.multiple_of(block * chunk, 16)
        before = packet_ref[pl.ds(start, MEDIUM_TAPS), :].astype(F32)
        x = packet_ref[pl.ds(start + MEDIUM_TAPS, 16), :].astype(F32)
        x1, x2 = x[:8], x[8:]
        last = last_ref[pl.ds(block, 1), :]

        s0 = features(s_ref[0, :, lanes].astype(F32), roll(x1, 6), tap_rows(sw_ref, 0, lanes))
        s1 = features(s_ref[1, :, lanes].astype(F32), roll(x2, 6), tap_rows(sw_ref, 1, lanes))
        s2 = features(s_ref[2, :, lanes].astype(F32), roll(x2, 4), tap_rows(sw_ref, 2, lanes))
        ext = jnp.concatenate([x1, (s1 * s2).astype(BF16).astype(F32)], axis=0)
        total = filter_ref[0:1, lanes] * ext
        for j in range(1, LSE):
            total = total + filter_ref[j : j + 1, lanes] * roll(ext, j)
        mixed = s0 * total[8:]
        se_ref[:, lanes] = mixed
        square_ref[0] += mixed * mixed

        taps = write_taps(taps_ref, raw_ref, decay_ref, lanes)
        z0 = features(m_ref[0, :, lanes].astype(F32), roll(x2, 2), tap_rows(mw_ref, 0, lanes))
        front2 = jnp.where(row_is(8, 7), last, roll(before[:8], 6))
        z1 = features(m_ref[1, :16, lanes].astype(F32), x2, tap_rows(mw_ref, 1, lanes))
        z2 = features(m_ref[2, :16, lanes].astype(F32), front2, tap_rows(mw_ref, 2, lanes))
        first = (z1[:8] * z2[:8]).astype(BF16).astype(F32)
        padded = jnp.concatenate([taps, jnp.zeros((rows - MEDIUM_TAPS, LANES), F32)], axis=0)
        base = own_ref[:, lanes] + padded * first[0:1] + roll(padded, 1) * first[1:2]
        total = [base[8 * i : 8 * i + 8] for i in range(tiles)]
        ext = jnp.concatenate([before, nothing], axis=0)
        count = MEDIUM_TAPS // 8
        for r in range(8):
            shifted = roll(ext, r)
            tap = [tap_tile(taps_ref, 8 * a + r) for a in range(count)]
            for i in range(count):
                for a in range(i if r else i + 1, count):
                    at_tile = 8 * (i - a + count)
                    total[i] = total[i] + tap[a] * shifted[at_tile : at_tile + 8]
        mixed = z0 * jnp.concatenate(total, axis=0)
        mr_ref[:, lanes] = mixed
        square_ref[1] += mixed * mixed


def mix(packet, own, mr, se, mr_short, se_short, raw, decay, se_filter, per):
    _, rows, channels = mr.shape
    width = per * LANES
    streams = pl.BlockSpec((3, rows, width), lambda i: (0, 0, i))
    short = pl.BlockSpec((3, 3, width), lambda i: (0, 0, i))
    flat = lambda n: pl.BlockSpec((n, width), lambda i: (0, i))
    mixed = jax.ShapeDtypeStruct((rows, channels), F32)
    return pl.pallas_call(
        functools.partial(mix_kernel, per),
        grid=(channels // width,),
        out_shape=(mixed, mixed, jax.ShapeDtypeStruct((2, rows, LANES), F32)),
        in_specs=[
            pl.BlockSpec(packet.shape, lambda i: (0, 0)),
            flat(rows),
            streams,
            streams,
            short,
            short,
            flat(MEDIUM_TAPS),
            flat(1),
            flat(LSE),
        ],
        out_specs=(flat(rows), flat(rows), pl.BlockSpec((2, rows, LANES), lambda i: (0, 0, 0))),
        scratch_shapes=[pltpu.VMEM((MEDIUM_TAPS, LANES), F32), pltpu.VMEM((16, LANES), F32)],
        compiler_params=params(),
        cost_estimate=cost(180 * rows * channels, 24 * rows * channels),
        name="mix",
    )(packet, own, mr, se, mr_short, se_short, raw, decay, se_filter)


def score_kernel(per, there_ref, q_ref, k_ref, before_ref, v_ref, probs_ref, out_ref):
    rows = q_ref.shape[0]
    at = lax.broadcasted_iota(jnp.int32, (rows, 2 * rows), 0)
    key = lax.broadcasted_iota(jnp.int32, (rows, 2 * rows), 1)
    valid = (key <= at + rows) & (key >= there_ref[0])
    factor = math.log2(math.e) / math.sqrt(HD)

    @pl.loop(0, per)
    def _(k):
        lanes = lane_block(k)
        both = jnp.concatenate([before_ref[:, lanes], k_ref[:, lanes]], axis=0)
        scores = lax.dot_general(
            q_ref[:, lanes], both, (((1,), (1,)), ((), ())), preferred_element_type=F32
        )
        scores = jnp.where(valid, scores, -1e30)
        top = jnp.max(scores, axis=-1, keepdims=True)
        raw = jnp.exp2((scores - top) * factor)
        probs = (raw * (1.0 / jnp.sum(raw, axis=-1, keepdims=True))).astype(BF16)
        probs_ref[k] = probs[:, :rows]
        own = jnp.concatenate([jnp.zeros((rows, LANES), BF16), v_ref[:, lanes]], axis=0)
        out_ref[:, lanes] = jnp.dot(probs, own, preferred_element_type=F32)


def score(there, queries, keys, before, values, per):
    rows, channels = queries.shape
    width = per * LANES
    flat = pl.BlockSpec((rows, width), lambda i: (0, i))
    return pl.pallas_call(
        functools.partial(score_kernel, per),
        grid=(channels // width,),
        out_shape=(
            jax.ShapeDtypeStruct((channels // HD, rows, rows), BF16),
            jax.ShapeDtypeStruct((rows, channels), F32),
        ),
        in_specs=[pl.BlockSpec(memory_space=pltpu.SMEM), flat, flat, flat, flat],
        out_specs=(pl.BlockSpec((per, rows, rows), lambda i: (i, 0, 0)), flat),
        compiler_params=params(),
        cost_estimate=cost(8 * rows * rows * channels, 14 * rows * channels, 4 * rows * rows * channels // HD),
        name="score",
    )(there, queries, keys, before, values)


def value_kernel(per, probs_ref, before_ref, own_ref, out_ref, square_ref):
    @pl.when(pl.program_id(0) == 0)
    def _():
        square_ref[...] = jnp.zeros_like(square_ref)

    for k in range(per):
        lanes = slice(k * LANES, (k + 1) * LANES)
        total = own_ref[:, lanes] + jnp.dot(
            probs_ref[k], before_ref[:, lanes], preferred_element_type=F32
        )
        out_ref[:, lanes] = total
        square_ref[...] += total * total


def value_mix(probs, before, own, per):
    rows, channels = own.shape
    width = per * LANES
    flat = pl.BlockSpec((rows, width), lambda i: (0, i))
    return pl.pallas_call(
        functools.partial(value_kernel, per),
        grid=(channels // width,),
        out_shape=(
            jax.ShapeDtypeStruct((rows, channels), F32),
            jax.ShapeDtypeStruct((rows, LANES), F32),
        ),
        in_specs=[pl.BlockSpec((per, rows, rows), lambda i: (i, 0, 0)), flat, flat],
        out_specs=(flat, pl.BlockSpec((rows, LANES), lambda i: (0, 0))),
        compiler_params=params(),
        cost_estimate=cost(2 * rows * rows * channels, 12 * rows * channels),
        name="value_mix",
    )(probs, before, own)


def normalize_kernel(count, *refs):
    square_refs, mixed_refs, out_refs = refs[:-2 * count], refs[-2 * count : -count], refs[-count:]
    for n in range(count):
        square = square_refs[0][n]
        for ref in square_refs[1:]:
            square = square + ref[n]
        scale = lax.rsqrt(jnp.sum(square, axis=-1, keepdims=True) * (1.0 / CHANNELS) + 1e-06)
        out_refs[n][...] = (mixed_refs[n][...] * scale).astype(BF16)


def normalize(squares, mixed, per):
    rows, channels = mixed[0].shape
    count = len(mixed)
    flat = pl.BlockSpec((rows, per * LANES), lambda i: (0, i))
    square = pl.BlockSpec((count, rows, LANES), lambda i: (0, 0, 0))
    return pl.pallas_call(
        functools.partial(normalize_kernel, count),
        grid=(channels // (per * LANES),),
        out_shape=(jax.ShapeDtypeStruct((rows, channels), BF16),) * count,
        in_specs=[square] * len(squares) + [flat] * count,
        out_specs=(flat,) * count,
        compiler_params=params(),
        cost_estimate=cost(4 * count * rows * channels, 6 * count * rows * channels),
        name="normalize",
    )(*squares, *mixed)


def from_behind(value):
    count = lax.axis_size("ctx")
    return lax.ppermute(value, "ctx", [(source, source + 1) for source in range(count - 1)])


def of_panels(square):
    count = lax.axis_size("panel")
    return [square] + [
        lax.ppermute(square, "panel", [(n, (n + shift) % count) for n in range(count)])
        for shift in range(1, count)
    ]


def body(se, se_short, se_filter, mr, mr_short, raw, decay, queries, keys, values):
    rows = queries.shape[0]
    decay = decay[None, :]
    packet = from_behind(pack(se, mr, se_short, mr_short, 4))
    key_before, value_before = from_behind(keys), from_behind(values)
    own = own_convolution(mr, mr_short, raw, decay, 4)
    se_mix, mr_mix, square = mix(packet, own, mr, se, mr_short, se_short, raw, decay, se_filter, 4)
    squares = of_panels(square)
    there = jnp.where(lax.axis_index("ctx") == 0, rows, 0).astype(jnp.int32)[None]
    probs, attended = score(there, queries, keys, key_before, values, 4)
    se_out, mr_out = normalize(squares, (se_mix, mr_mix), 4)
    attended, square = value_mix(probs, value_before, attended, 4)
    (attn_out,) = normalize(of_panels(square[None]), (attended,), 4)
    return se_out, mr_out, attn_out


def solution(mesh):
    placed = (
        P(None, "ctx", "panel"),
        P(None, None, "panel"),
        P(None, "panel"),
        P(None, "ctx", "panel"),
        P(None, None, "panel"),
        P(None, "panel"),
        P("panel"),
        P("ctx", "panel"),
        P("ctx", "panel"),
        P("ctx", "panel"),
    )
    return jax.shard_map(
        body,
        mesh=mesh,
        in_specs=placed,
        out_specs=(P("ctx", "panel"), P("ctx", "panel"), P("ctx", "panel")),
        check_vma=False,
    )
```

time: 104 us -> 57.6 us (0.55)
  Pallas kernels: 0 us -> 34 us
  local copies, waits for them, and re-layouts: 30.1 us -> 5.81 us
  matrix products: 20.6 us -> 0 us
  other arithmetic: 19.6 us -> 0 us
  starting transfers between devices: 18.9 us -> 13.7 us
  blocking collectives: 5.11 us -> 0 us
  waiting for transfers between devices: 7.71 us -> 2.92 us
    pallas_call x0 -> x7, Pallas kernels: none -> 34 us  [the longest x1 10.5 us: mix(): pl.pallas_call(functools.partial(mix_kernel, per), grid=(channels // widt...]
    conv_general_dilated x2 -> x0, matrix products: 15 us -> none  [long_conv(): lax.conv_general_dilated(signal, reversed_taps, (1,), 'VALID', dimension_...]
    rev x2 -> x0, local copies, waits for them, and re-layouts: 13 us -> none  [long_conv(): reversed_taps = filt[::-1][:, None, :]]
    convert_element_type x6 -> x0, other arithmetic: 6.6 us -> none  [the longest x3 4.52 us: body(): outputs.append((mixed * scale[:, None]).astype(jnp.bfloat16))]
    slice x6 -> x0, local copies, waits for them, and re-layouts: 6.43 us -> none  [the longest x2 2.84 us: featurize(): short[:, 0][:, None, :] * ext[:, taps - 1:count, :].astype(jnp.float32)]
    add x4 -> x0, other arithmetic: 5.75 us -> none  [the longest x2 5.18 us: featurize(): total + short[:, j][:, None, :] * ext[:, taps - 1 - j:count - j, :].astyp...]
    dot_general x2 -> x0, matrix products: 5.63 us -> none  [the longest x1 3.58 us: attend(): jnp.einsum('hqk,khd->qhd', probs, v3, preferred_element_type=jnp.float32)]
    ppermute x6 -> x5, starting transfers between devices: 18.9 us -> 13.7 us  [the longest x3 9.36 us: from_behind(): lax.ppermute(value, 'ctx', [(source, source + 1) for source in range(coun...]
  transfers between devices with their start and end apart: 6 -> 5, of which waited for: 1 -> 3; matrix products, arithmetic and copies ran while one was open for 58% -> 0% of each run, Pallas kernels for 0% -> 54%
where the time goes in v1:
time: 57.6 us; the launch traced here: 57.2 us
  Pallas kernels  34 us (59%)
  starting transfers between devices  13.7 us (24%)
  local copies, waits for them, and re-layouts  5.81 us (10%)
  waiting for transfers between devices  2.92 us (5%)
  between operations  0.75 us (1%)
    pallas_call x1, Pallas kernels, mix(): pl.pallas_call(functools.partial(mix_kernel, per), grid=(channels // widt...  10.5 us
    pallas_call x1, Pallas kernels, score(): pl.pallas_call(functools.partial(score_kernel, per), grid=(channels // wi...  9.39 us
    ppermute x3, starting transfers between devices, from_behind(): lax.ppermute(value, 'ctx', [(source, source + 1) for source in range(coun...  9.36 us
    pallas_call x1, Pallas kernels, own_convolution(): pl.pallas_call(functools.partial(own_kernel, per), grid=(channels // widt...  8.05 us
    unnamed x18, local copies, waits for them, and re-layouts  5.81 us
    ppermute x2, starting transfers between devices, of_panels(): lax.ppermute(square, 'panel', [(n, (n + shift) % count) for n in range(co...  4.37 us
    pallas_call x2, Pallas kernels, normalize(): pl.pallas_call(functools.partial(normalize_kernel, count), grid=(channels...  3.65 us
    ppermute x3, waiting for transfers between devices, from_behind(): lax.ppermute(value, 'ctx', [(source, source + 1) for source in range(coun...  2 us
  transfers between devices with their start and end apart: 5, of which 3 were waited for; matrix products, arithmetic and copies ran while one was open for 0% of the time, Pallas kernels for 54%

profile of v1, /device:TPU:9, one launch (start us, length us, event | category | flops | bytes accessed | tf_op | source)
XLA Modules:
  0.0 57.2 jit_solution(3258710151918869311)
XLA Ops:
  0.6 0.0 copy-start
  0.6 1.5 %copy-done = bf16[3,144,2048]{2,1,0:T(8,128)(2,1)S(1)} copy-done((bf16[3,144,2048]{2,1,0:T(8,128)(2,1)S(1)}, bf16[3,144,2048]{2,1,0:T(8,128)(2,1)}, u32[]{:S(2)}) %copy-start) | copy-done | bytes 1769496
  2.1 0.0 copy-start.1
  2.1 1.5 %copy-done.1 = bf16[3,144,2048]{2,1,0:T(8,128)(2,1)S(1)} copy-done((bf16[3,144,2048]{2,1,0:T(8,128)(2,1)S(1)}, bf16[3,144,2048]{2,1,0:T(8,128)(2,1)}, u32[]{:S(2)}) %copy-start.1) | copy-done | bytes 1769496
  3.6 0.0 copy-start.4
  3.6 0.9 %copy-done.4 = f32[3,3,2048]{2,1,0:T(4,128)S(1)} copy-done((f32[3,3,2048]{2,1,0:T(4,128)S(1)}, f32[3,3,2048]{2,1,0:T(4,128)}, u32[]{:S(2)}) %copy-start.4) | copy-done | bytes 73752
  4.5 0.0 copy-start.5
  4.5 0.9 %copy-done.5 = f32[3,3,2048]{2,1,0:T(4,128)S(1)} copy-done((f32[3,3,2048]{2,1,0:T(4,128)S(1)}, f32[3,3,2048]{2,1,0:T(4,128)}, u32[]{:S(2)}) %copy-start.5) | copy-done | bytes 73752
  5.4 1.2 %pack.1 = bf16[2320,128]{1,0:T(8,128)(2,1)S(1)} custom-call(bf16[3,144,2048]{2,1,0:T(8,128)(2,1)S(1)} %copy-done, bf16[3,144,2048]{2,1,0:T(8,128)(2,1)S(1)} %copy-done, bf16[3,144,2048]{2,1,0:T(8,128)(2,1)S(1)} %copy-done, bf16[3,144,2048]{2,1,0:T(8,128)(2,1)S(1)} %copy-done.1, bf16[3,144,2048]{2,1,0:T(8,128)(2,1)S(1)} %copy-done.1, ...), custom_call_target="tpu_custom_call" | custom-call | flops 5898240 | bytes 1769472 | tf_op jit(solution)/shard_map/pack/pallas_call | solution.py:117
  6.6 3.1 %collective-permute-start = (bf16[2320,128]{1,0:T(8,128)(2,1)S(1)}, bf16[2320,128]{1,0:T(8,128)(2,1)S(1)}, u32[]{:S(2)}, u32[]{:S(2)}) collective-permute-start(bf16[2320,128]{1,0:T(8,128)(2,1)S(1)} %pack.1), channel_id=1, source_target_pairs={{0,2},{2,4},{4,6},{6,8},{8,10},{10,12},{12,14},{14,16},{16,18},{18... | collective-permute-start | bytes 1781768 | tf_op jit(solution)/shard_map/ppermute | solution.py:387
  9.7 3.1 %collective-permute-start.2 = (bf16[144,2048]{1,0:T(8,128)(2,1)}, bf16[144,2048]{1,0:T(8,128)(2,1)}, u32[]{:S(2)}, u32[]{:S(2)}) collective-permute-start(bf16[144,2048]{1,0:T(8,128)(2,1)} %k_ref.1), channel_id=1, source_target_pairs={{0,2},{2,4},{4,6},{6,8},{8,10},{10,12},{12,14},{14,16},{16,18},{18... | collective-permute-start | bytes 1769480 | tf_op jit(solution)/shard_map/ppermute | solution.py:387
  12.8 3.1 %collective-permute-start.3 = (bf16[144,2048]{1,0:T(8,128)(2,1)}, bf16[144,2048]{1,0:T(8,128)(2,1)S(1)}, u32[]{:S(2)}, u32[]{:S(2)}) collective-permute-start(bf16[144,2048]{1,0:T(8,128)(2,1)} %v_ref.1), channel_id=1, source_target_pairs={{0,2},{2,4},{4,6},{6,8},{8,10},{10,12},{12,14},{14,16},{16,18},{18... | collective-permute-start | bytes 1769480 | tf_op jit(solution)/shard_map/ppermute | solution.py:387
  16.0 0.0 copy-done.3
  16.0 0.0 copy-done.7
  16.0 0.0 copy-start.2
  16.0 0.0 copy-start.6
  16.0 8.1 %own_convolution.1.own_ref = f32[144,2048]{1,0:T(8,128)S(1)} custom-call(bf16[3,144,2048]{2,1,0:T(8,128)(2,1)S(1)} %copy-done, bf16[3,144,2048]{2,1,0:T(8,128)(2,1)S(1)} %copy-done, f32[3,3,2048]{2,1,0:T(4,128)S(1)} %copy-done.4, f32[128,2048]{1,0:T(8,128)S(1)} %copy-done.3, f32[1,2048]{1,0:T(1,128)S(1)} %bitcast.5), custom_call_target="tpu_custom_call" | custom-call | flops 44236800 | bytes 3538944 | tf_op jit(solution)/shard_map/own_convolution/pallas_call | solution.py:162
  24.1 0.5 collective-permute-done.packet_ref
  24.6 0.0 copy-done.2
  24.6 0.0 copy-done.6
  24.6 10.5 %mix.1 = (f32[144,2048]{1,0:T(8,128)S(1)}, f32[144,2048]{1,0:T(8,128)S(1)}, f32[2,144,128]{2,1,0:T(8,128)S(1)}) custom-call(bf16[2320,128]{1,0:T(8,128)(2,1)S(1)} %collective-permute-done.packet_ref, f32[144,2048]{1,0:T(8,128)S(1)} %own_convolution.1.own_ref, bf16[3,144,2048]{2,1,0:T(8,128)(2,1)S(1)} %copy-done, bf16[3,144,2048]{2,1,0:T(8,128)(2,1)S(1)} %copy-done.2, ...), custom_call_target="tpu_custom_call" | custom-call | flops 53084160 | bytes 7077888 | tf_op jit(solution)/shard_map/mix/pallas_call | solution.py:260
  35.1 2.8 %collective-permute-start.1 = (f32[2,144,128]{2,1,0:T(8,128)S(1)}, f32[2,144,128]{2,1,0:T(8,128)S(1)}, u32[]{:S(2)}, u32[]{:S(2)}) collective-permute-start(f32[2,144,128]{2,1,0:T(8,128)S(1)} %get-tuple-element.12.refs_0_), channel_id=1, source_target_pairs={{0,1},{1,0},{2,3},{3,2},{4,5},{5,4},{6,7},{7,6},{8,9},{9,8},{10,11... | collective-permute-start | bytes 442376 | tf_op jit(solution)/shard_map/ppermute | solution.py:393
  37.9 0.0 collective-permute-done.2.before_ref
  37.9 1.1 %copy-done.8 = bf16[144,2048]{1,0:T(8,128)(2,1)S(1)} copy-done((bf16[144,2048]{1,0:T(8,128)(2,1)S(1)}, bf16[144,2048]{1,0:T(8,128)(2,1)}, u32[]{:S(2)}) %copy-start.8) | copy-done | bytes 589848
  38.9 9.4 %score.1 = (bf16[16,144,144]{2,1,0:T(8,128)(2,1)S(1)}, f32[144,2048]{1,0:T(8,128)S(1)}) custom-call(s32[1]{0:T(128)} %bitcast.1.there_ref, bf16[144,2048]{1,0:T(8,128)(2,1)S(1)} %copy-done.8, bf16[144,2048]{1,0:T(8,128)(2,1)} %k_ref.1, bf16[144,2048]{1,0:T(8,128)(2,1)} %collective-permute-done.2.before_ref, bf16[144,2048]{1,0:T(8,128)(2,1)} %v_ref.1), custom_call_target="tpu_custom_call" | custom-call | flops 339738624 | bytes 4128768 | tf_op jit(solution)/shard_map/score/pallas_call | solution.py:310
  48.3 1.5 %collective-permute-done.3.before_ref = bf16[144,2048]{1,0:T(8,128)(2,1)S(1)} collective-permute-done((bf16[144,2048]{1,0:T(8,128)(2,1)}, bf16[144,2048]{1,0:T(8,128)(2,1)S(1)}, u32[]{:S(2)}, u32[]{:S(2)}) %collective-permute-start.3) | collective-permute-done | bytes 589856 | tf_op jit(solution)/shard_map/ppermute | solution.py:387
  49.8 1.2 %value_mix.1 = (f32[144,2048]{1,0:T(8,128)S(1)}, f32[144,128]{1,0:T(8,128)S(1)}) custom-call(bf16[16,144,144]{2,1,0:T(8,128)(2,1)S(1)} %get-tuple-element.17.probs_ref, bf16[144,2048]{1,0:T(8,128)(2,1)S(1)} %collective-permute-done.3.before_ref, f32[144,2048]{1,0:T(8,128)S(1)} %get-tuple-element.18.own_ref), custom_call_target="tpu_custom_call" | custom-call | flops 84934656 | bytes 3538944 | tf_op jit(solution)/shard_map/value_mix/pallas_call | solution.py:343
  51.0 1.6 %collective-permute-start.4 = (f32[1,144,128]{2,1,0:T(8,128)S(1)}, f32[1,144,128]{2,1,0:T(8,128)S(1)}, u32[]{:S(2)}, u32[]{:S(2)}) collective-permute-start(f32[1,144,128]{2,1,0:T(8,128)S(1)} %bitcast.3), channel_id=1, source_target_pairs={{0,1},{1,0},{2,3},{3,2},{4,5},{5,4},{6,7},{7,6},{8,9},{9,8},{10,11... | collective-permute-start | bytes 221192 | tf_op jit(solution)/shard_map/ppermute | solution.py:393
  52.6 0.9 %collective-permute-done.4.refs_1_ = f32[1,144,128]{2,1,0:T(8,128)S(1)} collective-permute-done((f32[1,144,128]{2,1,0:T(8,128)S(1)}, f32[1,144,128]{2,1,0:T(8,128)S(1)}, u32[]{:S(2)}, u32[]{:S(2)}) %collective-permute-start.4) | collective-permute-done | bytes 73760 | tf_op jit(solution)/shard_map/ppermute | solution.py:393
  53.6 1.7 %normalize.3 = bf16[144,2048]{1,0:T(8,128)(2,1)} custom-call(f32[1,144,128]{2,1,0:T(8,128)S(1)} %bitcast.4, f32[1,144,128]{2,1,0:T(8,128)S(1)} %collective-permute-done.4.refs_1_, f32[144,2048]{1,0:T(8,128)S(1)} %get-tuple-element.20.refs_2_), custom_call_target="tpu_custom_call" | custom-call | flops 1179648 | bytes 1769472 | tf_op jit(solution)/shard_map/normalize/pallas_call | solution.py:373
  55.3 0.0 collective-permute-done.1.refs_1_
  55.3 1.9 %normalize.2 = (bf16[144,2048]{1,0:T(8,128)(2,1)}, bf16[144,2048]{1,0:T(8,128)(2,1)}) custom-call(f32[2,144,128]{2,1,0:T(8,128)S(1)} %get-tuple-element.12.refs_0_, f32[2,144,128]{2,1,0:T(8,128)S(1)} %collective-permute-done.1.refs_1_, f32[144,2048]{1,0:T(8,128)S(1)} %get-tuple-element.13.refs_2_, f32[144,2048]{1,0:T(8,128)S(1)} %get-tuple-element.14.refs_3_), custom_call_target="tpu_custom_call" | custom-call | flops 2359296 | bytes 3538944 | tf_op jit(solution)/shard_map/normalize/pallas_call | solution.py:373
  (3 shorter events, 0.0 us)
Async XLA Ops:
  0.6 1.5 %copy-start = (bf16[3,144,2048]{2,1,0:T(8,128)(2,1)S(1)}, bf16[3,144,2048]{2,1,0:T(8,128)(2,1)}, u32[]{:S(2)}) copy-start(bf16[3,144,2048]{2,1,0:T(8,128)(2,1)} %m_ref.1) | copy-start | bytes 5308420
  2.1 1.5 %copy-start.1 = (bf16[3,144,2048]{2,1,0:T(8,128)(2,1)S(1)}, bf16[3,144,2048]{2,1,0:T(8,128)(2,1)}, u32[]{:S(2)}) copy-start(bf16[3,144,2048]{2,1,0:T(8,128)(2,1)} %s_ref.1) | copy-start | bytes 5308420
  3.6 0.9 %copy-start.4 = (f32[3,3,2048]{2,1,0:T(4,128)S(1)}, f32[3,3,2048]{2,1,0:T(4,128)}, u32[]{:S(2)}) copy-start(f32[3,3,2048]{2,1,0:T(4,128)} %mw_ref.5) | copy-start | bytes 221188
  4.5 0.9 %copy-start.5 = (f32[3,3,2048]{2,1,0:T(4,128)S(1)}, f32[3,3,2048]{2,1,0:T(4,128)}, u32[]{:S(2)}) copy-start(f32[3,3,2048]{2,1,0:T(4,128)} %sw_ref.3) | copy-start | bytes 221188
  5.4 10.6 %copy-start.3 = (f32[128,2048]{1,0:T(8,128)S(1)}, f32[128,2048]{1,0:T(8,128)}, u32[]{:S(2)}) copy-start(f32[128,2048]{1,0:T(8,128)} %raw_ref.3) | copy-start | bytes 3145732
  5.4 10.6 %copy-start.7 = (f32[2048]{0:T(1024)S(1)}, f32[2048]{0:T(1024)}, u32[]{:S(2)}) copy-start(f32[2048]{0:T(1024)} %param.16) | copy-start | bytes 24580
  6.6 18.0 %collective-permute-start = (bf16[2320,128]{1,0:T(8,128)(2,1)S(1)}, bf16[2320,128]{1,0:T(8,128)(2,1)S(1)}, u32[]{:S(2)}, u32[]{:S(2)}) collective-permute-start(bf16[2320,128]{1,0:T(8,128)(2,1)S(1)} %pack.1), channel_id=1, source_target_pairs={{0,2},{2,4},{4,6},{6,8},{8,10},{10,12},{12,14},{14,16},{16,18},{18... | collective-permute-start | bytes 1781768 | tf_op jit(solution)/shard_map/ppermute | solution.py:387
  9.7 28.1 %collective-permute-start.2 = (bf16[144,2048]{1,0:T(8,128)(2,1)}, bf16[144,2048]{1,0:T(8,128)(2,1)}, u32[]{:S(2)}, u32[]{:S(2)}) collective-permute-start(bf16[144,2048]{1,0:T(8,128)(2,1)} %k_ref.1), channel_id=1, source_target_pairs={{0,2},{2,4},{4,6},{6,8},{8,10},{10,12},{12,14},{14,16},{16,18},{18... | collective-permute-start | bytes 1769480 | tf_op jit(solution)/shard_map/ppermute | solution.py:387
  12.8 37.0 %collective-permute-start.3 = (bf16[144,2048]{1,0:T(8,128)(2,1)}, bf16[144,2048]{1,0:T(8,128)(2,1)S(1)}, u32[]{:S(2)}, u32[]{:S(2)}) collective-permute-start(bf16[144,2048]{1,0:T(8,128)(2,1)} %v_ref.1), channel_id=1, source_target_pairs={{0,2},{2,4},{4,6},{6,8},{8,10},{10,12},{12,14},{14,16},{16,18},{18... | collective-permute-start | bytes 1769480 | tf_op jit(solution)/shard_map/ppermute | solution.py:387
  16.0 8.6 %copy-start.2 = (bf16[3,144,2048]{2,1,0:T(8,128)(2,1)S(1)}, bf16[3,144,2048]{2,1,0:T(8,128)(2,1)}, u32[]{:S(2)}) copy-start(bf16[3,144,2048]{2,1,0:T(8,128)(2,1)} %s_ref.1) | copy-start | bytes 5308420
  16.0 8.6 %copy-start.6 = (f32[7,2048]{1,0:T(8,128)S(1)}, f32[7,2048]{1,0:T(8,128)}, u32[]{:S(2)}) copy-start(f32[7,2048]{1,0:T(8,128)} %filter_ref.1) | copy-start | bytes 172036
  35.1 20.2 %collective-permute-start.1 = (f32[2,144,128]{2,1,0:T(8,128)S(1)}, f32[2,144,128]{2,1,0:T(8,128)S(1)}, u32[]{:S(2)}, u32[]{:S(2)}) collective-permute-start(f32[2,144,128]{2,1,0:T(8,128)S(1)} %get-tuple-element.12.refs_0_), channel_id=1, source_target_pairs={{0,1},{1,0},{2,3},{3,2},{4,5},{5,4},{6,7},{7,6},{8,9},{9,8},{10,11... | collective-permute-start | bytes 442376 | tf_op jit(solution)/shard_map/ppermute | solution.py:393
  37.9 1.1 %copy-start.8 = (bf16[144,2048]{1,0:T(8,128)(2,1)S(1)}, bf16[144,2048]{1,0:T(8,128)(2,1)}, u32[]{:S(2)}) copy-start(bf16[144,2048]{1,0:T(8,128)(2,1)} %q_ref.1) | copy-start | bytes 1769476
  51.0 2.5 %collective-permute-start.4 = (f32[1,144,128]{2,1,0:T(8,128)S(1)}, f32[1,144,128]{2,1,0:T(8,128)S(1)}, u32[]{:S(2)}, u32[]{:S(2)}) collective-permute-start(f32[1,144,128]{2,1,0:T(8,128)S(1)} %bitcast.3), channel_id=1, source_target_pairs={{0,1},{1,0},{2,3},{3,2},{4,5},{5,4},{6,7},{7,6},{8,9},{9,8},{10,11... | collective-permute-start | bytes 221192 | tf_op jit(solution)/shard_map/ppermute | solution.py:393

commit v2 on v1

v2 whole, which is shorter than its diff:
```python
import functools
import math

import jax
import jax.numpy as jnp
from jax import lax
from jax.experimental import pallas as pl
from jax.experimental.pallas import tpu as pltpu
from jax.sharding import PartitionSpec as P

CHANNELS = 4096
HD = 128
LSE = 7
MEDIUM_TAPS = 128
LANES = 128
F32 = jnp.float32
BF16 = jnp.bfloat16


def params(mebibytes=36):
    return pltpu.CompilerParams(vmem_limit_bytes=mebibytes * 1024 * 1024)


def in_vmem():
    return pl.BlockSpec(memory_space=pltpu.VMEM)


def cost(flops, nbytes, trans=0):
    return pl.CostEstimate(flops=int(flops), bytes_accessed=int(nbytes), transcendentals=int(trans))


def roll(value, shift):
    shift = shift % value.shape[0]
    return pltpu.roll(value, shift, 0) if shift else value


def row_is(rows, at):
    return lax.broadcasted_iota(jnp.int32, (rows, LANES), 0) == at


def features(u, front, taps):
    ext = jnp.concatenate([front, u], axis=0)
    total = taps[0] * ext
    for j in range(1, len(taps)):
        total = total + taps[j] * roll(ext, j)
    return total[8:]


def tap_rows(ref, stream, lanes):
    return [ref[stream, j : j + 1, lanes] for j in range(ref.shape[1])]


def lane_block(k):
    return pl.ds(pl.multiple_of(k * LANES, LANES), LANES)


def write_taps(taps_ref, raw_ref, decay_ref, lanes):
    steps = lax.broadcasted_iota(jnp.int32, (MEDIUM_TAPS, LANES), 0).astype(F32)
    taps = raw_ref[:, lanes] * jnp.exp(-decay_ref[0:1, lanes] * steps)
    taps_ref[...] = taps
    return taps


def tap_tile(taps_ref, j):
    return jnp.broadcast_to(taps_ref[j : j + 1, :], (8, LANES))


def pack_kernel(per, m1_ref, m2_ref, m0t_ref, s0t_ref, s1t_ref, s2t_ref, mw_ref, sw_ref, out_ref, last_ref):
    step = pl.program_id(0)
    rows = m1_ref.shape[1]
    chunk = MEDIUM_TAPS + 16
    nothing = jnp.zeros((8, LANES), F32)

    @pl.when(step == 0)
    def _():
        last_ref[...] = jnp.zeros_like(last_ref)

    @pl.loop(0, per)
    def _(k):
        lanes = lane_block(k)
        block = step * per + k
        m1 = m1_ref[0, :, lanes].astype(F32)
        m2 = m2_ref[0, :, lanes].astype(F32)
        z1 = features(m1, nothing, tap_rows(mw_ref, 1, lanes))
        z2 = features(m2, nothing, tap_rows(mw_ref, 2, lanes))
        product = (z1 * z2)[rows - MEDIUM_TAPS :]
        tail_m0 = m0t_ref[0, :, lanes].astype(F32)[8:]
        tail_m1, tail_m2 = m1[rows - 8 :], m2[rows - 8 :]
        head = jnp.where(row_is(8, 0), roll(tail_m2, 2), product[:8])
        product = jnp.concatenate([head, product[8:]], axis=0)
        s0 = s0t_ref[0, :, lanes].astype(F32)[8:]
        s1 = s1t_ref[0, :, lanes].astype(F32)
        s2 = s2t_ref[0, :, lanes].astype(F32)
        y1 = features(s1, nothing, tap_rows(sw_ref, 1, lanes))[8:]
        y2 = features(s2, nothing, tap_rows(sw_ref, 2, lanes))[8:]
        at = lax.broadcasted_iota(jnp.int32, (8, LANES), 0)
        x1 = jnp.where(at < 2, roll(s0, 2), y1 * y2)
        x2 = jnp.where(
            at < 2,
            roll(s1[8:], 2),
            jnp.where(at < 4, roll(s2[8:], 4), jnp.where(at < 6, roll(tail_m0, 6), tail_m1)),
        )
        start = pl.multiple_of(block * chunk, 16)
        out_ref[pl.ds(start, MEDIUM_TAPS), :] = product.astype(BF16)
        out_ref[pl.ds(start + MEDIUM_TAPS, 16), :] = jnp.concatenate([x1, x2], axis=0).astype(BF16)
        last_ref[pl.ds(block, 1), :] = tail_m2[7:8]

    out_ref[out_ref.shape[0] - 16 :, :] = last_ref[...].astype(BF16)


def pack(se, mr, se_short, mr_short, per):
    _, rows, channels = se.shape
    blocks = channels // LANES
    total = blocks * (MEDIUM_TAPS + 16) + 16
    width = per * LANES
    whole = lambda s: pl.BlockSpec((1, rows, width), lambda i: (s, 0, i))
    tail = lambda s: pl.BlockSpec((1, 16, width), lambda i: (s, rows // 16 - 1, i))
    short = pl.BlockSpec((3, 3, width), lambda i: (0, 0, i))
    return pl.pallas_call(
        functools.partial(pack_kernel, per),
        grid=(blocks // per,),
        out_shape=jax.ShapeDtypeStruct((total, LANES), BF16),
        in_specs=[whole(1), whole(2), tail(0), tail(0), tail(1), tail(2), short, short],
        out_specs=pl.BlockSpec((total, LANES), lambda i: (0, 0)),
        scratch_shapes=[pltpu.VMEM((16, LANES), F32)],
        compiler_params=params(60),
        cost_estimate=cost(20 * rows * channels, 6 * rows * channels),
        name="pack",
    )(mr, mr, mr, se, se, se, mr_short, se_short)


def own_kernel(m_ref, s_ref, mw_ref, sw_ref, raw_ref, decay_ref, filter_ref, own_ref, se_ref, square_ref, taps_ref):
    rows, channels = own_ref.shape
    tiles = rows // 8
    nothing = jnp.zeros((8, LANES), F32)
    square_ref[...] = jnp.zeros_like(square_ref)

    @pl.loop(0, channels // LANES)
    def _(k):
        lanes = lane_block(k)
        s = [features(s_ref[n, :, lanes].astype(F32), nothing, tap_rows(sw_ref, n, lanes)) for n in range(3)]
        ext = jnp.concatenate([nothing, (s[1] * s[2]).astype(BF16).astype(F32)], axis=0)
        total = filter_ref[0:1, lanes] * ext
        for j in range(1, LSE):
            total = total + filter_ref[j : j + 1, lanes] * roll(ext, j)
        mixed = s[0] * total[8:]
        se_ref[:, lanes] = mixed
        square_ref[8:, :] += mixed[8:] * mixed[8:]

        write_taps(taps_ref, raw_ref, decay_ref, lanes)
        z1 = features(m_ref[1, :, lanes].astype(F32), nothing, tap_rows(mw_ref, 1, lanes))
        z2 = features(m_ref[2, :, lanes].astype(F32), nothing, tap_rows(mw_ref, 2, lanes))
        product = (z1 * z2).astype(BF16).astype(F32)
        at = lax.broadcasted_iota(jnp.int32, (8, LANES), 0)
        head = jnp.where(at < 2, 0.0, product[:8])
        ext = jnp.concatenate([nothing, head, product[8:]], axis=0)
        total = [None] * tiles
        for r in range(8):
            shifted = roll(ext, r)
            tap = [tap_tile(taps_ref, 8 * a + r) for a in range(MEDIUM_TAPS // 8)]
            for i in range(tiles):
                for a in range(min(i + 1, MEDIUM_TAPS // 8)):
                    at_tile = 8 * (i - a + 1)
                    term = tap[a] * shifted[at_tile : at_tile + 8]
                    total[i] = term if total[i] is None else total[i] + term
        own_ref[:, lanes] = jnp.concatenate(total, axis=0)


def own_part(mr, se, mr_short, se_short, raw, decay, se_filter):
    _, rows, channels = mr.shape
    mixed = jax.ShapeDtypeStruct((rows, channels), F32)
    return pl.pallas_call(
        own_kernel,
        out_shape=(mixed, mixed, jax.ShapeDtypeStruct((rows, LANES), F32)),
        in_specs=[in_vmem()] * 7,
        out_specs=(in_vmem(),) * 3,
        scratch_shapes=[pltpu.VMEM((MEDIUM_TAPS, LANES), F32)],
        compiler_params=params(),
        cost_estimate=cost(180 * rows * channels, 24 * rows * channels),
        name="own_part",
    )(mr, se, mr_short, se_short, raw, decay, se_filter)


def mix_kernel(
    packet_ref,
    own_ref,
    se_square_ref,
    m_ref,
    s_ref,
    mw_ref,
    sw_ref,
    raw_ref,
    decay_ref,
    filter_ref,
    head_ref,
    mr_ref,
    square_ref,
    taps_ref,
    last_ref,
):
    rows, channels = own_ref.shape
    tiles = rows // 8
    chunk = MEDIUM_TAPS + 16
    nothing = jnp.zeros((8, LANES), F32)
    last_ref[...] = packet_ref[packet_ref.shape[0] - 16 :, :].astype(F32)
    square_ref[0] = se_square_ref[...]
    square_ref[1] = jnp.zeros((rows, LANES), F32)

    @pl.loop(0, channels // LANES)
    def _(k):
        lanes = lane_block(k)
        start = pl.multiple_of(k * chunk, 16)
        before = packet_ref[pl.ds(start, MEDIUM_TAPS), :].astype(F32)
        x = packet_ref[pl.ds(start + MEDIUM_TAPS, 16), :].astype(F32)
        x1, x2 = x[:8], x[8:]
        last = last_ref[pl.ds(k, 1), :]

        fronts = (roll(x1, 6), roll(x2, 6), roll(x2, 4))
        s = [
            features(s_ref[n, :16, lanes].astype(F32)[:8], fronts[n], tap_rows(sw_ref, n, lanes))
            for n in range(3)
        ]
        ext = jnp.concatenate([x1, (s[1] * s[2]).astype(BF16).astype(F32)], axis=0)
        total = filter_ref[0:1, lanes] * ext
        for j in range(1, LSE):
            total = total + filter_ref[j : j + 1, lanes] * roll(ext, j)
        mixed = s[0] * total[8:]
        head_ref[:, lanes] = mixed
        square_ref[0, :8, :] += mixed * mixed

        taps = write_taps(taps_ref, raw_ref, decay_ref, lanes)
        z0 = features(m_ref[0, :, lanes].astype(F32), roll(x2, 2), tap_rows(mw_ref, 0, lanes))
        front2 = jnp.where(row_is(8, 7), last, roll(before[:8], 6))
        z1 = features(m_ref[1, :16, lanes].astype(F32)[:8], x2, tap_rows(mw_ref, 1, lanes))
        z2 = features(m_ref[2, :16, lanes].astype(F32)[:8], front2, tap_rows(mw_ref, 2, lanes))
        first = (z1 * z2).astype(BF16).astype(F32)
        padded = jnp.concatenate([taps, jnp.zeros((rows - MEDIUM_TAPS, LANES), F32)], axis=0)
        base = own_ref[:, lanes] + padded * first[0:1] + roll(padded, 1) * first[1:2]
        total = [base[8 * i : 8 * i + 8] for i in range(tiles)]
        ext = jnp.concatenate([before, nothing], axis=0)
        count = MEDIUM_TAPS // 8
        for r in range(8):
            shifted = roll(ext, r)
            tap = [tap_tile(taps_ref, 8 * a + r) for a in range(count)]
            for i in range(count):
                for a in range(i if r else i + 1, count):
                    at_tile = 8 * (i - a + count)
                    total[i] = total[i] + tap[a] * shifted[at_tile : at_tile + 8]
        mixed = z0 * jnp.concatenate(total, axis=0)
        mr_ref[:, lanes] = mixed
        square_ref[1] += mixed * mixed


def mix(packet, own, se_square, mr, se, mr_short, se_short, raw, decay, se_filter):
    _, rows, channels = mr.shape
    return pl.pallas_call(
        mix_kernel,
        out_shape=(
            jax.ShapeDtypeStruct((8, channels), F32),
            jax.ShapeDtypeStruct((rows, channels), F32),
            jax.ShapeDtypeStruct((2, rows, LANES), F32),
        ),
        in_specs=[in_vmem()] * 10,
        out_specs=(in_vmem(),) * 3,
        scratch_shapes=[pltpu.VMEM((MEDIUM_TAPS, LANES), F32), pltpu.VMEM((16, LANES), F32)],
        compiler_params=params(),
        cost_estimate=cost(140 * rows * channels, 16 * rows * channels),
        name="mix",
    )(packet, own, se_square, mr, se, mr_short, se_short, raw, decay, se_filter)


def score_kernel(per, there_ref, q_ref, k_ref, before_ref, v_ref, probs_ref, out_ref, inverse_ref, bias_ref):
    rows, channels = q_ref.shape
    at = lax.broadcasted_iota(jnp.int32, (rows, 2 * rows), 0)
    key = lax.broadcasted_iota(jnp.int32, (rows, 2 * rows), 1)
    valid = (key <= at + rows) & (key >= there_ref[0])
    bias_ref[...] = jnp.where(valid, 0.0, -1e30)
    factor = math.log2(math.e) / math.sqrt(HD)
    zeros, ones = jnp.zeros((rows, LANES), BF16), jnp.ones((rows, LANES), BF16)

    @pl.loop(0, channels // (LANES * per))
    def _(group):
        for n in range(per):
            head = group * per + n
            lanes = lane_block(head)
            both = jnp.concatenate([before_ref[:, lanes], k_ref[:, lanes]], axis=0)
            scores = lax.dot_general(
                q_ref[:, lanes], both, (((1,), (1,)), ((), ())), preferred_element_type=F32
            )
            scores = scores + bias_ref[...]
            top = jnp.max(scores, axis=-1, keepdims=True)
            probs = jnp.exp2((scores - top) * factor).astype(BF16)
            probs_ref[head] = probs[:, :rows]
            own = jnp.concatenate(
                [
                    jnp.concatenate([zeros, v_ref[:, lanes]], axis=0),
                    jnp.concatenate([ones, ones], axis=0),
                ],
                axis=1,
            )
            total = jnp.dot(probs, own, preferred_element_type=F32)
            inverse = 1.0 / total[:, LANES:]
            inverse_ref[:, lanes] = inverse
            out_ref[:, lanes] = total[:, :LANES] * inverse


def score(there, queries, keys, before, values, per):
    rows, channels = queries.shape
    flat = jax.ShapeDtypeStruct((rows, channels), F32)
    return pl.pallas_call(
        functools.partial(score_kernel, per),
        out_shape=(jax.ShapeDtypeStruct((channels // HD, rows, rows), BF16), flat, flat),
        in_specs=[pl.BlockSpec(memory_space=pltpu.SMEM)] + [in_vmem()] * 4,
        out_specs=(in_vmem(),) * 3,
        scratch_shapes=[pltpu.VMEM((rows, 2 * rows), F32)],
        compiler_params=params(),
        cost_estimate=cost(
            8 * rows * rows * channels, 14 * rows * channels, 4 * rows * rows * channels // HD
        ),
        name="score",
    )(there, queries, keys, before, values)


def value_kernel(probs_ref, before_ref, own_ref, inverse_ref, out_ref, square_ref):
    rows, channels = own_ref.shape
    square = jnp.zeros((rows, LANES), F32)
    for k in range(channels // LANES):
        lanes = slice(k * LANES, (k + 1) * LANES)
        total = own_ref[:, lanes] + inverse_ref[:, lanes] * jnp.dot(
            probs_ref[k], before_ref[:, lanes], preferred_element_type=F32
        )
        out_ref[:, lanes] = total
        square = square + total * total
    square_ref[0] = square


def value_mix(probs, before, own, inverse):
    rows, channels = own.shape
    return pl.pallas_call(
        value_kernel,
        out_shape=(
            jax.ShapeDtypeStruct((rows, channels), F32),
            jax.ShapeDtypeStruct((1, rows, LANES), F32),
        ),
        in_specs=[in_vmem()] * 4,
        out_specs=(in_vmem(),) * 2,
        compiler_params=params(),
        cost_estimate=cost(2 * rows * rows * channels, 12 * rows * channels),
        name="value_mix",
    )(probs, before, own, inverse)


def normalize_kernel(count, panels, pieces, with_head, *refs):
    square_refs, refs = refs[:panels], refs[panels:]
    mixed_refs, refs = refs[:count], refs[count:]
    if with_head:
        head_ref, refs = refs[0], refs[1:]
    out_refs, (held_ref, sems) = refs[:count], refs[count:]
    rows = mixed_refs[0].shape[0]
    piece = rows // pieces
    copies = []
    for n in range(count):
        square = square_refs[0][n]
        for ref in square_refs[1:]:
            square = square + ref[n]
        scale = lax.rsqrt(jnp.sum(square, axis=-1, keepdims=True) * (1.0 / CHANNELS) + 1e-06)
        for m in range(pieces):
            at = slice(m * piece, (m + 1) * piece)
            value = mixed_refs[n][at, :]
            if with_head and n == 0 and m == 0:
                value = jnp.concatenate([head_ref[...], value[8:]], axis=0)
            held_ref[n, at, :] = (value * scale[at]).astype(BF16)
            copy = pltpu.make_async_copy(
                held_ref.at[n, pl.ds(m * piece, piece)],
                out_refs[n].at[pl.ds(m * piece, piece)],
                sems.at[n, m],
            )
            copy.start()
            copies.append(copy)
    for copy in copies:
        copy.wait()


def normalize(squares, mixed, head=None, pieces=3):
    rows, channels = mixed[0].shape
    count = len(mixed)
    operands = (*squares, *mixed) + (() if head is None else (head,))
    return pl.pallas_call(
        functools.partial(normalize_kernel, count, len(squares), pieces, head is not None),
        out_shape=(jax.ShapeDtypeStruct((rows, channels), BF16),) * count,
        in_specs=[in_vmem()] * len(operands),
        out_specs=(pl.BlockSpec(memory_space=pl.ANY),) * count,
        scratch_shapes=[
            pltpu.VMEM((count, rows, channels), BF16),
            pltpu.SemaphoreType.DMA((count, pieces)),
        ],
        compiler_params=params(),
        cost_estimate=cost(4 * count * rows * channels, 6 * count * rows * channels),
        name="normalize",
    )(*operands)


def from_behind(value):
    count = lax.axis_size("ctx")
    return lax.ppermute(value, "ctx", [(source, source + 1) for source in range(count - 1)])


def of_panels(square):
    count = lax.axis_size("panel")
    return [square] + [
        lax.ppermute(square, "panel", [(n, (n + shift) % count) for n in range(count)])
        for shift in range(1, count)
    ]


def body(se, se_short, se_filter, mr, mr_short, raw, decay, queries, keys, values):
    rows = queries.shape[0]
    decay = decay[None, :]
    key_before = from_behind(keys)
    packet = from_behind(pack(se, mr, se_short, mr_short, 4))
    value_before = from_behind(values)
    own, se_mix, se_square = own_part(mr, se, mr_short, se_short, raw, decay, se_filter)
    there = jnp.where(lax.axis_index("ctx") == 0, rows, 0).astype(jnp.int32)[None]
    probs, attended, inverse = score(there, queries, keys, key_before, values, 4)
    head, mr_mix, square = mix(
        packet, own, se_square, mr, se, mr_short, se_short, raw, decay, se_filter
    )
    se_out, mr_out = normalize(of_panels(square), (se_mix, mr_mix), head)
    value_before, se_out, mr_out = lax.optimization_barrier((value_before, se_out, mr_out))
    attended, square = value_mix(probs, value_before, attended, inverse)
    (attn_out,) = normalize(of_panels(square), (attended,))
    return se_out, mr_out, attn_out


def solution(mesh):
    placed = (
        P(None, "ctx", "panel"),
        P(None, None, "panel"),
        P(None, "panel"),
        P(None, "ctx", "panel"),
        P(None, None, "panel"),
        P(None, "panel"),
        P("panel"),
        P("ctx", "panel"),
        P("ctx", "panel"),
        P("ctx", "panel"),
    )
    return jax.shard_map(
        body,
        mesh=mesh,
        in_specs=placed,
        out_specs=(P("ctx", "panel"), P("ctx", "panel"), P("ctx", "panel")),
        check_vma=False,
    )
```

time: 57.6 us -> 53.6 us (0.931)
  Pallas kernels: 34 us -> 29.2 us
  waiting for transfers between devices: 2.92 us -> 4.17 us
  starting transfers between devices: 13.7 us -> 12.5 us
  local copies, waits for them, and re-layouts: 5.81 us -> 6.48 us
    pallas_call x6, Pallas kernels: 32.8 us -> 25.3 us  [the longest x1 10.2 us: own_part(): pl.pallas_call(own_kernel, out_shape=(mixed, mixed, jax.ShapeDtypeStruct(...]
    pallas_call x1, Pallas kernels: 1.2 us -> 3.85 us  [pack(): pl.pallas_call(functools.partial(pack_kernel, per), grid=(blocks // per,)...]
    ppermute x3, waiting for transfers between devices: 2 us -> 3.26 us  [from_behind(): lax.ppermute(value, 'ctx', [(source, source + 1) for source in range(coun...]
    ppermute x2, starting transfers between devices: 4.37 us -> 3.13 us  [of_panels(): lax.ppermute(square, 'panel', [(n, (n + shift) % count) for n in range(co...]
    unnamed x18 -> x28, local copies, waits for them, and re-layouts: 5.81 us -> 6.48 us
  transfers between devices with their start and end apart: 5 -> 5, of which waited for: 3 -> 2; matrix products, arithmetic and copies ran while one was open for 0% -> 0% of each run, Pallas kernels for 54% -> 43%
where the time goes in v2:
time: 53.6 us; the launch traced here: 53.1 us
  Pallas kernels  29.2 us (54%)
  starting transfers between devices  12.5 us (23%)
  local copies, waits for them, and re-layouts  6.48 us (12%)
  waiting for transfers between devices  4.17 us (8%)
  between operations  0.85 us (2%)
    pallas_call x1, Pallas kernels, own_part(): pl.pallas_call(own_kernel, out_shape=(mixed, mixed, jax.ShapeDtypeStruct(...  10.2 us
    ppermute x3, starting transfers between devices, from_behind(): lax.ppermute(value, 'ctx', [(source, source + 1) for source in range(coun...  9.35 us
    pallas_call x1, Pallas kernels, mix(): pl.pallas_call(mix_kernel, out_shape=(jax.ShapeDtypeStruct((8, channels),...  7.39 us
    unnamed x28, local copies, waits for them, and re-layouts  6.48 us
    pallas_call x1, Pallas kernels, score(): pl.pallas_call(functools.partial(score_kernel, per), out_shape=(jax.Shape...  4.03 us
    pallas_call x1, Pallas kernels, pack(): pl.pallas_call(functools.partial(pack_kernel, per), grid=(blocks // per,)...  3.85 us
    ppermute x3, waiting for transfers between devices, from_behind(): lax.ppermute(value, 'ctx', [(source, source + 1) for source in range(coun...  3.26 us
    ppermute x2, starting transfers between devices, of_panels(): lax.ppermute(square, 'panel', [(n, (n + shift) % count) for n in range(co...  3.13 us
  transfers between devices with their start and end apart: 5, of which 2 were waited for; matrix products, arithmetic and copies ran while one was open for 0% of the time, Pallas kernels for 43%

profile of v2, /device:TPU:9, one launch (start us, length us, event | category | flops | bytes accessed | tf_op | source)
XLA Modules:
  0.0 53.1 jit_solution(9830054544090309227)
XLA Ops:
  0.6 0.0 copy-start.7
  0.6 0.0 copy-start.8
  0.7 0.0 copy-start.9
  0.7 0.0 copy-start.10
  0.7 0.0 copy-start
  0.7 0.0 copy-start.1
  0.7 3.8 %pack.1 = bf16[2320,128]{1,0:T(8,128)(2,1)} custom-call(bf16[3,144,2048]{2,1,0:T(8,128)(2,1)} %m_ref.3, bf16[3,144,2048]{2,1,0:T(8,128)(2,1)} %m_ref.3, bf16[3,144,2048]{2,1,0:T(8,128)(2,1)} %m_ref.3, bf16[3,144,2048]{2,1,0:T(8,128)(2,1)} %s_ref.3, bf16[3,144,2048]{2,1,0:T(8,128)(2,1)} %s_ref.3, bf16[3,144,2048]{2,1,0:T(8,128)(2,1)} %s_ref.3, ...), custom_call_target="tpu_custom_call" | custom-call | flops 5898240 | bytes 1769472 | tf_op jit(solution)/shard_map/pack/pallas_call | solution.py:119
  4.5 3.1 %collective-permute-start.1 = (bf16[2320,128]{1,0:T(8,128)(2,1)}, bf16[2320,128]{1,0:T(8,128)(2,1)S(1)}, u32[]{:S(2)}, u32[]{:S(2)}) collective-permute-start(bf16[2320,128]{1,0:T(8,128)(2,1)} %pack.1), channel_id=1, source_target_pairs={{0,2},{2,4},{4,6},{6,8},{8,10},{10,12},{12,14},{14,16},{16,18},{18... | collective-permute-start | bytes 1781768 | tf_op jit(solution)/shard_map/ppermute | solution.py:405
  7.7 3.1 %collective-permute-start.3 = (bf16[144,2048]{1,0:T(8,128)(2,1)}, bf16[144,2048]{1,0:T(8,128)(2,1)}, u32[]{:S(2)}, u32[]{:S(2)}) collective-permute-start(bf16[144,2048]{1,0:T(8,128)(2,1)} %k_ref.1), channel_id=1, source_target_pairs={{0,2},{2,4},{4,6},{6,8},{8,10},{10,12},{12,14},{14,16},{16,18},{18... | collective-permute-start | bytes 1769480 | tf_op jit(solution)/shard_map/ppermute | solution.py:405
  10.8 3.1 %collective-permute-start = (bf16[144,2048]{1,0:T(8,128)(2,1)}, bf16[144,2048]{1,0:T(8,128)(2,1)}, u32[]{:S(2)}, u32[]{:S(2)}) collective-permute-start(bf16[144,2048]{1,0:T(8,128)(2,1)} %v_ref.1), channel_id=1, source_target_pairs={{0,2},{2,4},{4,6},{6,8},{8,10},{10,12},{12,14},{14,16},{16,18},{18... | collective-permute-start | bytes 1769480 | tf_op jit(solution)/shard_map/ppermute | solution.py:405
  13.9 0.0 copy-done.7
  14.0 0.0 copy-start.2
  14.0 1.2 %copy-done.2 = f32[128,2048]{1,0:T(8,128)S(1)} copy-done((f32[128,2048]{1,0:T(8,128)S(1)}, f32[128,2048]{1,0:T(8,128)}, u32[]{:S(2)}) %copy-start.2) | copy-done | bytes 1048600
  15.2 10.2 %own_part.1 = (f32[144,2048]{1,0:T(8,128)S(1)}, f32[144,2048]{1,0:T(8,128)S(1)}, f32[144,128]{1,0:T(8,128)S(1)}) custom-call(bf16[3,144,2048]{2,1,0:T(8,128)(2,1)S(1)} %copy-done, bf16[3,144,2048]{2,1,0:T(8,128)(2,1)S(1)} %copy-done.1, f32[3,3,2048]{2,1,0:T(4,128)S(1)} %copy-done.7, f32[3,3,2048]{2,1,0:T(4,128)S(1)} %copy-done.8, f32[128,2048]{1,0:T(8,128)S(1)} %copy-done.2, ...), custom_call_target="tpu_custom_call" | custom-call | flops 53084160 | bytes 7077888 | tf_op jit(solution)/shard_map/own_part/pallas_call | solution.py:172
  25.4 1.0 %copy-done.3 = f32[144,2048]{1,0:T(8,128)} copy-done((f32[144,2048]{1,0:T(8,128)}, f32[144,2048]{1,0:T(8,128)S(1)}, u32[]{:S(2)}) %copy-start.3) | copy-done | bytes 1179672
  26.4 0.0 collective-permute-done.1.packet_ref
  26.4 7.4 %mix.1 = (f32[8,2048]{1,0:T(8,128)S(1)}, f32[144,2048]{1,0:T(8,128)S(1)}, f32[2,144,128]{2,1,0:T(8,128)S(1)}) custom-call(bf16[2320,128]{1,0:T(8,128)(2,1)S(1)} %collective-permute-done.1.packet_ref, f32[144,2048]{1,0:T(8,128)S(1)} %get-tuple-element.19.own_ref, f32[144,128]{1,0:T(8,128)S(1)} %get-tuple-element.20.se_square_ref, ...), custom_call_target="tpu_custom_call" | custom-call | flops 41287680 | bytes 4718592 | tf_op jit(solution)/shard_map/mix/pallas_call | solution.py:256
  33.8 0.0 copy-start.5
  33.8 1.0 %copy-done.5 = f32[144,2048]{1,0:T(8,128)} copy-done((f32[144,2048]{1,0:T(8,128)}, f32[144,2048]{1,0:T(8,128)S(1)}, u32[]{:S(2)}) %copy-start.5) | copy-done | bytes 1179672
  34.8 1.5 %collective-permute-start.2 = (f32[2,144,128]{2,1,0:T(8,128)S(1)}, f32[2,144,128]{2,1,0:T(8,128)S(1)}, u32[]{:S(2)}, u32[]{:S(2)}) collective-permute-start(f32[2,144,128]{2,1,0:T(8,128)S(1)} %get-tuple-element.21.refs_0_), channel_id=1, source_target_pairs={{0,1},{1,0},{2,3},{3,2},{4,5},{5,4},{6,7},{7,6},{8,9},{9,8},{10,11... | collective-permute-start | bytes 442376 | tf_op jit(solution)/shard_map/ppermute | solution.py:411
  36.4 0.0 collective-permute-done.3.before_ref
  36.4 1.1 %copy-done.11 = bf16[144,2048]{1,0:T(8,128)(2,1)S(1)} copy-done((bf16[144,2048]{1,0:T(8,128)(2,1)S(1)}, bf16[144,2048]{1,0:T(8,128)(2,1)}, u32[]{:S(2)}) %copy-start.11) | copy-done | bytes 589848
  37.4 1.1 %copy-done.12 = bf16[144,2048]{1,0:T(8,128)(2,1)S(1)} copy-done((bf16[144,2048]{1,0:T(8,128)(2,1)S(1)}, bf16[144,2048]{1,0:T(8,128)(2,1)}, u32[]{:S(2)}) %copy-start.12) | copy-done | bytes 589848
  38.5 1.1 %copy-done.13 = bf16[144,2048]{1,0:T(8,128)(2,1)S(1)} copy-done((bf16[144,2048]{1,0:T(8,128)(2,1)S(1)}, bf16[144,2048]{1,0:T(8,128)(2,1)}, u32[]{:S(2)}) %copy-start.13) | copy-done | bytes 589848
  39.6 4.0 %score.1 = (bf16[16,144,144]{2,1,0:T(8,128)(2,1)S(1)}, f32[144,2048]{1,0:T(8,128)S(1)}, f32[144,2048]{1,0:T(8,128)S(1)}) custom-call(s32[1]{0:T(128)} %bitcast.1.there_ref, bf16[144,2048]{1,0:T(8,128)(2,1)S(1)} %copy-done.11, bf16[144,2048]{1,0:T(8,128)(2,1)S(1)} %copy-done.12, bf16[144,2048]{1,0:T(8,128)(2,1)} %collective-permute-done.3.before_ref, ...), custom_call_target="tpu_custom_call" | custom-call | flops 339738624 | bytes 4128768 | tf_op jit(solution)/shard_map/score/pallas_call | solution.py:310
  43.6 0.0 collective-permute-done.2.refs_1_
  43.6 1.2 %normalize.2 = (bf16[144,2048]{1,0:T(8,128)(2,1)}, bf16[144,2048]{1,0:T(8,128)(2,1)}) custom-call(f32[2,144,128]{2,1,0:T(8,128)S(1)} %get-tuple-element.21.refs_0_, f32[2,144,128]{2,1,0:T(8,128)S(1)} %collective-permute-done.2.refs_1_, f32[144,2048]{1,0:T(8,128)S(1)} %copy-done.4, f32[144,2048]{1,0:T(8,128)S(1)} %copy-done.6, ...), custom_call_target="tpu_custom_call" | custom-call | flops 2359296 | bytes 3538944 | tf_op jit(solution)/shard_map/normalize/pallas_call | solution.py:388
  44.8 3.3 %collective-permute-done.before_ref = bf16[144,2048]{1,0:T(8,128)(2,1)} collective-permute-done((bf16[144,2048]{1,0:T(8,128)(2,1)}, bf16[144,2048]{1,0:T(8,128)(2,1)}, u32[]{:S(2)}, u32[]{:S(2)}) %collective-permute-start) | collective-permute-done | bytes 589856 | tf_op jit(solution)/shard_map/ppermute | solution.py:405
  48.1 1.5 %value_mix.1 = (f32[144,2048]{1,0:T(8,128)S(1)}, f32[1,144,128]{2,1,0:T(8,128)S(1)}) custom-call(bf16[16,144,144]{2,1,0:T(8,128)(2,1)S(1)} %get-tuple-element.29.probs_ref, bf16[144,2048]{1,0:T(8,128)(2,1)} %collective-permute-done.before_ref, f32[144,2048]{1,0:T(8,128)S(1)} %get-tuple-element.31.own_ref, f32[144,2048]{1,0:T(8,128)S(1)} %get-tuple-element.32.inverse_ref), custom_call_target="tpu_custom_call" | custom-call | flops 84934656 | bytes 3538944 | tf_op jit(solution)/shard_map/value_mix/pallas_call | solution.py:339
  49.6 1.6 %collective-permute-start.4 = (f32[1,144,128]{2,1,0:T(8,128)S(1)}, f32[1,144,128]{2,1,0:T(8,128)S(1)}, u32[]{:S(2)}, u32[]{:S(2)}) collective-permute-start(f32[1,144,128]{2,1,0:T(8,128)S(1)} %get-tuple-element.33.refs_0_), channel_id=1, source_target_pairs={{0,1},{1,0},{2,3},{3,2},{4,5},{5,4},{6,7},{7,6},{8,9},{9,8},{10,11... | collective-permute-start | bytes 221192 | tf_op jit(solution)/shard_map/ppermute | solution.py:411
  51.3 0.9 %collective-permute-done.4.refs_1_ = f32[1,144,128]{2,1,0:T(8,128)S(1)} collective-permute-done((f32[1,144,128]{2,1,0:T(8,128)S(1)}, f32[1,144,128]{2,1,0:T(8,128)S(1)}, u32[]{:S(2)}, u32[]{:S(2)}) %collective-permute-start.4) | collective-permute-done | bytes 73760 | tf_op jit(solution)/shard_map/ppermute | solution.py:411
  52.2 1.0 %normalize.3 = bf16[144,2048]{1,0:T(8,128)(2,1)} custom-call(f32[1,144,128]{2,1,0:T(8,128)S(1)} %get-tuple-element.33.refs_0_, f32[1,144,128]{2,1,0:T(8,128)S(1)} %collective-permute-done.4.refs_1_, f32[144,2048]{1,0:T(8,128)S(1)} %get-tuple-element.34.refs_2_), custom_call_target="tpu_custom_call" | custom-call | flops 1179648 | bytes 1769472 | tf_op jit(solution)/shard_map/normalize/pallas_call | solution.py:388
  (13 shorter events, 0.0 us)
Async XLA Ops:
  0.6 13.3 %copy-start.7 = (f32[3,3,2048]{2,1,0:T(4,128)S(1)}, f32[3,3,2048]{2,1,0:T(4,128)}, u32[]{:S(2)}) copy-start(f32[3,3,2048]{2,1,0:T(4,128)} %mw_ref.5) | copy-start | bytes 221188
  0.6 13.3 %copy-start.8 = (f32[3,3,2048]{2,1,0:T(4,128)S(1)}, f32[3,3,2048]{2,1,0:T(4,128)}, u32[]{:S(2)}) copy-start(f32[3,3,2048]{2,1,0:T(4,128)} %sw_ref.5) | copy-start | bytes 221188
  0.7 13.3 %copy-start.9 = (f32[7,2048]{1,0:T(8,128)S(1)}, f32[7,2048]{1,0:T(8,128)}, u32[]{:S(2)}) copy-start(f32[7,2048]{1,0:T(8,128)} %filter_ref.3) | copy-start | bytes 172036
  0.7 13.3 %copy-start.10 = (f32[2048]{0:T(1024)S(1)}, f32[2048]{0:T(1024)}, u32[]{:S(2)}) copy-start(f32[2048]{0:T(1024)} %param.16) | copy-start | bytes 24580
  0.7 13.3 %copy-start = (bf16[3,144,2048]{2,1,0:T(8,128)(2,1)S(1)}, bf16[3,144,2048]{2,1,0:T(8,128)(2,1)}, u32[]{:S(2)}) copy-start(bf16[3,144,2048]{2,1,0:T(8,128)(2,1)} %m_ref.3) | copy-start | bytes 5308420
  0.7 13.3 %copy-start.1 = (bf16[3,144,2048]{2,1,0:T(8,128)(2,1)S(1)}, bf16[3,144,2048]{2,1,0:T(8,128)(2,1)}, u32[]{:S(2)}) copy-start(bf16[3,144,2048]{2,1,0:T(8,128)(2,1)} %s_ref.3) | copy-start | bytes 5308420
  4.5 21.9 %collective-permute-start.1 = (bf16[2320,128]{1,0:T(8,128)(2,1)}, bf16[2320,128]{1,0:T(8,128)(2,1)S(1)}, u32[]{:S(2)}, u32[]{:S(2)}) collective-permute-start(bf16[2320,128]{1,0:T(8,128)(2,1)} %pack.1), channel_id=1, source_target_pairs={{0,2},{2,4},{4,6},{6,8},{8,10},{10,12},{12,14},{14,16},{16,18},{18... | collective-permute-start | bytes 1781768 | tf_op jit(solution)/shard_map/ppermute | solution.py:405
  7.7 28.7 %collective-permute-start.3 = (bf16[144,2048]{1,0:T(8,128)(2,1)}, bf16[144,2048]{1,0:T(8,128)(2,1)}, u32[]{:S(2)}, u32[]{:S(2)}) collective-permute-start(bf16[144,2048]{1,0:T(8,128)(2,1)} %k_ref.1), channel_id=1, source_target_pairs={{0,2},{2,4},{4,6},{6,8},{8,10},{10,12},{12,14},{14,16},{16,18},{18... | collective-permute-start | bytes 1769480 | tf_op jit(solution)/shard_map/ppermute | solution.py:405
  10.8 37.3 %collective-permute-start = (bf16[144,2048]{1,0:T(8,128)(2,1)}, bf16[144,2048]{1,0:T(8,128)(2,1)}, u32[]{:S(2)}, u32[]{:S(2)}) collective-permute-start(bf16[144,2048]{1,0:T(8,128)(2,1)} %v_ref.1), channel_id=1, source_target_pairs={{0,2},{2,4},{4,6},{6,8},{8,10},{10,12},{12,14},{14,16},{16,18},{18... | collective-permute-start | bytes 1769480 | tf_op jit(solution)/shard_map/ppermute | solution.py:405
  14.0 1.2 %copy-start.2 = (f32[128,2048]{1,0:T(8,128)S(1)}, f32[128,2048]{1,0:T(8,128)}, u32[]{:S(2)}) copy-start(f32[128,2048]{1,0:T(8,128)} %raw_ref.3) | copy-start | bytes 3145732
  25.4 1.0 %copy-start.3 = (f32[144,2048]{1,0:T(8,128)}, f32[144,2048]{1,0:T(8,128)S(1)}, u32[]{:S(2)}) copy-start(f32[144,2048]{1,0:T(8,128)S(1)} %get-tuple-element.22.refs_2_) | copy-start | bytes 3538948
  33.8 1.0 %copy-start.5 = (f32[144,2048]{1,0:T(8,128)}, f32[144,2048]{1,0:T(8,128)S(1)}, u32[]{:S(2)}) copy-start(f32[144,2048]{1,0:T(8,128)S(1)} %get-tuple-element.23.refs_3_) | copy-start | bytes 3538948
  34.8 8.8 %collective-permute-start.2 = (f32[2,144,128]{2,1,0:T(8,128)S(1)}, f32[2,144,128]{2,1,0:T(8,128)S(1)}, u32[]{:S(2)}, u32[]{:S(2)}) collective-permute-start(f32[2,144,128]{2,1,0:T(8,128)S(1)} %get-tuple-element.21.refs_0_), channel_id=1, source_target_pairs={{0,1},{1,0},{2,3},{3,2},{4,5},{5,4},{6,7},{7,6},{8,9},{9,8},{10,11... | collective-permute-start | bytes 442376 | tf_op jit(solution)/shard_map/ppermute | solution.py:411
  36.4 1.1 %copy-start.11 = (bf16[144,2048]{1,0:T(8,128)(2,1)S(1)}, bf16[144,2048]{1,0:T(8,128)(2,1)}, u32[]{:S(2)}) copy-start(bf16[144,2048]{1,0:T(8,128)(2,1)} %q_ref.1) | copy-start | bytes 1769476
  37.4 1.1 %copy-start.12 = (bf16[144,2048]{1,0:T(8,128)(2,1)S(1)}, bf16[144,2048]{1,0:T(8,128)(2,1)}, u32[]{:S(2)}) copy-start(bf16[144,2048]{1,0:T(8,128)(2,1)} %k_ref.1) | copy-start | bytes 1769476
  38.5 1.1 %copy-start.13 = (bf16[144,2048]{1,0:T(8,128)(2,1)S(1)}, bf16[144,2048]{1,0:T(8,128)(2,1)}, u32[]{:S(2)}) copy-start(bf16[144,2048]{1,0:T(8,128)(2,1)} %v_ref.1) | copy-start | bytes 1769476
  39.5 4.1 %copy-start.4 = (f32[144,2048]{1,0:T(8,128)S(1)}, f32[144,2048]{1,0:T(8,128)}, u32[]{:S(2)}) copy-start(f32[144,2048]{1,0:T(8,128)} %copy-done.3) | copy-start | bytes 3538948
  39.6 4.1 %copy-start.6 = (f32[144,2048]{1,0:T(8,128)S(1)}, f32[144,2048]{1,0:T(8,128)}, u32[]{:S(2)}) copy-start(f32[144,2048]{1,0:T(8,128)} %copy-done.5) | copy-start | bytes 3538948
  49.6 2.5 %collective-permute-start.4 = (f32[1,144,128]{2,1,0:T(8,128)S(1)}, f32[1,144,128]{2,1,0:T(8,128)S(1)}, u32[]{:S(2)}, u32[]{:S(2)}) collective-permute-start(f32[1,144,128]{2,1,0:T(8,128)S(1)} %get-tuple-element.33.refs_0_), channel_id=1, source_target_pairs={{0,1},{1,0},{2,3},{3,2},{4,5},{5,4},{6,7},{7,6},{8,9},{9,8},{10,11... | collective-permute-start | bytes 221192 | tf_op jit(solution)/shard_map/ppermute | solution.py:411

commit v3 on v2

--- a/solution.py
+++ b/solution.py
@@ -17,7 +17,7 @@
 BF16 = jnp.bfloat16
 
 
-def params(mebibytes=36):
+def params(mebibytes=6):
     return pltpu.CompilerParams(vmem_limit_bytes=mebibytes * 1024 * 1024)
 
 
@@ -54,43 +54,52 @@
     return pl.ds(pl.multiple_of(k * LANES, LANES), LANES)
 
 
-def write_taps(taps_ref, raw_ref, decay_ref, lanes):
-    steps = lax.broadcasted_iota(jnp.int32, (MEDIUM_TAPS, LANES), 0).astype(F32)
-    taps = raw_ref[:, lanes] * jnp.exp(-decay_ref[0:1, lanes] * steps)
-    taps_ref[...] = taps
-    return taps
-
-
-def tap_tile(taps_ref, j):
-    return jnp.broadcast_to(taps_ref[j : j + 1, :], (8, LANES))
-
-
-def pack_kernel(per, m1_ref, m2_ref, m0t_ref, s0t_ref, s1t_ref, s2t_ref, mw_ref, sw_ref, out_ref, last_ref):
-    step = pl.program_id(0)
-    rows = m1_ref.shape[1]
+def tap_tile(taps_ref, j, lanes):
+    return jnp.broadcast_to(taps_ref[j : j + 1, lanes], (8, LANES))
+
+
+def pack_kernel(
+    per, mr_ref, se_ref, mr_short_ref, se_short_ref, out_ref, m_ref, tail_ref, mw_ref, sw_ref, last_ref, sems
+):
+    _, rows, channels = mr_ref.shape
+    width = per * LANES
     chunk = MEDIUM_TAPS + 16
     nothing = jnp.zeros((8, LANES), F32)
-
-    @pl.when(step == 0)
-    def _():
-        last_ref[...] = jnp.zeros_like(last_ref)
-
-    @pl.loop(0, per)
-    def _(k):
-        lanes = lane_block(k)
-        block = step * per + k
-        m1 = m1_ref[0, :, lanes].astype(F32)
-        m2 = m2_ref[0, :, lanes].astype(F32)
+    end = pl.ds(rows - 16, 16)
+    copies = [
+        pltpu.make_async_copy(mr_short_ref, mw_ref, sems.at[0]),
+        pltpu.make_async_copy(se_short_ref, sw_ref, sems.at[1]),
+        pltpu.make_async_copy(mr_ref.at[pl.ds(0, 1), end], tail_ref.at[pl.ds(0, 1)], sems.at[2]),
+        pltpu.make_async_copy(se_ref.at[:, end], tail_ref.at[pl.ds(1, 3)], sems.at[3]),
+    ]
+    first = len(copies)
+    for n in range(channels // width):
+        at = pl.ds(n * width, width)
+        copies.append(
+            pltpu.make_async_copy(
+                mr_ref.at[pl.ds(1, 2), :, at], m_ref.at[:, :, at], sems.at[first + n]
+            )
+        )
+    for copy in copies:
+        copy.start()
+    for copy in copies[:first]:
+        copy.wait()
+    last_ref[...] = jnp.zeros_like(last_ref)
+
+    def one(block):
+        lanes = lane_block(block)
+        m1 = m_ref[0, :, lanes].astype(F32)
+        m2 = m_ref[1, :, lanes].astype(F32)
         z1 = features(m1, nothing, tap_rows(mw_ref, 1, lanes))
         z2 = features(m2, nothing, tap_rows(mw_ref, 2, lanes))
         product = (z1 * z2)[rows - MEDIUM_TAPS :]
-        tail_m0 = m0t_ref[0, :, lanes].astype(F32)[8:]
+        tail_m0 = tail_ref[0, :, lanes].astype(F32)[8:]
         tail_m1, tail_m2 = m1[rows - 8 :], m2[rows - 8 :]
         head = jnp.where(row_is(8, 0), roll(tail_m2, 2), product[:8])
         product = jnp.concatenate([head, product[8:]], axis=0)
-        s0 = s0t_ref[0, :, lanes].astype(F32)[8:]
-        s1 = s1t_ref[0, :, lanes].astype(F32)
-        s2 = s2t_ref[0, :, lanes].astype(F32)
+        s0 = tail_ref[1, :, lanes].astype(F32)[8:]
+        s1 = tail_ref[2, :, lanes].astype(F32)
+        s2 = tail_ref[3, :, lanes].astype(F32)
         y1 = features(s1, nothing, tap_rows(sw_ref, 1, lanes))[8:]
         y2 = features(s2, nothing, tap_rows(sw_ref, 2, lanes))[8:]
         at = lax.broadcasted_iota(jnp.int32, (8, LANES), 0)
@@ -105,6 +114,10 @@
         out_ref[pl.ds(start + MEDIUM_TAPS, 16), :] = jnp.concatenate([x1, x2], axis=0).astype(BF16)
         last_ref[pl.ds(block, 1), :] = tail_m2[7:8]
 
+    for n in range(channels // width):
+        copies[first + n].wait()
+        pl.loop(n * per, (n + 1) * per)(one)
+
     out_ref[out_ref.shape[0] - 16 :, :] = last_ref[...].astype(BF16)
 
 
@@ -112,33 +125,67 @@
     _, rows, channels = se.shape
     blocks = channels // LANES
     total = blocks * (MEDIUM_TAPS + 16) + 16
-    width = per * LANES
-    whole = lambda s: pl.BlockSpec((1, rows, width), lambda i: (s, 0, i))
-    tail = lambda s: pl.BlockSpec((1, 16, width), lambda i: (s, rows // 16 - 1, i))
-    short = pl.BlockSpec((3, 3, width), lambda i: (0, 0, i))
     return pl.pallas_call(
         functools.partial(pack_kernel, per),
-        grid=(blocks // per,),
         out_shape=jax.ShapeDtypeStruct((total, LANES), BF16),
-        in_specs=[whole(1), whole(2), tail(0), tail(0), tail(1), tail(2), short, short],
-        out_specs=pl.BlockSpec((total, LANES), lambda i: (0, 0)),
-        scratch_shapes=[pltpu.VMEM((16, LANES), F32)],
-        compiler_params=params(60),
+        in_specs=[pl.BlockSpec(memory_space=pltpu.HBM)] * 4,
+        out_specs=in_vmem(),
+        scratch_shapes=[
+            pltpu.VMEM((2, rows, channels), BF16),
+            pltpu.VMEM((4, 16, channels), BF16),
+            pltpu.VMEM(mr_short.shape, F32),
+            pltpu.VMEM(se_short.shape, F32),
+            pltpu.VMEM((16, LANES), F32),
+            pltpu.SemaphoreType.DMA((4 + blocks // per,)),
+        ],
+        compiler_params=params(),
         cost_estimate=cost(20 * rows * channels, 6 * rows * channels),
         name="pack",
-    )(mr, mr, mr, se, se, se, mr_short, se_short)
-
-
-def own_kernel(m_ref, s_ref, mw_ref, sw_ref, raw_ref, decay_ref, filter_ref, own_ref, se_ref, square_ref, taps_ref):
+    )(*(pltpu.with_memory_space_constraint(x, pltpu.HBM) for x in (mr, se, mr_short, se_short)))
+
+
+def own_kernel(
+    per,
+    m_ref,
+    s_ref,
+    mw_ref,
+    sw_ref,
+    raw_hbm_ref,
+    decay_ref,
+    filter_ref,
+    own_ref,
+    z0_ref,
+    se_ref,
+    square_ref,
+    taps_ref,
+    heads_ref,
+    raw_ref,
+    sems,
+):
     rows, channels = own_ref.shape
     tiles = rows // 8
+    width = per * LANES
     nothing = jnp.zeros((8, LANES), F32)
+
+    def fetch(n):
+        at = pl.ds(pl.multiple_of(n * width, width), width)
+        return pltpu.make_async_copy(raw_hbm_ref.at[:, at], raw_ref.at[:, at], sems.at[n])
+
+    for n in range(channels // width):
+        fetch(n).start()
     square_ref[...] = jnp.zeros_like(square_ref)
 
     @pl.loop(0, channels // LANES)
     def _(k):
+        @pl.when(k % per == 0)
+        def _():
+            fetch(k // per).wait()
+
         lanes = lane_block(k)
-        s = [features(s_ref[n, :, lanes].astype(F32), nothing, tap_rows(sw_ref, n, lanes)) for n in range(3)]
+        u = [s_ref[n, :, lanes].astype(F32) for n in range(3)]
+        for n in range(3):
+            heads_ref[n, :, lanes] = u[n][:8]
+        s = [features(u[n], nothing, tap_rows(sw_ref, n, lanes)) for n in range(3)]
         ext = jnp.concatenate([nothing, (s[1] * s[2]).astype(BF16).astype(F32)], axis=0)
         total = filter_ref[0:1, lanes] * ext
         for j in range(1, LSE):
@@ -147,17 +194,21 @@
         se_ref[:, lanes] = mixed
         square_ref[8:, :] += mixed[8:] * mixed[8:]
 
-        write_taps(taps_ref, raw_ref, decay_ref, lanes)
-        z1 = features(m_ref[1, :, lanes].astype(F32), nothing, tap_rows(mw_ref, 1, lanes))
-        z2 = features(m_ref[2, :, lanes].astype(F32), nothing, tap_rows(mw_ref, 2, lanes))
-        product = (z1 * z2).astype(BF16).astype(F32)
+        steps = lax.broadcasted_iota(jnp.int32, (MEDIUM_TAPS, LANES), 0).astype(F32)
+        taps_ref[:, lanes] = raw_ref[:, lanes] * jnp.exp(-decay_ref[0:1, lanes] * steps)
+        u = [m_ref[n, :, lanes].astype(F32) for n in range(3)]
+        for n in range(3):
+            heads_ref[3 + n, :, lanes] = u[n][:8]
+        z = [features(u[n], nothing, tap_rows(mw_ref, n, lanes)) for n in range(3)]
+        z0_ref[:, lanes] = z[0]
+        product = (z[1] * z[2]).astype(BF16).astype(F32)
         at = lax.broadcasted_iota(jnp.int32, (8, LANES), 0)
         head = jnp.where(at < 2, 0.0, product[:8])
         ext = jnp.concatenate([nothing, head, product[8:]], axis=0)
         total = [None] * tiles
         for r in range(8):
             shifted = roll(ext, r)
-            tap = [tap_tile(taps_ref, 8 * a + r) for a in range(MEDIUM_TAPS // 8)]
+            tap = [tap_tile(taps_ref, 8 * a + r, lanes) for a in range(MEDIUM_TAPS // 8)]
             for i in range(tiles):
                 for a in range(min(i + 1, MEDIUM_TAPS // 8)):
                     at_tile = 8 * (i - a + 1)
@@ -166,15 +217,26 @@
         own_ref[:, lanes] = jnp.concatenate(total, axis=0)
 
 
-def own_part(mr, se, mr_short, se_short, raw, decay, se_filter):
+def own_part(mr, se, mr_short, se_short, raw, decay, se_filter, per):
     _, rows, channels = mr.shape
     mixed = jax.ShapeDtypeStruct((rows, channels), F32)
+    raw = pltpu.with_memory_space_constraint(raw, pltpu.HBM)
     return pl.pallas_call(
-        own_kernel,
-        out_shape=(mixed, mixed, jax.ShapeDtypeStruct((rows, LANES), F32)),
-        in_specs=[in_vmem()] * 7,
-        out_specs=(in_vmem(),) * 3,
-        scratch_shapes=[pltpu.VMEM((MEDIUM_TAPS, LANES), F32)],
+        functools.partial(own_kernel, per),
+        out_shape=(
+            mixed,
+            mixed,
+            mixed,
+            jax.ShapeDtypeStruct((rows, LANES), F32),
+            jax.ShapeDtypeStruct((MEDIUM_TAPS, channels), F32),
+            jax.ShapeDtypeStruct((6, 8, channels), F32),
+        ),
+        in_specs=[in_vmem()] * 4 + [pl.BlockSpec(memory_space=pltpu.HBM)] + [in_vmem()] * 2,
+        out_specs=(in_vmem(),) * 6,
+        scratch_shapes=[
+            pltpu.VMEM((MEDIUM_TAPS, channels), F32),
+            pltpu.SemaphoreType.DMA((channels // (per * LANES),)),
+        ],
         compiler_params=params(),
         cost_estimate=cost(180 * rows * channels, 24 * rows * channels),
         name="own_part",
@@ -184,18 +246,16 @@
 def mix_kernel(
     packet_ref,
     own_ref,
+    z0_ref,
     se_square_ref,
-    m_ref,
-    s_ref,
+    taps_ref,
+    heads_ref,
     mw_ref,
     sw_ref,
-    raw_ref,
-    decay_ref,
     filter_ref,
     head_ref,
     mr_ref,
     square_ref,
-    taps_ref,
     last_ref,
 ):
     rows, channels = own_ref.shape
@@ -217,7 +277,7 @@
 
         fronts = (roll(x1, 6), roll(x2, 6), roll(x2, 4))
         s = [
-            features(s_ref[n, :16, lanes].astype(F32)[:8], fronts[n], tap_rows(sw_ref, n, lanes))
+            features(heads_ref[n, :, lanes], fronts[n], tap_rows(sw_ref, n, lanes))
             for n in range(3)
         ]
         ext = jnp.concatenate([x1, (s[1] * s[2]).astype(BF16).astype(F32)], axis=0)
@@ -228,12 +288,14 @@
         head_ref[:, lanes] = mixed
         square_ref[0, :8, :] += mixed * mixed
 
-        taps = write_taps(taps_ref, raw_ref, decay_ref, lanes)
-        z0 = features(m_ref[0, :, lanes].astype(F32), roll(x2, 2), tap_rows(mw_ref, 0, lanes))
+        taps = taps_ref[:, lanes]
         front2 = jnp.where(row_is(8, 7), last, roll(before[:8], 6))
-        z1 = features(m_ref[1, :16, lanes].astype(F32)[:8], x2, tap_rows(mw_ref, 1, lanes))
-        z2 = features(m_ref[2, :16, lanes].astype(F32)[:8], front2, tap_rows(mw_ref, 2, lanes))
-        first = (z1 * z2).astype(BF16).astype(F32)
+        fronts = (roll(x2, 2), x2, front2)
+        z = [
+            features(heads_ref[3 + n, :, lanes], fronts[n], tap_rows(mw_ref, n, lanes))
+            for n in range(3)
+        ]
+        first = (z[1] * z[2]).astype(BF16).astype(F32)
         padded = jnp.concatenate([taps, jnp.zeros((rows - MEDIUM_TAPS, LANES), F32)], axis=0)
         base = own_ref[:, lanes] + padded * first[0:1] + roll(padded, 1) * first[1:2]
         total = [base[8 * i : 8 * i + 8] for i in range(tiles)]
@@ -241,18 +303,19 @@
         count = MEDIUM_TAPS // 8
         for r in range(8):
             shifted = roll(ext, r)
-            tap = [tap_tile(taps_ref, 8 * a + r) for a in range(count)]
+            tap = [tap_tile(taps_ref, 8 * a + r, lanes) for a in range(count)]
             for i in range(count):
                 for a in range(i if r else i + 1, count):
                     at_tile = 8 * (i - a + count)
                     total[i] = total[i] + tap[a] * shifted[at_tile : at_tile + 8]
+        z0 = jnp.concatenate([z[0], z0_ref[8:, lanes]], axis=0)
         mixed = z0 * jnp.concatenate(total, axis=0)
         mr_ref[:, lanes] = mixed
         square_ref[1] += mixed * mixed
 
 
-def mix(packet, own, se_square, mr, se, mr_short, se_short, raw, decay, se_filter):
-    _, rows, channels = mr.shape
+def mix(packet, own, z0, se_square, taps, heads, mr_short, se_short, se_filter):
+    rows, channels = own.shape
     return pl.pallas_call(
         mix_kernel,
         out_shape=(
@@ -260,13 +323,13 @@
             jax.ShapeDtypeStruct((rows, channels), F32),
             jax.ShapeDtypeStruct((2, rows, LANES), F32),
         ),
-        in_specs=[in_vmem()] * 10,
+        in_specs=[in_vmem()] * 9,
         out_specs=(in_vmem(),) * 3,
-        scratch_shapes=[pltpu.VMEM((MEDIUM_TAPS, LANES), F32), pltpu.VMEM((16, LANES), F32)],
+        scratch_shapes=[pltpu.VMEM((16, LANES), F32)],
         compiler_params=params(),
         cost_estimate=cost(140 * rows * channels, 16 * rows * channels),
         name="mix",
-    )(packet, own, se_square, mr, se, mr_short, se_short, raw, decay, se_filter)
+    )(packet, own, z0, se_square, taps, heads, mr_short, se_short, se_filter)
 
 
 def score_kernel(per, there_ref, q_ref, k_ref, before_ref, v_ref, probs_ref, out_ref, inverse_ref, bias_ref):
@@ -418,12 +481,16 @@
     decay = decay[None, :]
     key_before = from_behind(keys)
     packet = from_behind(pack(se, mr, se_short, mr_short, 4))
-    value_before = from_behind(values)
-    own, se_mix, se_square = own_part(mr, se, mr_short, se_short, raw, decay, se_filter)
+    own, z0, se_mix, se_square, taps, heads = own_part(
+        mr, se, mr_short, se_short, raw, decay, se_filter, 4
+    )
+    values_later, own = lax.optimization_barrier((values, own))
+    value_before = from_behind(values_later)
     there = jnp.where(lax.axis_index("ctx") == 0, rows, 0).astype(jnp.int32)[None]
     probs, attended, inverse = score(there, queries, keys, key_before, values, 4)
+    packet, attended = lax.optimization_barrier((packet, attended))
     head, mr_mix, square = mix(
-        packet, own, se_square, mr, se, mr_short, se_short, raw, decay, se_filter
+        packet, own, z0, se_square, taps, heads, mr_short, se_short, se_filter
     )
     se_out, mr_out = normalize(of_panels(square), (se_mix, mr_mix), head)
     value_before, se_out, mr_out = lax.optimization_barrier((value_before, se_out, mr_out))

time: 53.6 us -> 54.7 us (1.021)
  the two profiles are of different devices: /device:TPU:9 before, /device:TPU:0 now
where the time goes in v3:
time: 54.7 us; the launch traced here: 54.3 us
  Pallas kernels  33.3 us (61%)
  starting transfers between devices  13.1 us (24%)
  local copies, waits for them, and re-layouts  4.57 us (8%)
  waiting for transfers between devices  2.48 us (5%)
  between operations  0.84 us (2%)
    ppermute x3, starting transfers between devices, from_behind(): lax.ppermute(value, 'ctx', [(source, source + 1) for source in range(coun...  12.8 us
    pallas_call x1, Pallas kernels, own_part(): pl.pallas_call(functools.partial(own_kernel, per), out_shape=(mixed, mixe...  11.9 us
    pallas_call x1, Pallas kernels, mix(): pl.pallas_call(mix_kernel, out_shape=(jax.ShapeDtypeStruct((8, channels),...  10.5 us
    unnamed x34, local copies, waits for them, and re-layouts  4.57 us
    pallas_call x1, Pallas kernels, score(): pl.pallas_call(functools.partial(score_kernel, per), out_shape=(jax.Shape...  4.19 us
    pallas_call x1, Pallas kernels, pack(): pl.pallas_call(functools.partial(pack_kernel, per), out_shape=jax.ShapeDt...  3.03 us
    ppermute x2, waiting for transfers between devices, of_panels(): lax.ppermute(square, 'panel', [(n, (n + shift) % count) for n in range(co...  2.47 us
    pallas_call x2, Pallas kernels, normalize(): pl.pallas_call(functools.partial(normalize_kernel, count, len(squares), p...  2.19 us
  transfers between devices with their start and end apart: 5, of which 2 were waited for; matrix products, arithmetic and copies ran while one was open for 0% of the time, Pallas kernels for 57%

profile of v3, /device:TPU:0, one launch (start us, length us, event | category | flops | bytes accessed | tf_op | source)
XLA Modules:
  0.0 54.3 jit_solution(13074183705769446097)
XLA Ops:
  0.6 0.0 copy-start.4
  0.6 0.0 copy-start.6
  0.7 0.0 copy-start.10
  0.7 5.9 %collective-permute-start.2 = (bf16[144,2048]{1,0:T(8,128)(2,1)}, bf16[144,2048]{1,0:T(8,128)(2,1)}, u32[]{:S(2)}, u32[]{:S(2)}) collective-permute-start(bf16[144,2048]{1,0:T(8,128)(2,1)} %k_ref.1), channel_id=1, source_target_pairs={{0,2},{2,4},{4,6},{6,8},{8,10},{10,12},{12,14},{14,16},{16,18},{18... | collective-permute-start | bytes 1769480 | tf_op jit(solution)/shard_map/ppermute | solution.py:468
  6.6 3.0 %pack.1 = bf16[2320,128]{1,0:T(8,128)(2,1)} custom-call(bf16[3,144,2048]{2,1,0:T(8,128)(2,1)} %mr_ref.1, bf16[3,144,2048]{2,1,0:T(8,128)(2,1)} %se_ref.1, f32[3,3,2048]{2,1,0:T(4,128)} %mw_ref.3, f32[3,3,2048]{2,1,0:T(4,128)} %sw_ref.3), custom_call_target="tpu_custom_call" | custom-call | flops 5898240 | bytes 1769472 | tf_op jit(solution)/shard_map/pack/pallas_call | solution.py:128
  9.7 3.4 %collective-permute-start.1 = (bf16[2320,128]{1,0:T(8,128)(2,1)}, bf16[2320,128]{1,0:T(8,128)(2,1)}, u32[]{:S(2)}, u32[]{:S(2)}) collective-permute-start(bf16[2320,128]{1,0:T(8,128)(2,1)} %pack.1), channel_id=1, source_target_pairs={{0,2},{2,4},{4,6},{6,8},{8,10},{10,12},{12,14},{14,16},{16,18},{18... | collective-permute-start | bytes 1781768 | tf_op jit(solution)/shard_map/ppermute | solution.py:468
  13.1 0.0 copy-done.6
  13.1 0.0 copy-done.1
  13.2 11.9 %own_part.1 = (f32[144,2048]{1,0:T(8,128)S(1)}, f32[144,2048]{1,0:T(8,128)S(1)}, f32[144,2048]{1,0:T(8,128)S(1)}, f32[144,128]{1,0:T(8,128)S(1)}, f32[128,2048]{1,0:T(8,128)S(1)}, /*index=5*/f32[6,8,2048]{2,1,0:T(8,128)S(1)}) custom-call(bf16[3,144,2048]{2,1,0:T(8,128)(2,1)S(1)} %copy-done, bf16[3,144,2048]{2,1,0:T(8,128)(2,1)S(1)} %copy-done.1, ...), custom_call_target="tpu_custom_call" | custom-call | flops 53084160 | bytes 7077888 | tf_op jit(solution)/shard_map/own_part/pallas_call | solution.py:224
  25.0 1.0 %copy-done.2 = f32[128,2048]{1,0:T(8,128)} copy-done((f32[128,2048]{1,0:T(8,128)}, f32[128,2048]{1,0:T(8,128)S(1)}, u32[]{:S(2)}) %copy-start.2) | copy-done | bytes 1048600
  26.0 0.7 %copy-done.8 = f32[6,8,2048]{2,1,0:T(8,128)} copy-done((f32[6,8,2048]{2,1,0:T(8,128)}, f32[6,8,2048]{2,1,0:T(8,128)S(1)}, u32[]{:S(2)}) %copy-start.8) | copy-done | bytes 393240
  26.8 0.6 %copy-done.12 = f32[144,128]{1,0:T(8,128)} copy-done((f32[144,128]{1,0:T(8,128)}, f32[144,128]{1,0:T(8,128)S(1)}, u32[]{:S(2)}) %copy-start.12) | copy-done | bytes 73752
  27.4 3.4 %collective-permute-start = (bf16[144,2048]{1,0:T(8,128)(2,1)}, bf16[144,2048]{1,0:T(8,128)(2,1)}, u32[]{:S(2)}, u32[]{:S(2)}) collective-permute-start(bf16[144,2048]{1,0:T(8,128)(2,1)} %v_ref.1), channel_id=1, source_target_pairs={{0,2},{2,4},{4,6},{6,8},{8,10},{10,12},{12,14},{14,16},{16,18},{18... | collective-permute-start | bytes 1769480 | tf_op jit(solution)/shard_map/ppermute | solution.py:468
  30.8 0.0 collective-permute-done.2.before_ref
  30.8 1.1 %copy-done.15 = bf16[144,2048]{1,0:T(8,128)(2,1)S(1)} copy-done((bf16[144,2048]{1,0:T(8,128)(2,1)S(1)}, bf16[144,2048]{1,0:T(8,128)(2,1)}, u32[]{:S(2)}) %copy-start.15) | copy-done | bytes 589848
  31.9 1.1 %copy-done.16 = bf16[144,2048]{1,0:T(8,128)(2,1)S(1)} copy-done((bf16[144,2048]{1,0:T(8,128)(2,1)S(1)}, bf16[144,2048]{1,0:T(8,128)(2,1)}, u32[]{:S(2)}) %copy-start.16) | copy-done | bytes 589848
  33.0 0.0 copy-start.11
  33.0 0.0 copy-start.13
  33.0 4.2 %score.1 = (bf16[16,144,144]{2,1,0:T(8,128)(2,1)S(1)}, f32[144,2048]{1,0:T(8,128)S(1)}, f32[144,2048]{1,0:T(8,128)S(1)}) custom-call(s32[1]{0:T(128)} %bitcast.1.there_ref, bf16[144,2048]{1,0:T(8,128)(2,1)S(1)} %copy-done.15, bf16[144,2048]{1,0:T(8,128)(2,1)S(1)} %copy-done.16, bf16[144,2048]{1,0:T(8,128)(2,1)} %collective-permute-done.2.before_ref, ...), custom_call_target="tpu_custom_call" | custom-call | flops 339738624 | bytes 4128768 | tf_op jit(solution)/shard_map/score/pallas_call | solution.py:373
  37.2 0.0 collective-permute-done.1.packet_ref
  37.2 0.0 copy-done.3
  37.2 0.0 copy-done.5
  37.2 0.0 copy-done.7
  37.3 10.5 %mix.1 = (f32[8,2048]{1,0:T(8,128)S(1)}, f32[144,2048]{1,0:T(8,128)S(1)}, f32[2,144,128]{2,1,0:T(8,128)S(1)}) custom-call(bf16[2320,128]{1,0:T(8,128)(2,1)} %collective-permute-done.1.packet_ref, f32[144,2048]{1,0:T(8,128)S(1)} %get-tuple-element.30.own_ref, f32[144,2048]{1,0:T(8,128)S(1)} %get-tuple-element.31.z0_ref, f32[144,128]{1,0:T(8,128)S(1)} %copy-done.13, ...), custom_call_target="tpu_custom_call" | custom-call | flops 41287680 | bytes 4718592 | tf_op jit(solution)/shard_map/mix/pallas_call | solution.py:319
  47.7 0.1 collective-permute-start.3
  47.8 1.4 %collective-permute-done.3.refs_1_ = f32[2,144,128]{2,1,0:T(8,128)S(1)} collective-permute-done((f32[2,144,128]{2,1,0:T(8,128)S(1)}, f32[2,144,128]{2,1,0:T(8,128)S(1)}, u32[]{:S(2)}, u32[]{:S(2)}) %collective-permute-start.3) | collective-permute-done | bytes 147488 | tf_op jit(solution)/shard_map/ppermute | solution.py:474
  49.2 1.2 %normalize.2 = (bf16[144,2048]{1,0:T(8,128)(2,1)}, bf16[144,2048]{1,0:T(8,128)(2,1)}) custom-call(f32[2,144,128]{2,1,0:T(8,128)S(1)} %get-tuple-element.35.refs_0_, f32[2,144,128]{2,1,0:T(8,128)S(1)} %collective-permute-done.3.refs_1_, f32[144,2048]{1,0:T(8,128)S(1)} %get-tuple-element.36.refs_2_, f32[144,2048]{1,0:T(8,128)S(1)} %get-tuple-element.37.refs_3_, ...), custom_call_target="tpu_custom_call" | custom-call | flops 2359296 | bytes 3538944 | tf_op jit(solution)/shard_map/normalize/pallas_call | solution.py:451
  50.4 0.0 collective-permute-done.before_ref
  50.4 1.5 %value_mix.1 = (f32[144,2048]{1,0:T(8,128)S(1)}, f32[1,144,128]{2,1,0:T(8,128)S(1)}) custom-call(bf16[16,144,144]{2,1,0:T(8,128)(2,1)S(1)} %get-tuple-element.43.probs_ref, bf16[144,2048]{1,0:T(8,128)(2,1)} %collective-permute-done.before_ref, f32[144,2048]{1,0:T(8,128)S(1)} %get-tuple-element.45.own_ref, f32[144,2048]{1,0:T(8,128)S(1)} %get-tuple-element.46.inverse_ref), custom_call_target="tpu_custom_call" | custom-call | flops 84934656 | bytes 3538944 | tf_op jit(solution)/shard_map/value_mix/pallas_call | solution.py:402
  52.0 0.2 collective-permute-start.4
  52.2 1.1 %collective-permute-done.4.refs_1_ = f32[1,144,128]{2,1,0:T(8,128)S(1)} collective-permute-done((f32[1,144,128]{2,1,0:T(8,128)S(1)}, f32[1,144,128]{2,1,0:T(8,128)S(1)}, u32[]{:S(2)}, u32[]{:S(2)}) %collective-permute-start.4) | collective-permute-done | bytes 73760 | tf_op jit(solution)/shard_map/ppermute | solution.py:474
  53.3 1.0 %normalize.3 = bf16[144,2048]{1,0:T(8,128)(2,1)} custom-call(f32[1,144,128]{2,1,0:T(8,128)S(1)} %get-tuple-element.47.refs_0_, f32[1,144,128]{2,1,0:T(8,128)S(1)} %collective-permute-done.4.refs_1_, f32[144,2048]{1,0:T(8,128)S(1)} %get-tuple-element.48.refs_2_), custom_call_target="tpu_custom_call" | custom-call | flops 1179648 | bytes 1769472 | tf_op jit(solution)/shard_map/normalize/pallas_call | solution.py:451
  (19 shorter events, 0.0 us)
Async XLA Ops:
  0.6 12.5 %copy-start.4 = (f32[3,3,2048]{2,1,0:T(4,128)S(1)}, f32[3,3,2048]{2,1,0:T(4,128)}, u32[]{:S(2)}) copy-start(f32[3,3,2048]{2,1,0:T(4,128)} %mw_ref.3) | copy-start | bytes 221188
  0.6 12.5 %copy-start.6 = (f32[3,3,2048]{2,1,0:T(4,128)S(1)}, f32[3,3,2048]{2,1,0:T(4,128)}, u32[]{:S(2)}) copy-start(f32[3,3,2048]{2,1,0:T(4,128)} %sw_ref.3) | copy-start | bytes 221188
  0.7 12.5 %copy-start = (bf16[3,144,2048]{2,1,0:T(8,128)(2,1)S(1)}, bf16[3,144,2048]{2,1,0:T(8,128)(2,1)}, u32[]{:S(2)}) copy-start(bf16[3,144,2048]{2,1,0:T(8,128)(2,1)} %mr_ref.1) | copy-start | bytes 5308420
  0.7 12.5 %copy-start.1 = (bf16[3,144,2048]{2,1,0:T(8,128)(2,1)S(1)}, bf16[3,144,2048]{2,1,0:T(8,128)(2,1)}, u32[]{:S(2)}) copy-start(bf16[3,144,2048]{2,1,0:T(8,128)(2,1)} %se_ref.1) | copy-start | bytes 5308420
  0.7 12.5 %copy-start.10 = (f32[7,2048]{1,0:T(8,128)S(1)}, f32[7,2048]{1,0:T(8,128)}, u32[]{:S(2)}) copy-start(f32[7,2048]{1,0:T(8,128)} %filter_ref.3) | copy-start | bytes 172036
  0.7 12.5 %copy-start.14 = (f32[2048]{0:T(1024)S(1)}, f32[2048]{0:T(1024)}, u32[]{:S(2)}) copy-start(f32[2048]{0:T(1024)} %param.16) | copy-start | bytes 24580
  0.7 30.1 %collective-permute-start.2 = (bf16[144,2048]{1,0:T(8,128)(2,1)}, bf16[144,2048]{1,0:T(8,128)(2,1)}, u32[]{:S(2)}, u32[]{:S(2)}) collective-permute-start(bf16[144,2048]{1,0:T(8,128)(2,1)} %k_ref.1), channel_id=1, source_target_pairs={{0,2},{2,4},{4,6},{6,8},{8,10},{10,12},{12,14},{14,16},{16,18},{18... | collective-permute-start | bytes 1769480 | tf_op jit(solution)/shard_map/ppermute | solution.py:468
  9.7 27.5 %collective-permute-start.1 = (bf16[2320,128]{1,0:T(8,128)(2,1)}, bf16[2320,128]{1,0:T(8,128)(2,1)}, u32[]{:S(2)}, u32[]{:S(2)}) collective-permute-start(bf16[2320,128]{1,0:T(8,128)(2,1)} %pack.1), channel_id=1, source_target_pairs={{0,2},{2,4},{4,6},{6,8},{8,10},{10,12},{12,14},{14,16},{16,18},{18... | collective-permute-start | bytes 1781768 | tf_op jit(solution)/shard_map/ppermute | solution.py:468
  25.0 1.0 %copy-start.2 = (f32[128,2048]{1,0:T(8,128)}, f32[128,2048]{1,0:T(8,128)S(1)}, u32[]{:S(2)}) copy-start(f32[128,2048]{1,0:T(8,128)S(1)} %get-tuple-element.33.taps_ref) | copy-start | bytes 3145732
  26.0 0.7 %copy-start.8 = (f32[6,8,2048]{2,1,0:T(8,128)}, f32[6,8,2048]{2,1,0:T(8,128)S(1)}, u32[]{:S(2)}) copy-start(f32[6,8,2048]{2,1,0:T(8,128)S(1)} %get-tuple-element.34.heads_ref) | copy-start | bytes 1179652
  26.8 0.6 %copy-start.12 = (f32[144,128]{1,0:T(8,128)}, f32[144,128]{1,0:T(8,128)S(1)}, u32[]{:S(2)}) copy-start(f32[144,128]{1,0:T(8,128)S(1)} %get-tuple-element.32.se_square_ref) | copy-start | bytes 221188
  27.4 23.0 %collective-permute-start = (bf16[144,2048]{1,0:T(8,128)(2,1)}, bf16[144,2048]{1,0:T(8,128)(2,1)}, u32[]{:S(2)}, u32[]{:S(2)}) collective-permute-start(bf16[144,2048]{1,0:T(8,128)(2,1)} %v_ref.1), channel_id=1, source_target_pairs={{0,2},{2,4},{4,6},{6,8},{8,10},{10,12},{12,14},{14,16},{16,18},{18... | collective-permute-start | bytes 1769480 | tf_op jit(solution)/shard_map/ppermute | solution.py:468
  30.8 1.1 %copy-start.15 = (bf16[144,2048]{1,0:T(8,128)(2,1)S(1)}, bf16[144,2048]{1,0:T(8,128)(2,1)}, u32[]{:S(2)}) copy-start(bf16[144,2048]{1,0:T(8,128)(2,1)} %q_ref.1) | copy-start | bytes 1769476
  31.9 1.1 %copy-start.16 = (bf16[144,2048]{1,0:T(8,128)(2,1)S(1)}, bf16[144,2048]{1,0:T(8,128)(2,1)}, u32[]{:S(2)}) copy-start(bf16[144,2048]{1,0:T(8,128)(2,1)} %k_ref.1) | copy-start | bytes 1769476
  33.0 4.2 %copy-start.3 = (f32[128,2048]{1,0:T(8,128)S(1)}, f32[128,2048]{1,0:T(8,128)}, u32[]{:S(2)}) copy-start(f32[128,2048]{1,0:T(8,128)} %copy-done.2) | copy-start | bytes 3145732
  33.0 4.3 %copy-start.5 = (f32[3,3,2048]{2,1,0:T(4,128)S(1)}, f32[3,3,2048]{2,1,0:T(4,128)}, u32[]{:S(2)}) copy-start(f32[3,3,2048]{2,1,0:T(4,128)} %mw_ref.3) | copy-start | bytes 221188
  33.0 4.3 %copy-start.7 = (f32[3,3,2048]{2,1,0:T(4,128)S(1)}, f32[3,3,2048]{2,1,0:T(4,128)}, u32[]{:S(2)}) copy-start(f32[3,3,2048]{2,1,0:T(4,128)} %sw_ref.3) | copy-start | bytes 221188
  33.0 4.3 %copy-start.9 = (f32[6,8,2048]{2,1,0:T(8,128)S(1)}, f32[6,8,2048]{2,1,0:T(8,128)}, u32[]{:S(2)}) copy-start(f32[6,8,2048]{2,1,0:T(8,128)} %copy-done.8) | copy-start | bytes 1179652
  33.0 4.3 %copy-start.11 = (f32[7,2048]{1,0:T(8,128)S(1)}, f32[7,2048]{1,0:T(8,128)}, u32[]{:S(2)}) copy-start(f32[7,2048]{1,0:T(8,128)} %filter_ref.3) | copy-start | bytes 172036
  33.0 4.3 %copy-start.13 = (f32[144,128]{1,0:T(8,128)S(1)}, f32[144,128]{1,0:T(8,128)}, u32[]{:S(2)}) copy-start(f32[144,128]{1,0:T(8,128)} %copy-done.12) | copy-start | bytes 221188
  47.7 1.4 %collective-permute-start.3 = (f32[2,144,128]{2,1,0:T(8,128)S(1)}, f32[2,144,128]{2,1,0:T(8,128)S(1)}, u32[]{:S(2)}, u32[]{:S(2)}) collective-permute-start(f32[2,144,128]{2,1,0:T(8,128)S(1)} %get-tuple-element.35.refs_0_), channel_id=1, source_target_pairs={{0,1},{1,0},{2,3},{3,2},{4,5},{5,4},{6,7},{7,6},{8,9},{9,8},{10,11... | collective-permute-start | bytes 442376 | tf_op jit(solution)/shard_map/ppermute | solution.py:474
  52.0 1.3 %collective-permute-start.4 = (f32[1,144,128]{2,1,0:T(8,128)S(1)}, f32[1,144,128]{2,1,0:T(8,128)S(1)}, u32[]{:S(2)}, u32[]{:S(2)}) collective-permute-start(f32[1,144,128]{2,1,0:T(8,128)S(1)} %get-tuple-element.47.refs_0_), channel_id=1, source_target_pairs={{0,1},{1,0},{2,3},{3,2},{4,5},{5,4},{6,7},{7,6},{8,9},{9,8},{10,11... | collective-permute-start | bytes 221192 | tf_op jit(solution)/shard_map/ppermute | solution.py:474

commit v4 on v3

--- a/solution.py
+++ b/solution.py
@@ -54,8 +54,8 @@
     return pl.ds(pl.multiple_of(k * LANES, LANES), LANES)
 
 
-def tap_tile(taps_ref, j, lanes):
-    return jnp.broadcast_to(taps_ref[j : j + 1, lanes], (8, LANES))
+def tap_tile(held_ref, j):
+    return jnp.broadcast_to(held_ref[j : j + 1, :], (8, LANES))
 
 
 def pack_kernel(
@@ -160,6 +160,7 @@
     taps_ref,
     heads_ref,
     raw_ref,
+    held_ref,
     sems,
 ):
     rows, channels = own_ref.shape
@@ -195,7 +196,9 @@
         square_ref[8:, :] += mixed[8:] * mixed[8:]
 
         steps = lax.broadcasted_iota(jnp.int32, (MEDIUM_TAPS, LANES), 0).astype(F32)
-        taps_ref[:, lanes] = raw_ref[:, lanes] * jnp.exp(-decay_ref[0:1, lanes] * steps)
+        taps = raw_ref[:, lanes] * jnp.exp(-decay_ref[0:1, lanes] * steps)
+        held_ref[...] = taps
+        taps_ref[:, lanes] = taps
         u = [m_ref[n, :, lanes].astype(F32) for n in range(3)]
         for n in range(3):
             heads_ref[3 + n, :, lanes] = u[n][:8]
@@ -208,7 +211,7 @@
         total = [None] * tiles
         for r in range(8):
             shifted = roll(ext, r)
-            tap = [tap_tile(taps_ref, 8 * a + r, lanes) for a in range(MEDIUM_TAPS // 8)]
+            tap = [tap_tile(held_ref, 8 * a + r) for a in range(MEDIUM_TAPS // 8)]
             for i in range(tiles):
                 for a in range(min(i + 1, MEDIUM_TAPS // 8)):
                     at_tile = 8 * (i - a + 1)
@@ -235,6 +238,7 @@
         out_specs=(in_vmem(),) * 6,
         scratch_shapes=[
             pltpu.VMEM((MEDIUM_TAPS, channels), F32),
+            pltpu.VMEM((MEDIUM_TAPS, LANES), F32),
             pltpu.SemaphoreType.DMA((channels // (per * LANES),)),
         ],
         compiler_params=params(),
@@ -257,6 +261,7 @@
     mr_ref,
     square_ref,
     last_ref,
+    held_ref,
 ):
     rows, channels = own_ref.shape
     tiles = rows // 8
@@ -289,6 +294,7 @@
         square_ref[0, :8, :] += mixed * mixed
 
         taps = taps_ref[:, lanes]
+        held_ref[...] = taps
         front2 = jnp.where(row_is(8, 7), last, roll(before[:8], 6))
         fronts = (roll(x2, 2), x2, front2)
         z = [
@@ -303,7 +309,7 @@
         count = MEDIUM_TAPS // 8
         for r in range(8):
             shifted = roll(ext, r)
-            tap = [tap_tile(taps_ref, 8 * a + r, lanes) for a in range(count)]
+            tap = [tap_tile(held_ref, 8 * a + r) for a in range(count)]
             for i in range(count):
                 for a in range(i if r else i + 1, count):
                     at_tile = 8 * (i - a + count)
@@ -325,18 +331,18 @@
         ),
         in_specs=[in_vmem()] * 9,
         out_specs=(in_vmem(),) * 3,
-        scratch_shapes=[pltpu.VMEM((16, LANES), F32)],
+        scratch_shapes=[pltpu.VMEM((16, LANES), F32), pltpu.VMEM((MEDIUM_TAPS, LANES), F32)],
         compiler_params=params(),
         cost_estimate=cost(140 * rows * channels, 16 * rows * channels),
         name="mix",
     )(packet, own, z0, se_square, taps, heads, mr_short, se_short, se_filter)
 
 
-def score_kernel(per, there_ref, q_ref, k_ref, before_ref, v_ref, probs_ref, out_ref, inverse_ref, bias_ref):
+def score_kernel(per, q_ref, k_ref, before_ref, v_ref, probs_ref, out_ref, inverse_ref, bias_ref):
     rows, channels = q_ref.shape
     at = lax.broadcasted_iota(jnp.int32, (rows, 2 * rows), 0)
     key = lax.broadcasted_iota(jnp.int32, (rows, 2 * rows), 1)
-    valid = (key <= at + rows) & (key >= there_ref[0])
+    valid = (key <= at + rows) & ((key >= rows) | (lax.axis_index("ctx") > 0))
     bias_ref[...] = jnp.where(valid, 0.0, -1e30)
     factor = math.log2(math.e) / math.sqrt(HD)
     zeros, ones = jnp.zeros((rows, LANES), BF16), jnp.ones((rows, LANES), BF16)
@@ -367,13 +373,13 @@
             out_ref[:, lanes] = total[:, :LANES] * inverse
 
 
-def score(there, queries, keys, before, values, per):
+def score(queries, keys, before, values, per):
     rows, channels = queries.shape
     flat = jax.ShapeDtypeStruct((rows, channels), F32)
     return pl.pallas_call(
         functools.partial(score_kernel, per),
         out_shape=(jax.ShapeDtypeStruct((channels // HD, rows, rows), BF16), flat, flat),
-        in_specs=[pl.BlockSpec(memory_space=pltpu.SMEM)] + [in_vmem()] * 4,
+        in_specs=[in_vmem()] * 4,
         out_specs=(in_vmem(),) * 3,
         scratch_shapes=[pltpu.VMEM((rows, 2 * rows), F32)],
         compiler_params=params(),
@@ -381,7 +387,7 @@
             8 * rows * rows * channels, 14 * rows * channels, 4 * rows * rows * channels // HD
         ),
         name="score",
-    )(there, queries, keys, before, values)
+    )(queries, keys, before, values)
 
 
 def value_kernel(probs_ref, before_ref, own_ref, inverse_ref, out_ref, square_ref):
@@ -477,7 +483,6 @@
 
 
 def body(se, se_short, se_filter, mr, mr_short, raw, decay, queries, keys, values):
-    rows = queries.shape[0]
     decay = decay[None, :]
     key_before = from_behind(keys)
     packet = from_behind(pack(se, mr, se_short, mr_short, 4))
@@ -486,8 +491,7 @@
     )
     values_later, own = lax.optimization_barrier((values, own))
     value_before = from_behind(values_later)
-    there = jnp.where(lax.axis_index("ctx") == 0, rows, 0).astype(jnp.int32)[None]
-    probs, attended, inverse = score(there, queries, keys, key_before, values, 4)
+    probs, attended, inverse = score(queries, keys, key_before, values, 4)
     packet, attended = lax.optimization_barrier((packet, attended))
     head, mr_mix, square = mix(
         packet, own, z0, se_square, taps, heads, mr_short, se_short, se_filter

time: 54.7 us -> 48.6 us (0.89)
  the two profiles are of different devices: /device:TPU:0 before, /device:TPU:9 now
where the time goes in v4:
time: 48.6 us; the launch traced here: 48.4 us
  Pallas kernels  26.7 us (55%)
  starting transfers between devices  14 us (29%)
  waiting for transfers between devices  6.75 us (14%)
  between operations  0.86 us (2%)
    pallas_call x1, Pallas kernels, own_part(): pl.pallas_call(functools.partial(own_kernel, per), out_shape=(mixed, mixe...  12.2 us
    ppermute x3, starting transfers between devices, from_behind(): lax.ppermute(value, 'ctx', [(source, source + 1) for source in range(coun...  9.62 us
    pallas_call x1, Pallas kernels, mix(): pl.pallas_call(mix_kernel, out_shape=(jax.ShapeDtypeStruct((8, channels),...  6.86 us
    ppermute x3, waiting for transfers between devices, from_behind(): lax.ppermute(value, 'ctx', [(source, source + 1) for source in range(coun...  4.83 us
    ppermute x2, starting transfers between devices, of_panels(): lax.ppermute(square, 'panel', [(n, (n + shift) % count) for n in range(co...  4.38 us
    pallas_call x1, Pallas kernels, score(): pl.pallas_call(functools.partial(score_kernel, per), out_shape=(jax.Shape...  2.84 us
    pallas_call x1, Pallas kernels, pack(): pl.pallas_call(functools.partial(pack_kernel, per), out_shape=jax.ShapeDt...  2.22 us
    pallas_call x2, Pallas kernels, normalize(): pl.pallas_call(functools.partial(normalize_kernel, count, len(squares), p...  2.19 us
  transfers between devices with their start and end apart: 5, of which 4 were waited for; matrix products, arithmetic and copies ran while one was open for 0% of the time, Pallas kernels for 52%

profile of v4, /device:TPU:9, one launch (start us, length us, event | category | flops | bytes accessed | tf_op | source)
XLA Modules:
  0.0 48.4 jit_solution(10049852909715942639)
XLA Ops:
  0.6 0.0 copy-start.2
  0.6 0.0 copy-start.3
  0.7 0.0 copy-start
  0.7 0.0 copy-start.1
  0.7 0.0 copy-start.4
  0.7 0.0 copy-start.5
  0.7 3.4 %collective-permute-start.2 = (bf16[144,2048]{1,0:T(8,128)(2,1)}, bf16[144,2048]{1,0:T(8,128)(2,1)S(1)}, u32[]{:S(2)}, u32[]{:S(2)}) collective-permute-start(bf16[144,2048]{1,0:T(8,128)(2,1)} %k_ref.1), channel_id=1, source_target_pairs={{0,2},{2,4},{4,6},{6,8},{8,10},{10,12},{12,14},{14,16},{16,18},{18... | collective-permute-start | bytes 1769480 | tf_op jit(solution)/shard_map/ppermute | solution.py:474
  4.1 2.2 %pack.1 = bf16[2320,128]{1,0:T(8,128)(2,1)S(1)} custom-call(bf16[3,144,2048]{2,1,0:T(8,128)(2,1)} %mr_ref.1, bf16[3,144,2048]{2,1,0:T(8,128)(2,1)} %se_ref.1, f32[3,3,2048]{2,1,0:T(4,128)} %mw_ref.3, f32[3,3,2048]{2,1,0:T(4,128)} %sw_ref.3), custom_call_target="tpu_custom_call" | custom-call | flops 5898240 | bytes 1769472 | tf_op jit(solution)/shard_map/pack/pallas_call | solution.py:128
  6.3 3.1 %collective-permute-start.1 = (bf16[2320,128]{1,0:T(8,128)(2,1)S(1)}, bf16[2320,128]{1,0:T(8,128)(2,1)S(1)}, u32[]{:S(2)}, u32[]{:S(2)}) collective-permute-start(bf16[2320,128]{1,0:T(8,128)(2,1)S(1)} %pack.1), channel_id=1, source_target_pairs={{0,2},{2,4},{4,6},{6,8},{8,10},{10,12},{12,14},{14,16},{16,18},{18... | collective-permute-start | bytes 1781768 | tf_op jit(solution)/shard_map/ppermute | solution.py:474
  9.4 0.0 copy-done.2
  9.4 0.0 copy-done.3
  9.5 0.0 copy-done
  9.5 0.0 copy-done.1
  9.5 0.0 copy-done.4
  9.5 0.0 copy-done.5
  9.5 0.0 copy-start.8
  9.5 0.0 copy-start.6
  9.5 0.0 copy-start.7
  9.5 12.2 %own_part.1 = (f32[144,2048]{1,0:T(8,128)S(1)}, f32[144,2048]{1,0:T(8,128)S(1)}, f32[144,2048]{1,0:T(8,128)S(1)}, f32[144,128]{1,0:T(8,128)S(1)}, f32[128,2048]{1,0:T(8,128)S(1)}, /*index=5*/f32[6,8,2048]{2,1,0:T(8,128)S(1)}) custom-call(bf16[3,144,2048]{2,1,0:T(8,128)(2,1)S(1)} %copy-done, bf16[3,144,2048]{2,1,0:T(8,128)(2,1)S(1)} %copy-done.1, ...), custom_call_target="tpu_custom_call" | custom-call | flops 53084160 | bytes 7077888 | tf_op jit(solution)/shard_map/own_part/pallas_call | solution.py:227
  21.7 3.1 %collective-permute-start = (bf16[144,2048]{1,0:T(8,128)(2,1)S(1)}, bf16[144,2048]{1,0:T(8,128)(2,1)S(1)}, u32[]{:S(2)}, u32[]{:S(2)}) collective-permute-start(bf16[144,2048]{1,0:T(8,128)(2,1)S(1)} %copy-done.8), channel_id=1, source_target_pairs={{0,2},{2,4},{4,6},{6,8},{8,10},{10,12},{12,14},{14,16},{16,18},{18... | collective-permute-start | bytes 1769480 | tf_op jit(solution)/shard_map/ppermute | solution.py:474
  24.9 0.0 collective-permute-done.2.before_ref
  24.9 2.8 %score.1 = (bf16[16,144,144]{2,1,0:T(8,128)(2,1)S(1)}, f32[144,2048]{1,0:T(8,128)S(1)}, f32[144,2048]{1,0:T(8,128)S(1)}) custom-call(bf16[144,2048]{1,0:T(8,128)(2,1)S(1)} %copy-done.6, bf16[144,2048]{1,0:T(8,128)(2,1)S(1)} %copy-done.7, bf16[144,2048]{1,0:T(8,128)(2,1)S(1)} %collective-permute-done.2.before_ref, bf16[144,2048]{1,0:T(8,128)(2,1)S(1)} %copy-done.8), custom_call_target="tpu_custom_call" | custom-call | flops 339738624 | bytes 4128768 | tf_op jit(solution)/shard_map/score/pallas_call | solution.py:379
  27.7 4.0 %collective-permute-done.1.packet_ref = bf16[2320,128]{1,0:T(8,128)(2,1)S(1)} collective-permute-done((bf16[2320,128]{1,0:T(8,128)(2,1)S(1)}, bf16[2320,128]{1,0:T(8,128)(2,1)S(1)}, u32[]{:S(2)}, u32[]{:S(2)}) %collective-permute-start.1) | collective-permute-done | bytes 593952 | tf_op jit(solution)/shard_map/ppermute | solution.py:474
  31.8 6.9 %mix.1 = (f32[8,2048]{1,0:T(8,128)S(1)}, f32[144,2048]{1,0:T(8,128)S(1)}, f32[2,144,128]{2,1,0:T(8,128)S(1)}) custom-call(bf16[2320,128]{1,0:T(8,128)(2,1)S(1)} %collective-permute-done.1.packet_ref, f32[144,2048]{1,0:T(8,128)S(1)} %get-tuple-element.30.own_ref, f32[144,2048]{1,0:T(8,128)S(1)} %get-tuple-element.31.z0_ref, ...), custom_call_target="tpu_custom_call" | custom-call | flops 41287680 | bytes 4718592 | tf_op jit(solution)/shard_map/mix/pallas_call | solution.py:325
  38.7 2.8 %collective-permute-start.3 = (f32[2,144,128]{2,1,0:T(8,128)S(1)}, f32[2,144,128]{2,1,0:T(8,128)S(1)}, u32[]{:S(2)}, u32[]{:S(2)}) collective-permute-start(f32[2,144,128]{2,1,0:T(8,128)S(1)} %get-tuple-element.35.refs_0_), channel_id=1, source_target_pairs={{0,1},{1,0},{2,3},{3,2},{4,5},{5,4},{6,7},{7,6},{8,9},{9,8},{10,11... | collective-permute-start | bytes 442376 | tf_op jit(solution)/shard_map/ppermute | solution.py:480
  41.4 1.0 %collective-permute-done.3.refs_1_ = f32[2,144,128]{2,1,0:T(8,128)S(1)} collective-permute-done((f32[2,144,128]{2,1,0:T(8,128)S(1)}, f32[2,144,128]{2,1,0:T(8,128)S(1)}, u32[]{:S(2)}, u32[]{:S(2)}) %collective-permute-start.3) | collective-permute-done | bytes 147488 | tf_op jit(solution)/shard_map/ppermute | solution.py:480
  42.4 1.2 %normalize.2 = (bf16[144,2048]{1,0:T(8,128)(2,1)}, bf16[144,2048]{1,0:T(8,128)(2,1)}) custom-call(f32[2,144,128]{2,1,0:T(8,128)S(1)} %get-tuple-element.35.refs_0_, f32[2,144,128]{2,1,0:T(8,128)S(1)} %collective-permute-done.3.refs_1_, f32[144,2048]{1,0:T(8,128)S(1)} %get-tuple-element.36.refs_2_, f32[144,2048]{1,0:T(8,128)S(1)} %get-tuple-element.37.refs_3_, ...), custom_call_target="tpu_custom_call" | custom-call | flops 2359296 | bytes 3538944 | tf_op jit(solution)/shard_map/normalize/pallas_call | solution.py:457
  43.6 0.8 %collective-permute-done.before_ref = bf16[144,2048]{1,0:T(8,128)(2,1)S(1)} collective-permute-done((bf16[144,2048]{1,0:T(8,128)(2,1)S(1)}, bf16[144,2048]{1,0:T(8,128)(2,1)S(1)}, u32[]{:S(2)}, u32[]{:S(2)}) %collective-permute-start) | collective-permute-done | bytes 589856 | tf_op jit(solution)/shard_map/ppermute | solution.py:474
  44.4 0.5 value_mix.1
  44.9 1.6 %collective-permute-start.4 = (f32[1,144,128]{2,1,0:T(8,128)S(1)}, f32[1,144,128]{2,1,0:T(8,128)S(1)}, u32[]{:S(2)}, u32[]{:S(2)}) collective-permute-start(f32[1,144,128]{2,1,0:T(8,128)S(1)} %get-tuple-element.47.refs_0_), channel_id=1, source_target_pairs={{0,1},{1,0},{2,3},{3,2},{4,5},{5,4},{6,7},{7,6},{8,9},{9,8},{10,11... | collective-permute-start | bytes 221192 | tf_op jit(solution)/shard_map/ppermute | solution.py:480
  46.5 0.9 %collective-permute-done.4.refs_1_ = f32[1,144,128]{2,1,0:T(8,128)S(1)} collective-permute-done((f32[1,144,128]{2,1,0:T(8,128)S(1)}, f32[1,144,128]{2,1,0:T(8,128)S(1)}, u32[]{:S(2)}, u32[]{:S(2)}) %collective-permute-start.4) | collective-permute-done | bytes 73760 | tf_op jit(solution)/shard_map/ppermute | solution.py:480
  47.4 1.0 %normalize.3 = bf16[144,2048]{1,0:T(8,128)(2,1)} custom-call(f32[1,144,128]{2,1,0:T(8,128)S(1)} %get-tuple-element.47.refs_0_, f32[1,144,128]{2,1,0:T(8,128)S(1)} %collective-permute-done.4.refs_1_, f32[144,2048]{1,0:T(8,128)S(1)} %get-tuple-element.48.refs_2_), custom_call_target="tpu_custom_call" | custom-call | flops 1179648 | bytes 1769472 | tf_op jit(solution)/shard_map/normalize/pallas_call | solution.py:457
  (3 shorter events, 0.0 us)
Async XLA Ops:
  0.6 8.8 %copy-start.2 = (f32[3,3,2048]{2,1,0:T(4,128)S(1)}, f32[3,3,2048]{2,1,0:T(4,128)}, u32[]{:S(2)}) copy-start(f32[3,3,2048]{2,1,0:T(4,128)} %mw_ref.3) | copy-start | bytes 221188
  0.6 8.8 %copy-start.3 = (f32[3,3,2048]{2,1,0:T(4,128)S(1)}, f32[3,3,2048]{2,1,0:T(4,128)}, u32[]{:S(2)}) copy-start(f32[3,3,2048]{2,1,0:T(4,128)} %sw_ref.3) | copy-start | bytes 221188
  0.7 8.8 %copy-start = (bf16[3,144,2048]{2,1,0:T(8,128)(2,1)S(1)}, bf16[3,144,2048]{2,1,0:T(8,128)(2,1)}, u32[]{:S(2)}) copy-start(bf16[3,144,2048]{2,1,0:T(8,128)(2,1)} %mr_ref.1) | copy-start | bytes 5308420
  0.7 8.8 %copy-start.1 = (bf16[3,144,2048]{2,1,0:T(8,128)(2,1)S(1)}, bf16[3,144,2048]{2,1,0:T(8,128)(2,1)}, u32[]{:S(2)}) copy-start(bf16[3,144,2048]{2,1,0:T(8,128)(2,1)} %se_ref.1) | copy-start | bytes 5308420
  0.7 8.8 %copy-start.4 = (f32[7,2048]{1,0:T(8,128)S(1)}, f32[7,2048]{1,0:T(8,128)}, u32[]{:S(2)}) copy-start(f32[7,2048]{1,0:T(8,128)} %filter_ref.3) | copy-start | bytes 172036
  0.7 8.8 %copy-start.5 = (f32[2048]{0:T(1024)S(1)}, f32[2048]{0:T(1024)}, u32[]{:S(2)}) copy-start(f32[2048]{0:T(1024)} %param.16) | copy-start | bytes 24580
  0.7 24.2 %collective-permute-start.2 = (bf16[144,2048]{1,0:T(8,128)(2,1)}, bf16[144,2048]{1,0:T(8,128)(2,1)S(1)}, u32[]{:S(2)}, u32[]{:S(2)}) collective-permute-start(bf16[144,2048]{1,0:T(8,128)(2,1)} %k_ref.1), channel_id=1, source_target_pairs={{0,2},{2,4},{4,6},{6,8},{8,10},{10,12},{12,14},{14,16},{16,18},{18... | collective-permute-start | bytes 1769480 | tf_op jit(solution)/shard_map/ppermute | solution.py:474
  6.3 25.5 %collective-permute-start.1 = (bf16[2320,128]{1,0:T(8,128)(2,1)S(1)}, bf16[2320,128]{1,0:T(8,128)(2,1)S(1)}, u32[]{:S(2)}, u32[]{:S(2)}) collective-permute-start(bf16[2320,128]{1,0:T(8,128)(2,1)S(1)} %pack.1), channel_id=1, source_target_pairs={{0,2},{2,4},{4,6},{6,8},{8,10},{10,12},{12,14},{14,16},{16,18},{18... | collective-permute-start | bytes 1781768 | tf_op jit(solution)/shard_map/ppermute | solution.py:474
  9.5 12.2 %copy-start.8 = (bf16[144,2048]{1,0:T(8,128)(2,1)S(1)}, bf16[144,2048]{1,0:T(8,128)(2,1)}, u32[]{:S(2)}) copy-start(bf16[144,2048]{1,0:T(8,128)(2,1)} %v_ref.1) | copy-start | bytes 1769476
  9.5 15.4 %copy-start.6 = (bf16[144,2048]{1,0:T(8,128)(2,1)S(1)}, bf16[144,2048]{1,0:T(8,128)(2,1)}, u32[]{:S(2)}) copy-start(bf16[144,2048]{1,0:T(8,128)(2,1)} %q_ref.1) | copy-start | bytes 1769476
  9.5 15.4 %copy-start.7 = (bf16[144,2048]{1,0:T(8,128)(2,1)S(1)}, bf16[144,2048]{1,0:T(8,128)(2,1)}, u32[]{:S(2)}) copy-start(bf16[144,2048]{1,0:T(8,128)(2,1)} %k_ref.1) | copy-start | bytes 1769476
  21.7 22.7 %collective-permute-start = (bf16[144,2048]{1,0:T(8,128)(2,1)S(1)}, bf16[144,2048]{1,0:T(8,128)(2,1)S(1)}, u32[]{:S(2)}, u32[]{:S(2)}) collective-permute-start(bf16[144,2048]{1,0:T(8,128)(2,1)S(1)} %copy-done.8), channel_id=1, source_target_pairs={{0,2},{2,4},{4,6},{6,8},{8,10},{10,12},{12,14},{14,16},{16,18},{18... | collective-permute-start | bytes 1769480 | tf_op jit(solution)/shard_map/ppermute | solution.py:474
  38.7 3.8 %collective-permute-start.3 = (f32[2,144,128]{2,1,0:T(8,128)S(1)}, f32[2,144,128]{2,1,0:T(8,128)S(1)}, u32[]{:S(2)}, u32[]{:S(2)}) collective-permute-start(f32[2,144,128]{2,1,0:T(8,128)S(1)} %get-tuple-element.35.refs_0_), channel_id=1, source_target_pairs={{0,1},{1,0},{2,3},{3,2},{4,5},{5,4},{6,7},{7,6},{8,9},{9,8},{10,11... | collective-permute-start | bytes 442376 | tf_op jit(solution)/shard_map/ppermute | solution.py:480
  44.9 2.5 %collective-permute-start.4 = (f32[1,144,128]{2,1,0:T(8,128)S(1)}, f32[1,144,128]{2,1,0:T(8,128)S(1)}, u32[]{:S(2)}, u32[]{:S(2)}) collective-permute-start(f32[1,144,128]{2,1,0:T(8,128)S(1)} %get-tuple-element.47.refs_0_), channel_id=1, source_target_pairs={{0,1},{1,0},{2,3},{3,2},{4,5},{5,4},{6,7},{7,6},{8,9},{9,8},{10,11... | collective-permute-start | bytes 221192 | tf_op jit(solution)/shard_map/ppermute | solution.py:480

commit v5 on v4

--- a/solution.py
+++ b/solution.py
@@ -429,16 +429,16 @@
     piece = rows // pieces
     copies = []
     for n in range(count):
-        square = square_refs[0][n]
-        for ref in square_refs[1:]:
-            square = square + ref[n]
-        scale = lax.rsqrt(jnp.sum(square, axis=-1, keepdims=True) * (1.0 / CHANNELS) + 1e-06)
         for m in range(pieces):
             at = slice(m * piece, (m + 1) * piece)
+            square = square_refs[0][n, at, :]
+            for ref in square_refs[1:]:
+                square = square + ref[n, at, :]
+            scale = lax.rsqrt(jnp.sum(square, axis=-1, keepdims=True) * (1.0 / CHANNELS) + 1e-06)
             value = mixed_refs[n][at, :]
             if with_head and n == 0 and m == 0:
                 value = jnp.concatenate([head_ref[...], value[8:]], axis=0)
-            held_ref[n, at, :] = (value * scale[at]).astype(BF16)
+            held_ref[n, at, :] = (value * scale).astype(BF16)
             copy = pltpu.make_async_copy(
                 held_ref.at[n, pl.ds(m * piece, piece)],
                 out_refs[n].at[pl.ds(m * piece, piece)],
@@ -450,7 +450,7 @@
         copy.wait()
 
 
-def normalize(squares, mixed, head=None, pieces=3):
+def normalize(squares, mixed, head=None, pieces=9):
     rows, channels = mixed[0].shape
     count = len(mixed)
     operands = (*squares, *mixed) + (() if head is None else (head,))
@@ -489,8 +489,7 @@
     own, z0, se_mix, se_square, taps, heads = own_part(
         mr, se, mr_short, se_short, raw, decay, se_filter, 4
     )
-    values_later, own = lax.optimization_barrier((values, own))
-    value_before = from_behind(values_later)
+    value_before = from_behind(values)
     probs, attended, inverse = score(queries, keys, key_before, values, 4)
     packet, attended = lax.optimization_barrier((packet, attended))
     head, mr_mix, square = mix(

time: 48.6 us -> 48.6 us (level)
  no operation moved by 1% of the time
where the time goes in v5:
time: 48.6 us; the launch traced here: 48.4 us
  Pallas kernels  26.8 us (55%)
  starting transfers between devices  14 us (29%)
  waiting for transfers between devices  6.7 us (14%)
  between operations  0.85 us (2%)
    pallas_call x1, Pallas kernels, own_part(): pl.pallas_call(functools.partial(own_kernel, per), out_shape=(mixed, mixe...  12.2 us
    ppermute x3, starting transfers between devices, from_behind(): lax.ppermute(value, 'ctx', [(source, source + 1) for source in range(coun...  9.63 us
    pallas_call x1, Pallas kernels, mix(): pl.pallas_call(mix_kernel, out_shape=(jax.ShapeDtypeStruct((8, channels),...  6.86 us
    ppermute x3, waiting for transfers between devices, from_behind(): lax.ppermute(value, 'ctx', [(source, source + 1) for source in range(coun...  4.78 us
    ppermute x2, starting transfers between devices, of_panels(): lax.ppermute(square, 'panel', [(n, (n + shift) % count) for n in range(co...  4.37 us
    pallas_call x1, Pallas kernels, score(): pl.pallas_call(functools.partial(score_kernel, per), out_shape=(jax.Shape...  2.84 us
    pallas_call x2, Pallas kernels, normalize(): pl.pallas_call(functools.partial(normalize_kernel, count, len(squares), p...  2.26 us
    pallas_call x1, Pallas kernels, pack(): pl.pallas_call(functools.partial(pack_kernel, per), out_shape=jax.ShapeDt...  2.22 us
  transfers between devices with their start and end apart: 5, of which 4 were waited for; matrix products, arithmetic and copies ran while one was open for 0% of the time, Pallas kernels for 52%

profile of v5, /device:TPU:9, one launch (start us, length us, event | category | flops | bytes accessed | tf_op | source)
XLA Modules:
  0.0 48.4 jit_solution(15072171171251863275)
XLA Ops:
  0.6 0.0 copy-start.1
  0.6 0.0 copy-start.3
  0.7 0.0 copy-start
  0.7 0.0 copy-start.2
  0.7 0.0 copy-start.5
  0.7 0.0 copy-start.4
  0.7 3.4 %collective-permute-start.2 = (bf16[144,2048]{1,0:T(8,128)(2,1)}, bf16[144,2048]{1,0:T(8,128)(2,1)S(1)}, u32[]{:S(2)}, u32[]{:S(2)}) collective-permute-start(bf16[144,2048]{1,0:T(8,128)(2,1)} %k_ref.1), channel_id=1, source_target_pairs={{0,2},{2,4},{4,6},{6,8},{8,10},{10,12},{12,14},{14,16},{16,18},{18... | collective-permute-start | bytes 1769480 | tf_op jit(solution)/shard_map/ppermute | solution.py:474
  4.1 2.2 %pack.1 = bf16[2320,128]{1,0:T(8,128)(2,1)S(1)} custom-call(bf16[3,144,2048]{2,1,0:T(8,128)(2,1)} %m_ref.1, bf16[3,144,2048]{2,1,0:T(8,128)(2,1)} %s_ref.1, f32[3,3,2048]{2,1,0:T(4,128)} %mw_ref.3, f32[3,3,2048]{2,1,0:T(4,128)} %sw_ref.3), custom_call_target="tpu_custom_call" | custom-call | flops 5898240 | bytes 1769472 | tf_op jit(solution)/shard_map/pack/pallas_call | solution.py:128
  6.3 3.1 %collective-permute-start.1 = (bf16[2320,128]{1,0:T(8,128)(2,1)S(1)}, bf16[2320,128]{1,0:T(8,128)(2,1)S(1)}, u32[]{:S(2)}, u32[]{:S(2)}) collective-permute-start(bf16[2320,128]{1,0:T(8,128)(2,1)S(1)} %pack.1), channel_id=1, source_target_pairs={{0,2},{2,4},{4,6},{6,8},{8,10},{10,12},{12,14},{14,16},{16,18},{18... | collective-permute-start | bytes 1781768 | tf_op jit(solution)/shard_map/ppermute | solution.py:474
  9.4 3.1 %collective-permute-start = (bf16[144,2048]{1,0:T(8,128)(2,1)}, bf16[144,2048]{1,0:T(8,128)(2,1)S(1)}, u32[]{:S(2)}, u32[]{:S(2)}) collective-permute-start(bf16[144,2048]{1,0:T(8,128)(2,1)} %v_ref.1), channel_id=1, source_target_pairs={{0,2},{2,4},{4,6},{6,8},{8,10},{10,12},{12,14},{14,16},{16,18},{18... | collective-permute-start | bytes 1769480 | tf_op jit(solution)/shard_map/ppermute | solution.py:474
  12.6 0.0 copy-done.1
  12.6 0.0 copy-done.3
  12.6 0.0 copy-done
  12.6 0.0 copy-start.6
  12.6 0.0 copy-start.7
  12.6 0.0 copy-start.8
  12.7 12.2 %own_part.1 = (f32[144,2048]{1,0:T(8,128)S(1)}, f32[144,2048]{1,0:T(8,128)S(1)}, f32[144,2048]{1,0:T(8,128)S(1)}, f32[144,128]{1,0:T(8,128)S(1)}, f32[128,2048]{1,0:T(8,128)S(1)}, /*index=5*/f32[6,8,2048]{2,1,0:T(8,128)S(1)}) custom-call(bf16[3,144,2048]{2,1,0:T(8,128)(2,1)S(1)} %copy-done, bf16[3,144,2048]{2,1,0:T(8,128)(2,1)S(1)} %copy-done.1, ...), custom_call_target="tpu_custom_call" | custom-call | flops 53084160 | bytes 7077888 | tf_op jit(solution)/shard_map/own_part/pallas_call | solution.py:227
  24.9 0.0 collective-permute-done.2.before_ref
  24.9 0.0 copy-done.6
  24.9 0.0 copy-done.7
  24.9 0.0 copy-done.8
  24.9 2.8 %score.1 = (bf16[16,144,144]{2,1,0:T(8,128)(2,1)S(1)}, f32[144,2048]{1,0:T(8,128)S(1)}, f32[144,2048]{1,0:T(8,128)S(1)}) custom-call(bf16[144,2048]{1,0:T(8,128)(2,1)S(1)} %copy-done.6, bf16[144,2048]{1,0:T(8,128)(2,1)S(1)} %copy-done.7, bf16[144,2048]{1,0:T(8,128)(2,1)S(1)} %collective-permute-done.2.before_ref, bf16[144,2048]{1,0:T(8,128)(2,1)S(1)} %copy-done.8), custom_call_target="tpu_custom_call" | custom-call | flops 339738624 | bytes 4128768 | tf_op jit(solution)/shard_map/score/pallas_call | solution.py:379
  27.7 4.0 %collective-permute-done.1.packet_ref = bf16[2320,128]{1,0:T(8,128)(2,1)S(1)} collective-permute-done((bf16[2320,128]{1,0:T(8,128)(2,1)S(1)}, bf16[2320,128]{1,0:T(8,128)(2,1)S(1)}, u32[]{:S(2)}, u32[]{:S(2)}) %collective-permute-start.1) | collective-permute-done | bytes 593952 | tf_op jit(solution)/shard_map/ppermute | solution.py:474
  31.8 6.9 %mix.1 = (f32[8,2048]{1,0:T(8,128)S(1)}, f32[144,2048]{1,0:T(8,128)S(1)}, f32[2,144,128]{2,1,0:T(8,128)S(1)}) custom-call(bf16[2320,128]{1,0:T(8,128)(2,1)S(1)} %collective-permute-done.1.packet_ref, f32[144,2048]{1,0:T(8,128)S(1)} %get-tuple-element.26.own_ref, f32[144,2048]{1,0:T(8,128)S(1)} %get-tuple-element.27.z0_ref, ...), custom_call_target="tpu_custom_call" | custom-call | flops 41287680 | bytes 4718592 | tf_op jit(solution)/shard_map/mix/pallas_call | solution.py:325
  38.7 2.8 %collective-permute-start.3 = (f32[2,144,128]{2,1,0:T(8,128)S(1)}, f32[2,144,128]{2,1,0:T(8,128)S(1)}, u32[]{:S(2)}, u32[]{:S(2)}) collective-permute-start(f32[2,144,128]{2,1,0:T(8,128)S(1)} %get-tuple-element.31.refs_0_), channel_id=1, source_target_pairs={{0,1},{1,0},{2,3},{3,2},{4,5},{5,4},{6,7},{7,6},{8,9},{9,8},{10,11... | collective-permute-start | bytes 442376 | tf_op jit(solution)/shard_map/ppermute | solution.py:480
  41.4 1.0 %collective-permute-done.3.refs_1_ = f32[2,144,128]{2,1,0:T(8,128)S(1)} collective-permute-done((f32[2,144,128]{2,1,0:T(8,128)S(1)}, f32[2,144,128]{2,1,0:T(8,128)S(1)}, u32[]{:S(2)}, u32[]{:S(2)}) %collective-permute-start.3) | collective-permute-done | bytes 147488 | tf_op jit(solution)/shard_map/ppermute | solution.py:480
  42.4 1.3 %normalize.2 = (bf16[144,2048]{1,0:T(8,128)(2,1)}, bf16[144,2048]{1,0:T(8,128)(2,1)}) custom-call(f32[2,144,128]{2,1,0:T(8,128)S(1)} %get-tuple-element.31.refs_0_, f32[2,144,128]{2,1,0:T(8,128)S(1)} %collective-permute-done.3.refs_1_, f32[144,2048]{1,0:T(8,128)S(1)} %get-tuple-element.32.refs_2_, f32[144,2048]{1,0:T(8,128)S(1)} %get-tuple-element.33.refs_3_, ...), custom_call_target="tpu_custom_call" | custom-call | flops 2359296 | bytes 3538944 | tf_op jit(solution)/shard_map/normalize/pallas_call | solution.py:457
  43.7 0.7 %collective-permute-done.before_ref = bf16[144,2048]{1,0:T(8,128)(2,1)S(1)} collective-permute-done((bf16[144,2048]{1,0:T(8,128)(2,1)}, bf16[144,2048]{1,0:T(8,128)(2,1)S(1)}, u32[]{:S(2)}, u32[]{:S(2)}) %collective-permute-start) | collective-permute-done | bytes 589856 | tf_op jit(solution)/shard_map/ppermute | solution.py:474
  44.4 0.5 value_mix.1
  44.9 1.6 %collective-permute-start.4 = (f32[1,144,128]{2,1,0:T(8,128)S(1)}, f32[1,144,128]{2,1,0:T(8,128)S(1)}, u32[]{:S(2)}, u32[]{:S(2)}) collective-permute-start(f32[1,144,128]{2,1,0:T(8,128)S(1)} %get-tuple-element.43.refs_0_), channel_id=1, source_target_pairs={{0,1},{1,0},{2,3},{3,2},{4,5},{5,4},{6,7},{7,6},{8,9},{9,8},{10,11... | collective-permute-start | bytes 221192 | tf_op jit(solution)/shard_map/ppermute | solution.py:480
  46.5 0.9 %collective-permute-done.4.refs_1_ = f32[1,144,128]{2,1,0:T(8,128)S(1)} collective-permute-done((f32[1,144,128]{2,1,0:T(8,128)S(1)}, f32[1,144,128]{2,1,0:T(8,128)S(1)}, u32[]{:S(2)}, u32[]{:S(2)}) %collective-permute-start.4) | collective-permute-done | bytes 73760 | tf_op jit(solution)/shard_map/ppermute | solution.py:480
  47.4 1.0 %normalize.3 = bf16[144,2048]{1,0:T(8,128)(2,1)} custom-call(f32[1,144,128]{2,1,0:T(8,128)S(1)} %get-tuple-element.43.refs_0_, f32[1,144,128]{2,1,0:T(8,128)S(1)} %collective-permute-done.4.refs_1_, f32[144,2048]{1,0:T(8,128)S(1)} %get-tuple-element.44.refs_2_), custom_call_target="tpu_custom_call" | custom-call | flops 1179648 | bytes 1769472 | tf_op jit(solution)/shard_map/normalize/pallas_call | solution.py:457
  (3 shorter events, 0.0 us)
Async XLA Ops:
  0.6 11.9 %copy-start.1 = (bf16[3,144,2048]{2,1,0:T(8,128)(2,1)S(1)}, bf16[3,144,2048]{2,1,0:T(8,128)(2,1)}, u32[]{:S(2)}) copy-start(bf16[3,144,2048]{2,1,0:T(8,128)(2,1)} %s_ref.1) | copy-start | bytes 5308420
  0.6 11.9 %copy-start.3 = (f32[3,3,2048]{2,1,0:T(4,128)S(1)}, f32[3,3,2048]{2,1,0:T(4,128)}, u32[]{:S(2)}) copy-start(f32[3,3,2048]{2,1,0:T(4,128)} %sw_ref.3) | copy-start | bytes 221188
  0.7 11.9 %copy-start = (bf16[3,144,2048]{2,1,0:T(8,128)(2,1)S(1)}, bf16[3,144,2048]{2,1,0:T(8,128)(2,1)}, u32[]{:S(2)}) copy-start(bf16[3,144,2048]{2,1,0:T(8,128)(2,1)} %m_ref.1) | copy-start | bytes 5308420
  0.7 11.9 %copy-start.2 = (f32[3,3,2048]{2,1,0:T(4,128)S(1)}, f32[3,3,2048]{2,1,0:T(4,128)}, u32[]{:S(2)}) copy-start(f32[3,3,2048]{2,1,0:T(4,128)} %mw_ref.3) | copy-start | bytes 221188
  0.7 11.9 %copy-start.5 = (f32[2048]{0:T(1024)S(1)}, f32[2048]{0:T(1024)}, u32[]{:S(2)}) copy-start(f32[2048]{0:T(1024)} %param.16) | copy-start | bytes 24580
  0.7 11.9 %copy-start.4 = (f32[7,2048]{1,0:T(8,128)S(1)}, f32[7,2048]{1,0:T(8,128)}, u32[]{:S(2)}) copy-start(f32[7,2048]{1,0:T(8,128)} %filter_ref.3) | copy-start | bytes 172036
  0.7 24.2 %collective-permute-start.2 = (bf16[144,2048]{1,0:T(8,128)(2,1)}, bf16[144,2048]{1,0:T(8,128)(2,1)S(1)}, u32[]{:S(2)}, u32[]{:S(2)}) collective-permute-start(bf16[144,2048]{1,0:T(8,128)(2,1)} %k_ref.1), channel_id=1, source_target_pairs={{0,2},{2,4},{4,6},{6,8},{8,10},{10,12},{12,14},{14,16},{16,18},{18... | collective-permute-start | bytes 1769480 | tf_op jit(solution)/shard_map/ppermute | solution.py:474
  6.3 25.5 %collective-permute-start.1 = (bf16[2320,128]{1,0:T(8,128)(2,1)S(1)}, bf16[2320,128]{1,0:T(8,128)(2,1)S(1)}, u32[]{:S(2)}, u32[]{:S(2)}) collective-permute-start(bf16[2320,128]{1,0:T(8,128)(2,1)S(1)} %pack.1), channel_id=1, source_target_pairs={{0,2},{2,4},{4,6},{6,8},{8,10},{10,12},{12,14},{14,16},{16,18},{18... | collective-permute-start | bytes 1781768 | tf_op jit(solution)/shard_map/ppermute | solution.py:474
  9.4 35.0 %collective-permute-start = (bf16[144,2048]{1,0:T(8,128)(2,1)}, bf16[144,2048]{1,0:T(8,128)(2,1)S(1)}, u32[]{:S(2)}, u32[]{:S(2)}) collective-permute-start(bf16[144,2048]{1,0:T(8,128)(2,1)} %v_ref.1), channel_id=1, source_target_pairs={{0,2},{2,4},{4,6},{6,8},{8,10},{10,12},{12,14},{14,16},{16,18},{18... | collective-permute-start | bytes 1769480 | tf_op jit(solution)/shard_map/ppermute | solution.py:474
  12.6 12.2 %copy-start.6 = (bf16[144,2048]{1,0:T(8,128)(2,1)S(1)}, bf16[144,2048]{1,0:T(8,128)(2,1)}, u32[]{:S(2)}) copy-start(bf16[144,2048]{1,0:T(8,128)(2,1)} %q_ref.1) | copy-start | bytes 1769476
  12.6 12.2 %copy-start.7 = (bf16[144,2048]{1,0:T(8,128)(2,1)S(1)}, bf16[144,2048]{1,0:T(8,128)(2,1)}, u32[]{:S(2)}) copy-start(bf16[144,2048]{1,0:T(8,128)(2,1)} %k_ref.1) | copy-start | bytes 1769476
  12.6 12.2 %copy-start.8 = (bf16[144,2048]{1,0:T(8,128)(2,1)S(1)}, bf16[144,2048]{1,0:T(8,128)(2,1)}, u32[]{:S(2)}) copy-start(bf16[144,2048]{1,0:T(8,128)(2,1)} %v_ref.1) | copy-start | bytes 1769476
  38.7 3.8 %collective-permute-start.3 = (f32[2,144,128]{2,1,0:T(8,128)S(1)}, f32[2,144,128]{2,1,0:T(8,128)S(1)}, u32[]{:S(2)}, u32[]{:S(2)}) collective-permute-start(f32[2,144,128]{2,1,0:T(8,128)S(1)} %get-tuple-element.31.refs_0_), channel_id=1, source_target_pairs={{0,1},{1,0},{2,3},{3,2},{4,5},{5,4},{6,7},{7,6},{8,9},{9,8},{10,11... | collective-permute-start | bytes 442376 | tf_op jit(solution)/shard_map/ppermute | solution.py:480
  44.9 2.5 %collective-permute-start.4 = (f32[1,144,128]{2,1,0:T(8,128)S(1)}, f32[1,144,128]{2,1,0:T(8,128)S(1)}, u32[]{:S(2)}, u32[]{:S(2)}) collective-permute-start(f32[1,144,128]{2,1,0:T(8,128)S(1)} %get-tuple-element.43.refs_0_), channel_id=1, source_target_pairs={{0,1},{1,0},{2,3},{3,2},{4,5},{5,4},{6,7},{7,6},{8,9},{9,8},{10,11... | collective-permute-start | bytes 221192 | tf_op jit(solution)/shard_map/ppermute | solution.py:480

commit v6 on v5

--- a/solution.py
+++ b/solution.py
@@ -390,7 +390,7 @@
     )(queries, keys, before, values)
 
 
-def value_kernel(probs_ref, before_ref, own_ref, inverse_ref, out_ref, square_ref):
+def value_kernel(probs_ref, before_ref, own_ref, inverse_ref, others_ref, out_ref, square_ref):
     rows, channels = own_ref.shape
     square = jnp.zeros((rows, LANES), F32)
     for k in range(channels // LANES):
@@ -400,23 +400,24 @@
         )
         out_ref[:, lanes] = total
         square = square + total * total
-    square_ref[0] = square
-
-
-def value_mix(probs, before, own, inverse):
+    square_ref[:2] = others_ref[...]
+    square_ref[2] = square
+
+
+def value_mix(probs, before, own, inverse, square):
     rows, channels = own.shape
     return pl.pallas_call(
         value_kernel,
         out_shape=(
             jax.ShapeDtypeStruct((rows, channels), F32),
-            jax.ShapeDtypeStruct((1, rows, LANES), F32),
+            jax.ShapeDtypeStruct((3, rows, LANES), F32),
         ),
-        in_specs=[in_vmem()] * 4,
+        in_specs=[in_vmem()] * 5,
         out_specs=(in_vmem(),) * 2,
         compiler_params=params(),
         cost_estimate=cost(2 * rows * rows * channels, 12 * rows * channels),
         name="value_mix",
-    )(probs, before, own, inverse)
+    )(probs, before, own, inverse, square)
 
 
 def normalize_kernel(count, panels, pieces, with_head, *refs):
@@ -450,7 +451,7 @@
         copy.wait()
 
 
-def normalize(squares, mixed, head=None, pieces=9):
+def normalize(squares, mixed, head=None, pieces=3):
     rows, channels = mixed[0].shape
     count = len(mixed)
     operands = (*squares, *mixed) + (() if head is None else (head,))
@@ -495,11 +496,8 @@
     head, mr_mix, square = mix(
         packet, own, z0, se_square, taps, heads, mr_short, se_short, se_filter
     )
-    se_out, mr_out = normalize(of_panels(square), (se_mix, mr_mix), head)
-    value_before, se_out, mr_out = lax.optimization_barrier((value_before, se_out, mr_out))
-    attended, square = value_mix(probs, value_before, attended, inverse)
-    (attn_out,) = normalize(of_panels(square), (attended,))
-    return se_out, mr_out, attn_out
+    attended, square = value_mix(probs, value_before, attended, inverse, square)
+    return normalize(of_panels(square), (se_mix, mr_mix, attended), head)
 
 
 def solution(mesh):

time: 48.6 us -> 49.3 us (1.014)
  waiting for transfers between devices: 6.7 us -> 10.9 us
  starting transfers between devices: 14 us -> 11.2 us
  Pallas kernels: 26.8 us -> 26 us
    ppermute x3, waiting for transfers between devices: 4.78 us -> 9.81 us  [from_behind(): lax.ppermute(value, 'ctx', [(source, source + 1) for source in range(coun...]
    ppermute x2 -> x1, starting transfers between devices: 4.37 us -> 1.62 us  [of_panels(): lax.ppermute(square, 'panel', [(n, (n + shift) % count) for n in range(co...]
    pallas_call x2 -> x1, Pallas kernels: 2.26 us -> 1.44 us  [normalize(): pl.pallas_call(functools.partial(normalize_kernel, count, len(squares), p...]
    ppermute x2 -> x1, waiting for transfers between devices: 1.92 us -> 1.1 us  [of_panels(): lax.ppermute(square, 'panel', [(n, (n + shift) % count) for n in range(co...]
  transfers between devices with their start and end apart: 5 -> 4, of which waited for: 4 -> 3; matrix products, arithmetic and copies ran while one was open for 0% -> 0% of each run, Pallas kernels for 52% -> 49%
where the time goes in v6:
time: 49.3 us; the launch traced here: 49 us
  Pallas kernels  26 us (53%)
  starting transfers between devices  11.2 us (23%)
  waiting for transfers between devices  10.9 us (22%)
  between operations  0.85 us (2%)
    pallas_call x1, Pallas kernels, own_part(): pl.pallas_call(functools.partial(own_kernel, per), out_shape=(mixed, mixe...  12.2 us
    ppermute x3, waiting for transfers between devices, from_behind(): lax.ppermute(value, 'ctx', [(source, source + 1) for source in range(coun...  9.81 us
    ppermute x3, starting transfers between devices, from_behind(): lax.ppermute(value, 'ctx', [(source, source + 1) for source in range(coun...  9.63 us
    pallas_call x1, Pallas kernels, mix(): pl.pallas_call(mix_kernel, out_shape=(jax.ShapeDtypeStruct((8, channels),...  6.87 us
    pallas_call x1, Pallas kernels, score(): pl.pallas_call(functools.partial(score_kernel, per), out_shape=(jax.Shape...  2.83 us
    pallas_call x1, Pallas kernels, pack(): pl.pallas_call(functools.partial(pack_kernel, per), out_shape=jax.ShapeDt...  2.22 us
    ppermute x1, starting transfers between devices, of_panels(): lax.ppermute(square, 'panel', [(n, (n + shift) % count) for n in range(co...  1.62 us
    pallas_call x1, Pallas kernels, normalize(): pl.pallas_call(functools.partial(normalize_kernel, count, len(squares), p...  1.44 us
  transfers between devices with their start and end apart: 4, of which 3 were waited for; matrix products, arithmetic and copies ran while one was open for 0% of the time, Pallas kernels for 49%

profile of v6, /device:TPU:9, one launch (start us, length us, event | category | flops | bytes accessed | tf_op | source)
XLA Modules:
  0.0 49.0 jit_solution(9902470449040840532)
XLA Ops:
  0.6 0.0 copy-start.1
  0.6 0.0 copy-start.3
  0.7 0.0 copy-start
  0.7 0.0 copy-start.2
  0.7 0.0 copy-start.5
  0.7 0.0 copy-start.4
  0.7 3.4 %collective-permute-start = (bf16[144,2048]{1,0:T(8,128)(2,1)}, bf16[144,2048]{1,0:T(8,128)(2,1)S(1)}, u32[]{:S(2)}, u32[]{:S(2)}) collective-permute-start(bf16[144,2048]{1,0:T(8,128)(2,1)} %k_ref.1), channel_id=1, source_target_pairs={{0,2},{2,4},{4,6},{6,8},{8,10},{10,12},{12,14},{14,16},{16,18},{18... | collective-permute-start | bytes 1769480 | tf_op jit(solution)/shard_map/ppermute | solution.py:475
  4.1 2.2 %pack.1 = bf16[2320,128]{1,0:T(8,128)(2,1)S(1)} custom-call(bf16[3,144,2048]{2,1,0:T(8,128)(2,1)} %m_ref.1, bf16[3,144,2048]{2,1,0:T(8,128)(2,1)} %s_ref.1, f32[3,3,2048]{2,1,0:T(4,128)} %mw_ref.3, f32[3,3,2048]{2,1,0:T(4,128)} %sw_ref.3), custom_call_target="tpu_custom_call" | custom-call | flops 5898240 | bytes 1769472 | tf_op jit(solution)/shard_map/pack/pallas_call | solution.py:128
  6.3 3.1 %collective-permute-start.2 = (bf16[2320,128]{1,0:T(8,128)(2,1)S(1)}, bf16[2320,128]{1,0:T(8,128)(2,1)S(1)}, u32[]{:S(2)}, u32[]{:S(2)}) collective-permute-start(bf16[2320,128]{1,0:T(8,128)(2,1)S(1)} %pack.1), channel_id=1, source_target_pairs={{0,2},{2,4},{4,6},{6,8},{8,10},{10,12},{12,14},{14,16},{16,18},{18... | collective-permute-start | bytes 1781768 | tf_op jit(solution)/shard_map/ppermute | solution.py:475
  9.4 3.1 %collective-permute-start.1 = (bf16[144,2048]{1,0:T(8,128)(2,1)}, bf16[144,2048]{1,0:T(8,128)(2,1)S(1)}, u32[]{:S(2)}, u32[]{:S(2)}) collective-permute-start(bf16[144,2048]{1,0:T(8,128)(2,1)} %v_ref.1), channel_id=1, source_target_pairs={{0,2},{2,4},{4,6},{6,8},{8,10},{10,12},{12,14},{14,16},{16,18},{18... | collective-permute-start | bytes 1769480 | tf_op jit(solution)/shard_map/ppermute | solution.py:475
  12.6 0.0 copy-done.1
  12.6 0.0 copy-done.3
  12.6 0.0 copy-done
  12.6 0.0 copy-done.2
  12.6 0.0 copy-done.5
  12.6 0.0 copy-done.4
  12.6 0.0 copy-start.6
  12.6 0.0 copy-start.7
  12.6 0.0 copy-start.8
  12.7 12.2 %own_part.1 = (f32[144,2048]{1,0:T(8,128)S(1)}, f32[144,2048]{1,0:T(8,128)S(1)}, f32[144,2048]{1,0:T(8,128)S(1)}, f32[144,128]{1,0:T(8,128)S(1)}, f32[128,2048]{1,0:T(8,128)S(1)}, /*index=5*/f32[6,8,2048]{2,1,0:T(8,128)S(1)}) custom-call(bf16[3,144,2048]{2,1,0:T(8,128)(2,1)S(1)} %copy-done, bf16[3,144,2048]{2,1,0:T(8,128)(2,1)S(1)} %copy-done.1, ...), custom_call_target="tpu_custom_call" | custom-call | flops 53084160 | bytes 7077888 | tf_op jit(solution)/shard_map/own_part/pallas_call | solution.py:227
  24.9 0.0 collective-permute-done.before_ref
  24.9 0.0 copy-done.6
  24.9 0.0 copy-done.7
  24.9 0.0 copy-done.8
  24.9 2.8 %score.1 = (bf16[16,144,144]{2,1,0:T(8,128)(2,1)S(1)}, f32[144,2048]{1,0:T(8,128)S(1)}, f32[144,2048]{1,0:T(8,128)S(1)}) custom-call(bf16[144,2048]{1,0:T(8,128)(2,1)S(1)} %copy-done.6, bf16[144,2048]{1,0:T(8,128)(2,1)S(1)} %copy-done.7, bf16[144,2048]{1,0:T(8,128)(2,1)S(1)} %collective-permute-done.before_ref, bf16[144,2048]{1,0:T(8,128)(2,1)S(1)} %copy-done.8), custom_call_target="tpu_custom_call" | custom-call | flops 339738624 | bytes 4128768 | tf_op jit(solution)/shard_map/score/pallas_call | solution.py:379
  27.7 4.0 %collective-permute-done.2.packet_ref = bf16[2320,128]{1,0:T(8,128)(2,1)S(1)} collective-permute-done((bf16[2320,128]{1,0:T(8,128)(2,1)S(1)}, bf16[2320,128]{1,0:T(8,128)(2,1)S(1)}, u32[]{:S(2)}, u32[]{:S(2)}) %collective-permute-start.2) | collective-permute-done | bytes 593952 | tf_op jit(solution)/shard_map/ppermute | solution.py:475
  31.8 6.9 %mix.1 = (f32[8,2048]{1,0:T(8,128)S(1)}, f32[144,2048]{1,0:T(8,128)S(1)}, f32[2,144,128]{2,1,0:T(8,128)S(1)}) custom-call(bf16[2320,128]{1,0:T(8,128)(2,1)S(1)} %collective-permute-done.2.packet_ref, f32[144,2048]{1,0:T(8,128)S(1)} %get-tuple-element.24.own_ref, f32[144,2048]{1,0:T(8,128)S(1)} %get-tuple-element.25.z0_ref, ...), custom_call_target="tpu_custom_call" | custom-call | flops 41287680 | bytes 4718592 | tf_op jit(solution)/shard_map/mix/pallas_call | solution.py:325
  38.7 5.8 %collective-permute-done.1.before_ref = bf16[144,2048]{1,0:T(8,128)(2,1)S(1)} collective-permute-done((bf16[144,2048]{1,0:T(8,128)(2,1)}, bf16[144,2048]{1,0:T(8,128)(2,1)S(1)}, u32[]{:S(2)}, u32[]{:S(2)}) %collective-permute-start.1) | collective-permute-done | bytes 589856 | tf_op jit(solution)/shard_map/ppermute | solution.py:475
  44.4 0.5 value_mix.1
  44.9 1.6 %collective-permute-start.3 = (f32[3,144,128]{2,1,0:T(8,128)S(1)}, f32[3,144,128]{2,1,0:T(8,128)S(1)}, u32[]{:S(2)}, u32[]{:S(2)}) collective-permute-start(f32[3,144,128]{2,1,0:T(8,128)S(1)} %get-tuple-element.30.refs_0_), channel_id=1, source_target_pairs={{0,1},{1,0},{2,3},{3,2},{4,5},{5,4},{6,7},{7,6},{8,9},{9,8},{10,11... | collective-permute-start | bytes 663560 | tf_op jit(solution)/shard_map/ppermute | solution.py:481
  46.5 1.1 %collective-permute-done.3.refs_1_ = f32[3,144,128]{2,1,0:T(8,128)S(1)} collective-permute-done((f32[3,144,128]{2,1,0:T(8,128)S(1)}, f32[3,144,128]{2,1,0:T(8,128)S(1)}, u32[]{:S(2)}, u32[]{:S(2)}) %collective-permute-start.3) | collective-permute-done | bytes 221216 | tf_op jit(solution)/shard_map/ppermute | solution.py:481
  47.6 1.4 %normalize.1 = (bf16[144,2048]{1,0:T(8,128)(2,1)}, bf16[144,2048]{1,0:T(8,128)(2,1)}, bf16[144,2048]{1,0:T(8,128)(2,1)}) custom-call(f32[3,144,128]{2,1,0:T(8,128)S(1)} %get-tuple-element.30.refs_0_, f32[3,144,128]{2,1,0:T(8,128)S(1)} %collective-permute-done.3.refs_1_, f32[144,2048]{1,0:T(8,128)S(1)} %get-tuple-element.31.refs_2_, ...), custom_call_target="tpu_custom_call" | custom-call | flops 3538944 | bytes 5308416 | tf_op jit(solution)/shard_map/normalize/pallas_call | solution.py:458
Async XLA Ops:
  0.6 11.9 %copy-start.1 = (bf16[3,144,2048]{2,1,0:T(8,128)(2,1)S(1)}, bf16[3,144,2048]{2,1,0:T(8,128)(2,1)}, u32[]{:S(2)}) copy-start(bf16[3,144,2048]{2,1,0:T(8,128)(2,1)} %s_ref.1) | copy-start | bytes 5308420
  0.6 11.9 %copy-start.3 = (f32[3,3,2048]{2,1,0:T(4,128)S(1)}, f32[3,3,2048]{2,1,0:T(4,128)}, u32[]{:S(2)}) copy-start(f32[3,3,2048]{2,1,0:T(4,128)} %sw_ref.3) | copy-start | bytes 221188
  0.7 11.9 %copy-start = (bf16[3,144,2048]{2,1,0:T(8,128)(2,1)S(1)}, bf16[3,144,2048]{2,1,0:T(8,128)(2,1)}, u32[]{:S(2)}) copy-start(bf16[3,144,2048]{2,1,0:T(8,128)(2,1)} %m_ref.1) | copy-start | bytes 5308420
  0.7 11.9 %copy-start.2 = (f32[3,3,2048]{2,1,0:T(4,128)S(1)}, f32[3,3,2048]{2,1,0:T(4,128)}, u32[]{:S(2)}) copy-start(f32[3,3,2048]{2,1,0:T(4,128)} %mw_ref.3) | copy-start | bytes 221188
  0.7 11.9 %copy-start.5 = (f32[2048]{0:T(1024)S(1)}, f32[2048]{0:T(1024)}, u32[]{:S(2)}) copy-start(f32[2048]{0:T(1024)} %param.16) | copy-start | bytes 24580
  0.7 11.9 %copy-start.4 = (f32[7,2048]{1,0:T(8,128)S(1)}, f32[7,2048]{1,0:T(8,128)}, u32[]{:S(2)}) copy-start(f32[7,2048]{1,0:T(8,128)} %filter_ref.3) | copy-start | bytes 172036
  0.7 24.2 %collective-permute-start = (bf16[144,2048]{1,0:T(8,128)(2,1)}, bf16[144,2048]{1,0:T(8,128)(2,1)S(1)}, u32[]{:S(2)}, u32[]{:S(2)}) collective-permute-start(bf16[144,2048]{1,0:T(8,128)(2,1)} %k_ref.1), channel_id=1, source_target_pairs={{0,2},{2,4},{4,6},{6,8},{8,10},{10,12},{12,14},{14,16},{16,18},{18... | collective-permute-start | bytes 1769480 | tf_op jit(solution)/shard_map/ppermute | solution.py:475
  6.3 25.5 %collective-permute-start.2 = (bf16[2320,128]{1,0:T(8,128)(2,1)S(1)}, bf16[2320,128]{1,0:T(8,128)(2,1)S(1)}, u32[]{:S(2)}, u32[]{:S(2)}) collective-permute-start(bf16[2320,128]{1,0:T(8,128)(2,1)S(1)} %pack.1), channel_id=1, source_target_pairs={{0,2},{2,4},{4,6},{6,8},{8,10},{10,12},{12,14},{14,16},{16,18},{18... | collective-permute-start | bytes 1781768 | tf_op jit(solution)/shard_map/ppermute | solution.py:475
  9.4 35.0 %collective-permute-start.1 = (bf16[144,2048]{1,0:T(8,128)(2,1)}, bf16[144,2048]{1,0:T(8,128)(2,1)S(1)}, u32[]{:S(2)}, u32[]{:S(2)}) collective-permute-start(bf16[144,2048]{1,0:T(8,128)(2,1)} %v_ref.1), channel_id=1, source_target_pairs={{0,2},{2,4},{4,6},{6,8},{8,10},{10,12},{12,14},{14,16},{16,18},{18... | collective-permute-start | bytes 1769480 | tf_op jit(solution)/shard_map/ppermute | solution.py:475
  12.6 12.2 %copy-start.6 = (bf16[144,2048]{1,0:T(8,128)(2,1)S(1)}, bf16[144,2048]{1,0:T(8,128)(2,1)}, u32[]{:S(2)}) copy-start(bf16[144,2048]{1,0:T(8,128)(2,1)} %q_ref.1) | copy-start | bytes 1769476
  12.6 12.2 %copy-start.7 = (bf16[144,2048]{1,0:T(8,128)(2,1)S(1)}, bf16[144,2048]{1,0:T(8,128)(2,1)}, u32[]{:S(2)}) copy-start(bf16[144,2048]{1,0:T(8,128)(2,1)} %k_ref.1) | copy-start | bytes 1769476
  12.6 12.2 %copy-start.8 = (bf16[144,2048]{1,0:T(8,128)(2,1)S(1)}, bf16[144,2048]{1,0:T(8,128)(2,1)}, u32[]{:S(2)}) copy-start(bf16[144,2048]{1,0:T(8,128)(2,1)} %v_ref.1) | copy-start | bytes 1769476
  44.9 2.7 %collective-permute-start.3 = (f32[3,144,128]{2,1,0:T(8,128)S(1)}, f32[3,144,128]{2,1,0:T(8,128)S(1)}, u32[]{:S(2)}, u32[]{:S(2)}) collective-permute-start(f32[3,144,128]{2,1,0:T(8,128)S(1)} %get-tuple-element.30.refs_0_), channel_id=1, source_target_pairs={{0,1},{1,0},{2,3},{3,2},{4,5},{5,4},{6,7},{7,6},{8,9},{9,8},{10,11... | collective-permute-start | bytes 663560 | tf_op jit(solution)/shard_map/ppermute | solution.py:481

commit v7 on v4

--- a/solution.py
+++ b/solution.py
@@ -146,8 +146,8 @@
 
 def own_kernel(
     per,
-    m_ref,
-    s_ref,
+    m_hbm_ref,
+    s_hbm_ref,
     mw_ref,
     sw_ref,
     raw_hbm_ref,
@@ -159,6 +159,8 @@
     square_ref,
     taps_ref,
     heads_ref,
+    m_ref,
+    s_ref,
     raw_ref,
     held_ref,
     sems,
@@ -170,17 +172,23 @@
 
     def fetch(n):
         at = pl.ds(pl.multiple_of(n * width, width), width)
-        return pltpu.make_async_copy(raw_hbm_ref.at[:, at], raw_ref.at[:, at], sems.at[n])
+        return (
+            pltpu.make_async_copy(s_hbm_ref.at[:, :, at], s_ref.at[:, :, at], sems.at[0, n]),
+            pltpu.make_async_copy(m_hbm_ref.at[:, :, at], m_ref.at[:, :, at], sems.at[1, n]),
+            pltpu.make_async_copy(raw_hbm_ref.at[:, at], raw_ref.at[:, at], sems.at[2, n]),
+        )
 
     for n in range(channels // width):
-        fetch(n).start()
+        for copy in fetch(n):
+            copy.start()
     square_ref[...] = jnp.zeros_like(square_ref)
 
     @pl.loop(0, channels // LANES)
     def _(k):
         @pl.when(k % per == 0)
         def _():
-            fetch(k // per).wait()
+            for copy in fetch(k // per):
+                copy.wait()
 
         lanes = lane_block(k)
         u = [s_ref[n, :, lanes].astype(F32) for n in range(3)]
@@ -223,7 +231,8 @@
 def own_part(mr, se, mr_short, se_short, raw, decay, se_filter, per):
     _, rows, channels = mr.shape
     mixed = jax.ShapeDtypeStruct((rows, channels), F32)
-    raw = pltpu.with_memory_space_constraint(raw, pltpu.HBM)
+    mr, se, raw = (pltpu.with_memory_space_constraint(x, pltpu.HBM) for x in (mr, se, raw))
+    in_hbm = pl.BlockSpec(memory_space=pltpu.HBM)
     return pl.pallas_call(
         functools.partial(own_kernel, per),
         out_shape=(
@@ -234,14 +243,16 @@
             jax.ShapeDtypeStruct((MEDIUM_TAPS, channels), F32),
             jax.ShapeDtypeStruct((6, 8, channels), F32),
         ),
-        in_specs=[in_vmem()] * 4 + [pl.BlockSpec(memory_space=pltpu.HBM)] + [in_vmem()] * 2,
+        in_specs=[in_hbm] * 2 + [in_vmem()] * 2 + [in_hbm] + [in_vmem()] * 2,
         out_specs=(in_vmem(),) * 6,
         scratch_shapes=[
+            pltpu.VMEM(mr.shape, BF16),
+            pltpu.VMEM(se.shape, BF16),
             pltpu.VMEM((MEDIUM_TAPS, channels), F32),
             pltpu.VMEM((MEDIUM_TAPS, LANES), F32),
-            pltpu.SemaphoreType.DMA((channels // (per * LANES),)),
+            pltpu.SemaphoreType.DMA((3, channels // (per * LANES))),
         ],
-        compiler_params=params(),
+        compiler_params=params(10),
         cost_estimate=cost(180 * rows * channels, 24 * rows * channels),
         name="own_part",
     )(mr, se, mr_short, se_short, raw, decay, se_filter)

time: 48.6 us -> 48.5 us (level)
  transfers between devices with their start and end apart: 5 -> 5, of which waited for: 4 -> 4; matrix products, arithmetic and copies ran while one was open for 0% -> 0% of each run, Pallas kernels for 52% -> 53%
where the time goes in v7:
time: 48.5 us; the launch traced here: 48.2 us
  Pallas kernels  27.1 us (56%)
  starting transfers between devices  13.9 us (29%)
  waiting for transfers between devices  6.4 us (13%)
  between operations  0.82 us (2%)
    pallas_call x1, Pallas kernels, own_part(): pl.pallas_call(functools.partial(own_kernel, per), out_shape=(mixed, mixe...  12.6 us
    ppermute x3, starting transfers between devices, from_behind(): lax.ppermute(value, 'ctx', [(source, source + 1) for source in range(coun...  9.49 us
    pallas_call x1, Pallas kernels, mix(): pl.pallas_call(mix_kernel, out_shape=(jax.ShapeDtypeStruct((8, channels),...  6.86 us
    ppermute x3, waiting for transfers between devices, from_behind(): lax.ppermute(value, 'ctx', [(source, source + 1) for source in range(coun...  4.48 us
    ppermute x2, starting transfers between devices, of_panels(): lax.ppermute(square, 'panel', [(n, (n + shift) % count) for n in range(co...  4.37 us
    pallas_call x1, Pallas kernels, score(): pl.pallas_call(functools.partial(score_kernel, per), out_shape=(jax.Shape...  2.83 us
    pallas_call x1, Pallas kernels, pack(): pl.pallas_call(functools.partial(pack_kernel, per), out_shape=jax.ShapeDt...  2.22 us
    pallas_call x2, Pallas kernels, normalize(): pl.pallas_call(functools.partial(normalize_kernel, count, len(squares), p...  2.19 us
  transfers between devices with their start and end apart: 5, of which 4 were waited for; matrix products, arithmetic and copies ran while one was open for 0% of the time, Pallas kernels for 53%

profile of v7, /device:TPU:9, one launch (start us, length us, event | category | flops | bytes accessed | tf_op | source)
XLA Modules:
  0.0 48.2 jit_solution(16809073583964949676)
XLA Ops:
  0.6 0.0 copy-start
  0.6 0.0 copy-start.1
  0.7 0.0 copy-start.2
  0.7 0.0 copy-start.3
  0.7 3.3 %collective-permute-start.2 = (bf16[144,2048]{1,0:T(8,128)(2,1)}, bf16[144,2048]{1,0:T(8,128)(2,1)S(1)}, u32[]{:S(2)}, u32[]{:S(2)}) collective-permute-start(bf16[144,2048]{1,0:T(8,128)(2,1)} %k_ref.1), channel_id=1, source_target_pairs={{0,2},{2,4},{4,6},{6,8},{8,10},{10,12},{12,14},{14,16},{16,18},{18... | collective-permute-start | bytes 1769480 | tf_op jit(solution)/shard_map/ppermute | solution.py:485
  3.9 2.2 %pack.1 = bf16[2320,128]{1,0:T(8,128)(2,1)S(1)} custom-call(bf16[3,144,2048]{2,1,0:T(8,128)(2,1)} %mr_ref.1, bf16[3,144,2048]{2,1,0:T(8,128)(2,1)} %se_ref.1, f32[3,3,2048]{2,1,0:T(4,128)} %mw_ref.3, f32[3,3,2048]{2,1,0:T(4,128)} %sw_ref.3), custom_call_target="tpu_custom_call" | custom-call | flops 5898240 | bytes 1769472 | tf_op jit(solution)/shard_map/pack/pallas_call | solution.py:128
  6.2 3.1 %collective-permute-start.1 = (bf16[2320,128]{1,0:T(8,128)(2,1)S(1)}, bf16[2320,128]{1,0:T(8,128)(2,1)S(1)}, u32[]{:S(2)}, u32[]{:S(2)}) collective-permute-start(bf16[2320,128]{1,0:T(8,128)(2,1)S(1)} %pack.1), channel_id=1, source_target_pairs={{0,2},{2,4},{4,6},{6,8},{8,10},{10,12},{12,14},{14,16},{16,18},{18... | collective-permute-start | bytes 1781768 | tf_op jit(solution)/shard_map/ppermute | solution.py:485
  9.3 0.0 copy-done
  9.3 0.0 copy-done.1
  9.3 0.0 copy-done.2
  9.3 0.0 copy-done.3
  9.3 0.0 copy-start.6
  9.3 0.0 copy-start.4
  9.3 0.0 copy-start.5
  9.4 12.6 %own_part.1 = (f32[144,2048]{1,0:T(8,128)S(1)}, f32[144,2048]{1,0:T(8,128)S(1)}, f32[144,2048]{1,0:T(8,128)S(1)}, f32[144,128]{1,0:T(8,128)S(1)}, f32[128,2048]{1,0:T(8,128)S(1)}, /*index=5*/f32[6,8,2048]{2,1,0:T(8,128)S(1)}) custom-call(bf16[3,144,2048]{2,1,0:T(8,128)(2,1)} %mr_ref.1, bf16[3,144,2048]{2,1,0:T(8,128)(2,1)} %se_ref.1, ...), custom_call_target="tpu_custom_call" | custom-call | flops 53084160 | bytes 7077888 | tf_op jit(solution)/shard_map/own_part/pallas_call | solution.py:236
  21.9 0.0 copy-done.6
  21.9 3.1 %collective-permute-start = (bf16[144,2048]{1,0:T(8,128)(2,1)S(1)}, bf16[144,2048]{1,0:T(8,128)(2,1)S(1)}, u32[]{:S(2)}, u32[]{:S(2)}) collective-permute-start(bf16[144,2048]{1,0:T(8,128)(2,1)S(1)} %copy-done.6), channel_id=1, source_target_pairs={{0,2},{2,4},{4,6},{6,8},{8,10},{10,12},{12,14},{14,16},{16,18},{18... | collective-permute-start | bytes 1769480 | tf_op jit(solution)/shard_map/ppermute | solution.py:485
  25.1 0.0 collective-permute-done.2.before_ref
  25.1 0.0 copy-done.4
  25.1 0.0 copy-done.5
  25.1 2.8 %score.1 = (bf16[16,144,144]{2,1,0:T(8,128)(2,1)S(1)}, f32[144,2048]{1,0:T(8,128)S(1)}, f32[144,2048]{1,0:T(8,128)S(1)}) custom-call(bf16[144,2048]{1,0:T(8,128)(2,1)S(1)} %copy-done.4, bf16[144,2048]{1,0:T(8,128)(2,1)S(1)} %copy-done.5, bf16[144,2048]{1,0:T(8,128)(2,1)S(1)} %collective-permute-done.2.before_ref, bf16[144,2048]{1,0:T(8,128)(2,1)S(1)} %copy-done.6), custom_call_target="tpu_custom_call" | custom-call | flops 339738624 | bytes 4128768 | tf_op jit(solution)/shard_map/score/pallas_call | solution.py:390
  27.9 3.7 %collective-permute-done.1.packet_ref = bf16[2320,128]{1,0:T(8,128)(2,1)S(1)} collective-permute-done((bf16[2320,128]{1,0:T(8,128)(2,1)S(1)}, bf16[2320,128]{1,0:T(8,128)(2,1)S(1)}, u32[]{:S(2)}, u32[]{:S(2)}) %collective-permute-start.1) | collective-permute-done | bytes 593952 | tf_op jit(solution)/shard_map/ppermute | solution.py:485
  31.6 6.9 %mix.1 = (f32[8,2048]{1,0:T(8,128)S(1)}, f32[144,2048]{1,0:T(8,128)S(1)}, f32[2,144,128]{2,1,0:T(8,128)S(1)}) custom-call(bf16[2320,128]{1,0:T(8,128)(2,1)S(1)} %collective-permute-done.1.packet_ref, f32[144,2048]{1,0:T(8,128)S(1)} %get-tuple-element.30.own_ref, f32[144,2048]{1,0:T(8,128)S(1)} %get-tuple-element.31.z0_ref, ...), custom_call_target="tpu_custom_call" | custom-call | flops 41287680 | bytes 4718592 | tf_op jit(solution)/shard_map/mix/pallas_call | solution.py:336
  38.5 2.8 %collective-permute-start.3 = (f32[2,144,128]{2,1,0:T(8,128)S(1)}, f32[2,144,128]{2,1,0:T(8,128)S(1)}, u32[]{:S(2)}, u32[]{:S(2)}) collective-permute-start(f32[2,144,128]{2,1,0:T(8,128)S(1)} %get-tuple-element.35.refs_0_), channel_id=1, source_target_pairs={{0,1},{1,0},{2,3},{3,2},{4,5},{5,4},{6,7},{7,6},{8,9},{9,8},{10,11... | collective-permute-start | bytes 442376 | tf_op jit(solution)/shard_map/ppermute | solution.py:491
  41.3 1.0 %collective-permute-done.3.refs_1_ = f32[2,144,128]{2,1,0:T(8,128)S(1)} collective-permute-done((f32[2,144,128]{2,1,0:T(8,128)S(1)}, f32[2,144,128]{2,1,0:T(8,128)S(1)}, u32[]{:S(2)}, u32[]{:S(2)}) %collective-permute-start.3) | collective-permute-done | bytes 147488 | tf_op jit(solution)/shard_map/ppermute | solution.py:491
  42.3 1.2 %normalize.2 = (bf16[144,2048]{1,0:T(8,128)(2,1)}, bf16[144,2048]{1,0:T(8,128)(2,1)}) custom-call(f32[2,144,128]{2,1,0:T(8,128)S(1)} %get-tuple-element.35.refs_0_, f32[2,144,128]{2,1,0:T(8,128)S(1)} %collective-permute-done.3.refs_1_, f32[144,2048]{1,0:T(8,128)S(1)} %get-tuple-element.36.refs_2_, f32[144,2048]{1,0:T(8,128)S(1)} %get-tuple-element.37.refs_3_, ...), custom_call_target="tpu_custom_call" | custom-call | flops 2359296 | bytes 3538944 | tf_op jit(solution)/shard_map/normalize/pallas_call | solution.py:468
  43.5 0.8 %collective-permute-done.before_ref = bf16[144,2048]{1,0:T(8,128)(2,1)S(1)} collective-permute-done((bf16[144,2048]{1,0:T(8,128)(2,1)S(1)}, bf16[144,2048]{1,0:T(8,128)(2,1)S(1)}, u32[]{:S(2)}, u32[]{:S(2)}) %collective-permute-start) | collective-permute-done | bytes 589856 | tf_op jit(solution)/shard_map/ppermute | solution.py:485
  44.3 0.5 value_mix.1
  44.7 1.6 %collective-permute-start.4 = (f32[1,144,128]{2,1,0:T(8,128)S(1)}, f32[1,144,128]{2,1,0:T(8,128)S(1)}, u32[]{:S(2)}, u32[]{:S(2)}) collective-permute-start(f32[1,144,128]{2,1,0:T(8,128)S(1)} %get-tuple-element.47.refs_0_), channel_id=1, source_target_pairs={{0,1},{1,0},{2,3},{3,2},{4,5},{5,4},{6,7},{7,6},{8,9},{9,8},{10,11... | collective-permute-start | bytes 221192 | tf_op jit(solution)/shard_map/ppermute | solution.py:491
  46.4 0.9 %collective-permute-done.4.refs_1_ = f32[1,144,128]{2,1,0:T(8,128)S(1)} collective-permute-done((f32[1,144,128]{2,1,0:T(8,128)S(1)}, f32[1,144,128]{2,1,0:T(8,128)S(1)}, u32[]{:S(2)}, u32[]{:S(2)}) %collective-permute-start.4) | collective-permute-done | bytes 73760 | tf_op jit(solution)/shard_map/ppermute | solution.py:491
  47.3 1.0 %normalize.3 = bf16[144,2048]{1,0:T(8,128)(2,1)} custom-call(f32[1,144,128]{2,1,0:T(8,128)S(1)} %get-tuple-element.47.refs_0_, f32[1,144,128]{2,1,0:T(8,128)S(1)} %collective-permute-done.4.refs_1_, f32[144,2048]{1,0:T(8,128)S(1)} %get-tuple-element.48.refs_2_), custom_call_target="tpu_custom_call" | custom-call | flops 1179648 | bytes 1769472 | tf_op jit(solution)/shard_map/normalize/pallas_call | solution.py:468
Async XLA Ops:
  0.6 8.7 %copy-start = (f32[3,3,2048]{2,1,0:T(4,128)S(1)}, f32[3,3,2048]{2,1,0:T(4,128)}, u32[]{:S(2)}) copy-start(f32[3,3,2048]{2,1,0:T(4,128)} %mw_ref.3) | copy-start | bytes 221188
  0.6 8.7 %copy-start.1 = (f32[3,3,2048]{2,1,0:T(4,128)S(1)}, f32[3,3,2048]{2,1,0:T(4,128)}, u32[]{:S(2)}) copy-start(f32[3,3,2048]{2,1,0:T(4,128)} %sw_ref.3) | copy-start | bytes 221188
  0.7 8.7 %copy-start.2 = (f32[7,2048]{1,0:T(8,128)S(1)}, f32[7,2048]{1,0:T(8,128)}, u32[]{:S(2)}) copy-start(f32[7,2048]{1,0:T(8,128)} %filter_ref.3) | copy-start | bytes 172036
  0.7 8.7 %copy-start.3 = (f32[2048]{0:T(1024)S(1)}, f32[2048]{0:T(1024)}, u32[]{:S(2)}) copy-start(f32[2048]{0:T(1024)} %param.16) | copy-start | bytes 24580
  0.7 24.4 %collective-permute-start.2 = (bf16[144,2048]{1,0:T(8,128)(2,1)}, bf16[144,2048]{1,0:T(8,128)(2,1)S(1)}, u32[]{:S(2)}, u32[]{:S(2)}) collective-permute-start(bf16[144,2048]{1,0:T(8,128)(2,1)} %k_ref.1), channel_id=1, source_target_pairs={{0,2},{2,4},{4,6},{6,8},{8,10},{10,12},{12,14},{14,16},{16,18},{18... | collective-permute-start | bytes 1769480 | tf_op jit(solution)/shard_map/ppermute | solution.py:485
  6.2 25.5 %collective-permute-start.1 = (bf16[2320,128]{1,0:T(8,128)(2,1)S(1)}, bf16[2320,128]{1,0:T(8,128)(2,1)S(1)}, u32[]{:S(2)}, u32[]{:S(2)}) collective-permute-start(bf16[2320,128]{1,0:T(8,128)(2,1)S(1)} %pack.1), channel_id=1, source_target_pairs={{0,2},{2,4},{4,6},{6,8},{8,10},{10,12},{12,14},{14,16},{16,18},{18... | collective-permute-start | bytes 1781768 | tf_op jit(solution)/shard_map/ppermute | solution.py:485
  9.3 12.6 %copy-start.6 = (bf16[144,2048]{1,0:T(8,128)(2,1)S(1)}, bf16[144,2048]{1,0:T(8,128)(2,1)}, u32[]{:S(2)}) copy-start(bf16[144,2048]{1,0:T(8,128)(2,1)} %v_ref.1) | copy-start | bytes 1769476
  9.3 15.7 %copy-start.4 = (bf16[144,2048]{1,0:T(8,128)(2,1)S(1)}, bf16[144,2048]{1,0:T(8,128)(2,1)}, u32[]{:S(2)}) copy-start(bf16[144,2048]{1,0:T(8,128)(2,1)} %q_ref.1) | copy-start | bytes 1769476
  9.3 15.7 %copy-start.5 = (bf16[144,2048]{1,0:T(8,128)(2,1)S(1)}, bf16[144,2048]{1,0:T(8,128)(2,1)}, u32[]{:S(2)}) copy-start(bf16[144,2048]{1,0:T(8,128)(2,1)} %k_ref.1) | copy-start | bytes 1769476
  21.9 22.3 %collective-permute-start = (bf16[144,2048]{1,0:T(8,128)(2,1)S(1)}, bf16[144,2048]{1,0:T(8,128)(2,1)S(1)}, u32[]{:S(2)}, u32[]{:S(2)}) collective-permute-start(bf16[144,2048]{1,0:T(8,128)(2,1)S(1)} %copy-done.6), channel_id=1, source_target_pairs={{0,2},{2,4},{4,6},{6,8},{8,10},{10,12},{12,14},{14,16},{16,18},{18... | collective-permute-start | bytes 1769480 | tf_op jit(solution)/shard_map/ppermute | solution.py:485
  38.5 3.8 %collective-permute-start.3 = (f32[2,144,128]{2,1,0:T(8,128)S(1)}, f32[2,144,128]{2,1,0:T(8,128)S(1)}, u32[]{:S(2)}, u32[]{:S(2)}) collective-permute-start(f32[2,144,128]{2,1,0:T(8,128)S(1)} %get-tuple-element.35.refs_0_), channel_id=1, source_target_pairs={{0,1},{1,0},{2,3},{3,2},{4,5},{5,4},{6,7},{7,6},{8,9},{9,8},{10,11... | collective-permute-start | bytes 442376 | tf_op jit(solution)/shard_map/ppermute | solution.py:491
  44.7 2.5 %collective-permute-start.4 = (f32[1,144,128]{2,1,0:T(8,128)S(1)}, f32[1,144,128]{2,1,0:T(8,128)S(1)}, u32[]{:S(2)}, u32[]{:S(2)}) collective-permute-start(f32[1,144,128]{2,1,0:T(8,128)S(1)} %get-tuple-element.47.refs_0_), channel_id=1, source_target_pairs={{0,1},{1,0},{2,3},{3,2},{4,5},{5,4},{6,7},{7,6},{8,9},{9,8},{10,11... | collective-permute-start | bytes 221192 | tf_op jit(solution)/shard_map/ppermute | solution.py:491

commit v8 on v7

--- a/solution.py
+++ b/solution.py
@@ -148,22 +148,27 @@
     per,
     m_hbm_ref,
     s_hbm_ref,
-    mw_ref,
-    sw_ref,
     raw_hbm_ref,
-    decay_ref,
-    filter_ref,
+    mw_hbm_ref,
+    sw_hbm_ref,
+    decay_hbm_ref,
+    filter_hbm_ref,
     own_ref,
     z0_ref,
     se_ref,
     square_ref,
     taps_ref,
     heads_ref,
+    mw_ref,
+    sw_ref,
+    filter_ref,
     m_ref,
     s_ref,
     raw_ref,
+    decay_ref,
     held_ref,
     sems,
+    small_sems,
 ):
     rows, channels = own_ref.shape
     tiles = rows // 8
@@ -178,9 +183,19 @@
             pltpu.make_async_copy(raw_hbm_ref.at[:, at], raw_ref.at[:, at], sems.at[2, n]),
         )
 
+    small = [
+        pltpu.make_async_copy(mw_hbm_ref, mw_ref, small_sems.at[0]),
+        pltpu.make_async_copy(sw_hbm_ref, sw_ref, small_sems.at[1]),
+        pltpu.make_async_copy(decay_hbm_ref, decay_ref, small_sems.at[2]),
+        pltpu.make_async_copy(filter_hbm_ref, filter_ref, small_sems.at[3]),
+    ]
+    for copy in small:
+        copy.start()
     for n in range(channels // width):
         for copy in fetch(n):
             copy.start()
+    for copy in small:
+        copy.wait()
     square_ref[...] = jnp.zeros_like(square_ref)
 
     @pl.loop(0, channels // LANES)
@@ -231,8 +246,7 @@
 def own_part(mr, se, mr_short, se_short, raw, decay, se_filter, per):
     _, rows, channels = mr.shape
     mixed = jax.ShapeDtypeStruct((rows, channels), F32)
-    mr, se, raw = (pltpu.with_memory_space_constraint(x, pltpu.HBM) for x in (mr, se, raw))
-    in_hbm = pl.BlockSpec(memory_space=pltpu.HBM)
+    operands = (mr, se, raw, mr_short, se_short, decay, se_filter)
     return pl.pallas_call(
         functools.partial(own_kernel, per),
         out_shape=(
@@ -242,20 +256,25 @@
             jax.ShapeDtypeStruct((rows, LANES), F32),
             jax.ShapeDtypeStruct((MEDIUM_TAPS, channels), F32),
             jax.ShapeDtypeStruct((6, 8, channels), F32),
+            jax.ShapeDtypeStruct(mr_short.shape, F32),
+            jax.ShapeDtypeStruct(se_short.shape, F32),
+            jax.ShapeDtypeStruct(se_filter.shape, F32),
         ),
-        in_specs=[in_hbm] * 2 + [in_vmem()] * 2 + [in_hbm] + [in_vmem()] * 2,
-        out_specs=(in_vmem(),) * 6,
+        in_specs=[pl.BlockSpec(memory_space=pltpu.HBM)] * 7,
+        out_specs=(in_vmem(),) * 9,
         scratch_shapes=[
             pltpu.VMEM(mr.shape, BF16),
             pltpu.VMEM(se.shape, BF16),
             pltpu.VMEM((MEDIUM_TAPS, channels), F32),
+            pltpu.VMEM(decay.shape, F32),
             pltpu.VMEM((MEDIUM_TAPS, LANES), F32),
             pltpu.SemaphoreType.DMA((3, channels // (per * LANES))),
+            pltpu.SemaphoreType.DMA((4,)),
         ],
         compiler_params=params(10),
         cost_estimate=cost(180 * rows * channels, 24 * rows * channels),
         name="own_part",
-    )(mr, se, mr_short, se_short, raw, decay, se_filter)
+    )(*(pltpu.with_memory_space_constraint(x, pltpu.HBM) for x in operands))
 
 
 def mix_kernel(
@@ -497,7 +516,7 @@
     decay = decay[None, :]
     key_before = from_behind(keys)
     packet = from_behind(pack(se, mr, se_short, mr_short, 4))
-    own, z0, se_mix, se_square, taps, heads = own_part(
+    own, z0, se_mix, se_square, taps, heads, mr_taps, se_taps, filter_taps = own_part(
         mr, se, mr_short, se_short, raw, decay, se_filter, 4
     )
     values_later, own = lax.optimization_barrier((values, own))
@@ -505,7 +524,7 @@
     probs, attended, inverse = score(queries, keys, key_before, values, 4)
     packet, attended = lax.optimization_barrier((packet, attended))
     head, mr_mix, square = mix(
-        packet, own, z0, se_square, taps, heads, mr_short, se_short, se_filter
+        packet, own, z0, se_square, taps, heads, mr_taps, se_taps, filter_taps
     )
     se_out, mr_out = normalize(of_panels(square), (se_mix, mr_mix), head)
     value_before, se_out, mr_out = lax.optimization_barrier((value_before, se_out, mr_out))

time: 48.5 us -> 48.3 us (level)
  Pallas kernels: 27.1 us -> 28.2 us
  waiting for transfers between devices: 6.4 us -> 5.38 us
    pallas_call x1, Pallas kernels: 12.6 us -> 13.6 us  [own_part(): pl.pallas_call(functools.partial(own_kernel, per), out_shape=(mixed, mixe...]
    ppermute x3, waiting for transfers between devices: 4.48 us -> 3.46 us  [from_behind(): lax.ppermute(value, 'ctx', [(source, source + 1) for source in range(coun...]
  transfers between devices with their start and end apart: 5 -> 5, of which waited for: 4 -> 4; matrix products, arithmetic and copies ran while one was open for 0% -> 0% of each run, Pallas kernels for 53% -> 56%
where the time goes in v8:
time: 48.3 us; the launch traced here: 48.1 us
  Pallas kernels  28.2 us (58%)
  starting transfers between devices  13.7 us (28%)
  waiting for transfers between devices  5.38 us (11%)
  between operations  0.76 us (2%)
    pallas_call x1, Pallas kernels, own_part(): pl.pallas_call(functools.partial(own_kernel, per), out_shape=(mixed, mixe...  13.6 us
    ppermute x3, starting transfers between devices, from_behind(): lax.ppermute(value, 'ctx', [(source, source + 1) for source in range(coun...  9.36 us
    pallas_call x1, Pallas kernels, mix(): pl.pallas_call(mix_kernel, out_shape=(jax.ShapeDtypeStruct((8, channels),...  6.86 us
    ppermute x2, starting transfers between devices, of_panels(): lax.ppermute(square, 'panel', [(n, (n + shift) % count) for n in range(co...  4.36 us
    ppermute x3, waiting for transfers between devices, from_behind(): lax.ppermute(value, 'ctx', [(source, source + 1) for source in range(coun...  3.46 us
    pallas_call x1, Pallas kernels, score(): pl.pallas_call(functools.partial(score_kernel, per), out_shape=(jax.Shape...  2.83 us
    pallas_call x1, Pallas kernels, pack(): pl.pallas_call(functools.partial(pack_kernel, per), out_shape=jax.ShapeDt...  2.22 us
    pallas_call x2, Pallas kernels, normalize(): pl.pallas_call(functools.partial(normalize_kernel, count, len(squares), p...  2.19 us
  transfers between devices with their start and end apart: 5, of which 4 were waited for; matrix products, arithmetic and copies ran while one was open for 0% of the time, Pallas kernels for 56%

profile of v8, /device:TPU:9, one launch (start us, length us, event | category | flops | bytes accessed | tf_op | source)
XLA Modules:
  0.0 48.1 jit_solution(15380582012153423363)
XLA Ops:
  0.6 3.1 %collective-permute-start.2 = (bf16[144,2048]{1,0:T(8,128)(2,1)}, bf16[144,2048]{1,0:T(8,128)(2,1)S(1)}, u32[]{:S(2)}, u32[]{:S(2)}) collective-permute-start(bf16[144,2048]{1,0:T(8,128)(2,1)} %k_ref.1), channel_id=1, source_target_pairs={{0,2},{2,4},{4,6},{6,8},{8,10},{10,12},{12,14},{14,16},{16,18},{18... | collective-permute-start | bytes 1769480 | tf_op jit(solution)/shard_map/ppermute | solution.py:504
  3.8 2.2 %pack.1 = bf16[2320,128]{1,0:T(8,128)(2,1)S(1)} custom-call(bf16[3,144,2048]{2,1,0:T(8,128)(2,1)} %mr_ref.1, bf16[3,144,2048]{2,1,0:T(8,128)(2,1)} %se_ref.1, f32[3,3,2048]{2,1,0:T(4,128)} %mr_short_ref.1, f32[3,3,2048]{2,1,0:T(4,128)} %se_short_ref.1), custom_call_target="tpu_custom_call" | custom-call | flops 5898240 | bytes 1769472 | tf_op jit(solution)/shard_map/pack/pallas_call | solution.py:128
  6.0 3.1 %collective-permute-start.1 = (bf16[2320,128]{1,0:T(8,128)(2,1)S(1)}, bf16[2320,128]{1,0:T(8,128)(2,1)S(1)}, u32[]{:S(2)}, u32[]{:S(2)}) collective-permute-start(bf16[2320,128]{1,0:T(8,128)(2,1)S(1)} %pack.1), channel_id=1, source_target_pairs={{0,2},{2,4},{4,6},{6,8},{8,10},{10,12},{12,14},{14,16},{16,18},{18... | collective-permute-start | bytes 1781768 | tf_op jit(solution)/shard_map/ppermute | solution.py:504
  9.1 0.0 copy-start.2
  9.1 0.0 copy-start
  9.1 0.0 copy-start.1
  9.1 13.6 %own_part.1 = (f32[144,2048]{1,0:T(8,128)S(1)}, f32[144,2048]{1,0:T(8,128)S(1)}, f32[144,2048]{1,0:T(8,128)S(1)}, f32[144,128]{1,0:T(8,128)S(1)}, f32[128,2048]{...) custom-call(bf16[3,144,2048]{2,1,0:T(8,128)(2,1)} %mr_ref.1, ...), custom_call_target="tpu_custom_call" | custom-call | flops 53084160 | bytes 7077888 | tf_op jit(solution)/shard_map/own_part/pallas_call | solution.py:250
  22.8 0.0 copy-done.2
  22.8 3.1 %collective-permute-start = (bf16[144,2048]{1,0:T(8,128)(2,1)S(1)}, bf16[144,2048]{1,0:T(8,128)(2,1)S(1)}, u32[]{:S(2)}, u32[]{:S(2)}) collective-permute-start(bf16[144,2048]{1,0:T(8,128)(2,1)S(1)} %copy-done.2), channel_id=1, source_target_pairs={{0,2},{2,4},{4,6},{6,8},{8,10},{10,12},{12,14},{14,16},{16,18},{18... | collective-permute-start | bytes 1769480 | tf_op jit(solution)/shard_map/ppermute | solution.py:504
  25.9 0.0 collective-permute-done.2.before_ref
  25.9 0.0 copy-done
  25.9 0.0 copy-done.1
  25.9 2.8 %score.1 = (bf16[16,144,144]{2,1,0:T(8,128)(2,1)S(1)}, f32[144,2048]{1,0:T(8,128)S(1)}, f32[144,2048]{1,0:T(8,128)S(1)}) custom-call(bf16[144,2048]{1,0:T(8,128)(2,1)S(1)} %copy-done, bf16[144,2048]{1,0:T(8,128)(2,1)S(1)} %copy-done.1, bf16[144,2048]{1,0:T(8,128)(2,1)S(1)} %collective-permute-done.2.before_ref, bf16[144,2048]{1,0:T(8,128)(2,1)S(1)} %copy-done.2), custom_call_target="tpu_custom_call" | custom-call | flops 339738624 | bytes 4128768 | tf_op jit(solution)/shard_map/score/pallas_call | solution.py:409
  28.8 2.7 %collective-permute-done.1.packet_ref = bf16[2320,128]{1,0:T(8,128)(2,1)S(1)} collective-permute-done((bf16[2320,128]{1,0:T(8,128)(2,1)S(1)}, bf16[2320,128]{1,0:T(8,128)(2,1)S(1)}, u32[]{:S(2)}, u32[]{:S(2)}) %collective-permute-start.1) | collective-permute-done | bytes 593952 | tf_op jit(solution)/shard_map/ppermute | solution.py:504
  31.5 6.9 %mix.1 = (f32[8,2048]{1,0:T(8,128)S(1)}, f32[144,2048]{1,0:T(8,128)S(1)}, f32[2,144,128]{2,1,0:T(8,128)S(1)}) custom-call(bf16[2320,128]{1,0:T(8,128)(2,1)S(1)} %collective-permute-done.1.packet_ref, f32[144,2048]{1,0:T(8,128)S(1)} %get-tuple-element.33.own_ref, f32[144,2048]{1,0:T(8,128)S(1)} %get-tuple-element.34.z0_ref, ...), custom_call_target="tpu_custom_call" | custom-call | flops 41287680 | bytes 4718592 | tf_op jit(solution)/shard_map/mix/pallas_call | solution.py:355
  38.3 2.8 %collective-permute-start.3 = (f32[2,144,128]{2,1,0:T(8,128)S(1)}, f32[2,144,128]{2,1,0:T(8,128)S(1)}, u32[]{:S(2)}, u32[]{:S(2)}) collective-permute-start(f32[2,144,128]{2,1,0:T(8,128)S(1)} %get-tuple-element.41.refs_0_), channel_id=1, source_target_pairs={{0,1},{1,0},{2,3},{3,2},{4,5},{5,4},{6,7},{7,6},{8,9},{9,8},{10,11... | collective-permute-start | bytes 442376 | tf_op jit(solution)/shard_map/ppermute | solution.py:510
  41.1 1.0 %collective-permute-done.3.refs_1_ = f32[2,144,128]{2,1,0:T(8,128)S(1)} collective-permute-done((f32[2,144,128]{2,1,0:T(8,128)S(1)}, f32[2,144,128]{2,1,0:T(8,128)S(1)}, u32[]{:S(2)}, u32[]{:S(2)}) %collective-permute-start.3) | collective-permute-done | bytes 147488 | tf_op jit(solution)/shard_map/ppermute | solution.py:510
  42.1 1.2 %normalize.2 = (bf16[144,2048]{1,0:T(8,128)(2,1)}, bf16[144,2048]{1,0:T(8,128)(2,1)}) custom-call(f32[2,144,128]{2,1,0:T(8,128)S(1)} %get-tuple-element.41.refs_0_, f32[2,144,128]{2,1,0:T(8,128)S(1)} %collective-permute-done.3.refs_1_, f32[144,2048]{1,0:T(8,128)S(1)} %get-tuple-element.42.refs_2_, f32[144,2048]{1,0:T(8,128)S(1)} %get-tuple-element.43.refs_3_, ...), custom_call_target="tpu_custom_call" | custom-call | flops 2359296 | bytes 3538944 | tf_op jit(solution)/shard_map/normalize/pallas_call | solution.py:487
  43.3 0.8 %collective-permute-done.before_ref = bf16[144,2048]{1,0:T(8,128)(2,1)S(1)} collective-permute-done((bf16[144,2048]{1,0:T(8,128)(2,1)S(1)}, bf16[144,2048]{1,0:T(8,128)(2,1)S(1)}, u32[]{:S(2)}, u32[]{:S(2)}) %collective-permute-start) | collective-permute-done | bytes 589856 | tf_op jit(solution)/shard_map/ppermute | solution.py:504
  44.1 0.5 value_mix.1
  44.6 1.6 %collective-permute-start.4 = (f32[1,144,128]{2,1,0:T(8,128)S(1)}, f32[1,144,128]{2,1,0:T(8,128)S(1)}, u32[]{:S(2)}, u32[]{:S(2)}) collective-permute-start(f32[1,144,128]{2,1,0:T(8,128)S(1)} %get-tuple-element.53.refs_0_), channel_id=1, source_target_pairs={{0,1},{1,0},{2,3},{3,2},{4,5},{5,4},{6,7},{7,6},{8,9},{9,8},{10,11... | collective-permute-start | bytes 221192 | tf_op jit(solution)/shard_map/ppermute | solution.py:510
  46.2 0.9 %collective-permute-done.4.refs_1_ = f32[1,144,128]{2,1,0:T(8,128)S(1)} collective-permute-done((f32[1,144,128]{2,1,0:T(8,128)S(1)}, f32[1,144,128]{2,1,0:T(8,128)S(1)}, u32[]{:S(2)}, u32[]{:S(2)}) %collective-permute-start.4) | collective-permute-done | bytes 73760 | tf_op jit(solution)/shard_map/ppermute | solution.py:510
  47.1 1.0 %normalize.3 = bf16[144,2048]{1,0:T(8,128)(2,1)} custom-call(f32[1,144,128]{2,1,0:T(8,128)S(1)} %get-tuple-element.53.refs_0_, f32[1,144,128]{2,1,0:T(8,128)S(1)} %collective-permute-done.4.refs_1_, f32[144,2048]{1,0:T(8,128)S(1)} %get-tuple-element.54.refs_2_), custom_call_target="tpu_custom_call" | custom-call | flops 1179648 | bytes 1769472 | tf_op jit(solution)/shard_map/normalize/pallas_call | solution.py:487
Async XLA Ops:
  0.6 25.3 %collective-permute-start.2 = (bf16[144,2048]{1,0:T(8,128)(2,1)}, bf16[144,2048]{1,0:T(8,128)(2,1)S(1)}, u32[]{:S(2)}, u32[]{:S(2)}) collective-permute-start(bf16[144,2048]{1,0:T(8,128)(2,1)} %k_ref.1), channel_id=1, source_target_pairs={{0,2},{2,4},{4,6},{6,8},{8,10},{10,12},{12,14},{14,16},{16,18},{18... | collective-permute-start | bytes 1769480 | tf_op jit(solution)/shard_map/ppermute | solution.py:504
  6.0 25.5 %collective-permute-start.1 = (bf16[2320,128]{1,0:T(8,128)(2,1)S(1)}, bf16[2320,128]{1,0:T(8,128)(2,1)S(1)}, u32[]{:S(2)}, u32[]{:S(2)}) collective-permute-start(bf16[2320,128]{1,0:T(8,128)(2,1)S(1)} %pack.1), channel_id=1, source_target_pairs={{0,2},{2,4},{4,6},{6,8},{8,10},{10,12},{12,14},{14,16},{16,18},{18... | collective-permute-start | bytes 1781768 | tf_op jit(solution)/shard_map/ppermute | solution.py:504
  9.1 13.7 %copy-start.2 = (bf16[144,2048]{1,0:T(8,128)(2,1)S(1)}, bf16[144,2048]{1,0:T(8,128)(2,1)}, u32[]{:S(2)}) copy-start(bf16[144,2048]{1,0:T(8,128)(2,1)} %v_ref.1) | copy-start | bytes 1769476
  9.1 16.8 %copy-start = (bf16[144,2048]{1,0:T(8,128)(2,1)S(1)}, bf16[144,2048]{1,0:T(8,128)(2,1)}, u32[]{:S(2)}) copy-start(bf16[144,2048]{1,0:T(8,128)(2,1)} %q_ref.1) | copy-start | bytes 1769476
  9.1 16.8 %copy-start.1 = (bf16[144,2048]{1,0:T(8,128)(2,1)S(1)}, bf16[144,2048]{1,0:T(8,128)(2,1)}, u32[]{:S(2)}) copy-start(bf16[144,2048]{1,0:T(8,128)(2,1)} %k_ref.1) | copy-start | bytes 1769476
  22.8 21.3 %collective-permute-start = (bf16[144,2048]{1,0:T(8,128)(2,1)S(1)}, bf16[144,2048]{1,0:T(8,128)(2,1)S(1)}, u32[]{:S(2)}, u32[]{:S(2)}) collective-permute-start(bf16[144,2048]{1,0:T(8,128)(2,1)S(1)} %copy-done.2), channel_id=1, source_target_pairs={{0,2},{2,4},{4,6},{6,8},{8,10},{10,12},{12,14},{14,16},{16,18},{18... | collective-permute-start | bytes 1769480 | tf_op jit(solution)/shard_map/ppermute | solution.py:504
  38.3 3.8 %collective-permute-start.3 = (f32[2,144,128]{2,1,0:T(8,128)S(1)}, f32[2,144,128]{2,1,0:T(8,128)S(1)}, u32[]{:S(2)}, u32[]{:S(2)}) collective-permute-start(f32[2,144,128]{2,1,0:T(8,128)S(1)} %get-tuple-element.41.refs_0_), channel_id=1, source_target_pairs={{0,1},{1,0},{2,3},{3,2},{4,5},{5,4},{6,7},{7,6},{8,9},{9,8},{10,11... | collective-permute-start | bytes 442376 | tf_op jit(solution)/shard_map/ppermute | solution.py:510
  44.6 2.5 %collective-permute-start.4 = (f32[1,144,128]{2,1,0:T(8,128)S(1)}, f32[1,144,128]{2,1,0:T(8,128)S(1)}, u32[]{:S(2)}, u32[]{:S(2)}) collective-permute-start(f32[1,144,128]{2,1,0:T(8,128)S(1)} %get-tuple-element.53.refs_0_), channel_id=1, source_target_pairs={{0,1},{1,0},{2,3},{3,2},{4,5},{5,4},{6,7},{7,6},{8,9},{9,8},{10,11... | collective-permute-start | bytes 221192 | tf_op jit(solution)/shard_map/ppermute | solution.py:510

commit v9 on v8

--- a/solution.py
+++ b/solution.py
@@ -430,16 +430,17 @@
         )
         out_ref[:, lanes] = total
         square = square + total * total
-    square_ref[0] = square
-
-
-def value_mix(probs, before, own, inverse):
+    for n in range(square_ref.shape[0]):
+        square_ref[n] = square
+
+
+def value_mix(probs, before, own, inverse, panels):
     rows, channels = own.shape
     return pl.pallas_call(
         value_kernel,
         out_shape=(
             jax.ShapeDtypeStruct((rows, channels), F32),
-            jax.ShapeDtypeStruct((1, rows, LANES), F32),
+            jax.ShapeDtypeStruct((panels, rows, LANES), F32),
         ),
         in_specs=[in_vmem()] * 4,
         out_specs=(in_vmem(),) * 2,
@@ -449,7 +450,7 @@
     )(probs, before, own, inverse)
 
 
-def normalize_kernel(count, panels, pieces, with_head, *refs):
+def normalize_kernel(count, panels, terms, pieces, with_head, *refs):
     square_refs, refs = refs[:panels], refs[panels:]
     mixed_refs, refs = refs[:count], refs[count:]
     if with_head:
@@ -459,9 +460,7 @@
     piece = rows // pieces
     copies = []
     for n in range(count):
-        square = square_refs[0][n]
-        for ref in square_refs[1:]:
-            square = square + ref[n]
+        square = sum(ref[n + m] for ref in square_refs for m in range(terms))
         scale = lax.rsqrt(jnp.sum(square, axis=-1, keepdims=True) * (1.0 / CHANNELS) + 1e-06)
         for m in range(pieces):
             at = slice(m * piece, (m + 1) * piece)
@@ -480,12 +479,14 @@
         copy.wait()
 
 
-def normalize(squares, mixed, head=None, pieces=3):
+def normalize(squares, mixed, head=None, pieces=3, terms=1):
     rows, channels = mixed[0].shape
     count = len(mixed)
     operands = (*squares, *mixed) + (() if head is None else (head,))
     return pl.pallas_call(
-        functools.partial(normalize_kernel, count, len(squares), pieces, head is not None),
+        functools.partial(
+            normalize_kernel, count, len(squares), terms, pieces, head is not None
+        ),
         out_shape=(jax.ShapeDtypeStruct((rows, channels), BF16),) * count,
         in_specs=[in_vmem()] * len(operands),
         out_specs=(pl.BlockSpec(memory_space=pl.ANY),) * count,
@@ -528,8 +529,10 @@
     )
     se_out, mr_out = normalize(of_panels(square), (se_mix, mr_mix), head)
     value_before, se_out, mr_out = lax.optimization_barrier((value_before, se_out, mr_out))
-    attended, square = value_mix(probs, value_before, attended, inverse)
-    (attn_out,) = normalize(of_panels(square), (attended,))
+    panels = lax.axis_size("panel")
+    attended, square = value_mix(probs, value_before, attended, inverse, panels)
+    square = lax.all_to_all(square, "panel", 0, 0, tiled=True)
+    (attn_out,) = normalize([square], (attended,), terms=panels)
     return se_out, mr_out, attn_out
 
 

time: 48.3 us -> 50.8 us (1.052)
  blocking collectives: 0 us -> 5.01 us
  starting transfers between devices: 13.7 us -> 12.1 us
  waiting for transfers between devices: 5.38 us -> 4.47 us
    all_to_all x0 -> x1, blocking collectives: none -> 5.01 us  [body(): square = lax.all_to_all(square, 'panel', 0, 0, tiled=True)]
    ppermute x2 -> x1, starting transfers between devices: 4.36 us -> 2.76 us  [of_panels(): lax.ppermute(square, 'panel', [(n, (n + shift) % count) for n in range(co...]
    ppermute x2 -> x1, waiting for transfers between devices: 1.92 us -> 1.01 us  [of_panels(): lax.ppermute(square, 'panel', [(n, (n + shift) % count) for n in range(co...]
  transfers between devices with their start and end apart: 5 -> 4, of which waited for: 4 -> 3; matrix products, arithmetic and copies ran while one was open for 0% -> 0% of each run, Pallas kernels for 56% -> 53%
where the time goes in v9:
time: 50.8 us; the launch traced here: 50.6 us
  Pallas kernels  28.2 us (56%)
  starting transfers between devices  12.1 us (24%)
  blocking collectives  5.01 us (10%)
  waiting for transfers between devices  4.47 us (9%)
  between operations  0.76 us (1%)
    pallas_call x1, Pallas kernels, own_part(): pl.pallas_call(functools.partial(own_kernel, per), out_shape=(mixed, mixe...  13.6 us
    ppermute x3, starting transfers between devices, from_behind(): lax.ppermute(value, 'ctx', [(source, source + 1) for source in range(coun...  9.36 us
    pallas_call x1, Pallas kernels, mix(): pl.pallas_call(mix_kernel, out_shape=(jax.ShapeDtypeStruct((8, channels),...  6.86 us
    all_to_all x1, blocking collectives, body(): square = lax.all_to_all(square, 'panel', 0, 0, tiled=True)  5.01 us
    ppermute x3, waiting for transfers between devices, from_behind(): lax.ppermute(value, 'ctx', [(source, source + 1) for source in range(coun...  3.46 us
    pallas_call x1, Pallas kernels, score(): pl.pallas_call(functools.partial(score_kernel, per), out_shape=(jax.Shape...  2.83 us
    ppermute x1, starting transfers between devices, of_panels(): lax.ppermute(square, 'panel', [(n, (n + shift) % count) for n in range(co...  2.76 us
    pallas_call x1, Pallas kernels, pack(): pl.pallas_call(functools.partial(pack_kernel, per), out_shape=jax.ShapeDt...  2.22 us
  transfers between devices with their start and end apart: 4, of which 3 were waited for; matrix products, arithmetic and copies ran while one was open for 0% of the time, Pallas kernels for 53%

profile of v9, /device:TPU:9, one launch (start us, length us, event | category | flops | bytes accessed | tf_op | source)
XLA Modules:
  0.0 50.6 jit_solution(4558489803587581109)
XLA Ops:
  0.6 3.1 %collective-permute-start.2 = (bf16[144,2048]{1,0:T(8,128)(2,1)}, bf16[144,2048]{1,0:T(8,128)(2,1)S(1)}, u32[]{:S(2)}, u32[]{:S(2)}) collective-permute-start(bf16[144,2048]{1,0:T(8,128)(2,1)} %k_ref.1), channel_id=1, source_target_pairs={{0,2},{2,4},{4,6},{6,8},{8,10},{10,12},{12,14},{14,16},{16,18},{18... | collective-permute-start | bytes 1769480 | tf_op jit(solution)/shard_map/ppermute | solution.py:505
  3.8 2.2 %pack.1 = bf16[2320,128]{1,0:T(8,128)(2,1)S(1)} custom-call(bf16[3,144,2048]{2,1,0:T(8,128)(2,1)} %mr_ref.1, bf16[3,144,2048]{2,1,0:T(8,128)(2,1)} %se_ref.1, f32[3,3,2048]{2,1,0:T(4,128)} %mr_short_ref.1, f32[3,3,2048]{2,1,0:T(4,128)} %se_short_ref.1), custom_call_target="tpu_custom_call" | custom-call | flops 5898240 | bytes 1769472 | tf_op jit(solution)/shard_map/pack/pallas_call | solution.py:128
  6.0 3.1 %collective-permute-start.1 = (bf16[2320,128]{1,0:T(8,128)(2,1)S(1)}, bf16[2320,128]{1,0:T(8,128)(2,1)S(1)}, u32[]{:S(2)}, u32[]{:S(2)}) collective-permute-start(bf16[2320,128]{1,0:T(8,128)(2,1)S(1)} %pack.1), channel_id=1, source_target_pairs={{0,2},{2,4},{4,6},{6,8},{8,10},{10,12},{12,14},{14,16},{16,18},{18... | collective-permute-start | bytes 1781768 | tf_op jit(solution)/shard_map/ppermute | solution.py:505
  9.1 0.0 copy-start.2
  9.1 0.0 copy-start
  9.1 0.0 copy-start.1
  9.1 13.6 %own_part.1 = (f32[144,2048]{1,0:T(8,128)S(1)}, f32[144,2048]{1,0:T(8,128)S(1)}, f32[144,2048]{1,0:T(8,128)S(1)}, f32[144,128]{1,0:T(8,128)S(1)}, f32[128,2048]{...) custom-call(bf16[3,144,2048]{2,1,0:T(8,128)(2,1)} %mr_ref.1, ...), custom_call_target="tpu_custom_call" | custom-call | flops 53084160 | bytes 7077888 | tf_op jit(solution)/shard_map/own_part/pallas_call | solution.py:250
  22.8 0.0 copy-done.2
  22.8 3.1 %collective-permute-start = (bf16[144,2048]{1,0:T(8,128)(2,1)S(1)}, bf16[144,2048]{1,0:T(8,128)(2,1)S(1)}, u32[]{:S(2)}, u32[]{:S(2)}) collective-permute-start(bf16[144,2048]{1,0:T(8,128)(2,1)S(1)} %copy-done.2), channel_id=1, source_target_pairs={{0,2},{2,4},{4,6},{6,8},{8,10},{10,12},{12,14},{14,16},{16,18},{18... | collective-permute-start | bytes 1769480 | tf_op jit(solution)/shard_map/ppermute | solution.py:505
  25.9 0.0 collective-permute-done.2.before_ref
  25.9 0.0 copy-done
  25.9 0.0 copy-done.1
  25.9 2.8 %score.1 = (bf16[16,144,144]{2,1,0:T(8,128)(2,1)S(1)}, f32[144,2048]{1,0:T(8,128)S(1)}, f32[144,2048]{1,0:T(8,128)S(1)}) custom-call(bf16[144,2048]{1,0:T(8,128)(2,1)S(1)} %copy-done, bf16[144,2048]{1,0:T(8,128)(2,1)S(1)} %copy-done.1, bf16[144,2048]{1,0:T(8,128)(2,1)S(1)} %collective-permute-done.2.before_ref, bf16[144,2048]{1,0:T(8,128)(2,1)S(1)} %copy-done.2), custom_call_target="tpu_custom_call" | custom-call | flops 339738624 | bytes 4128768 | tf_op jit(solution)/shard_map/score/pallas_call | solution.py:409
  28.8 2.7 %collective-permute-done.1.packet_ref = bf16[2320,128]{1,0:T(8,128)(2,1)S(1)} collective-permute-done((bf16[2320,128]{1,0:T(8,128)(2,1)S(1)}, bf16[2320,128]{1,0:T(8,128)(2,1)S(1)}, u32[]{:S(2)}, u32[]{:S(2)}) %collective-permute-start.1) | collective-permute-done | bytes 593952 | tf_op jit(solution)/shard_map/ppermute | solution.py:505
  31.5 6.9 %mix.1 = (f32[8,2048]{1,0:T(8,128)S(1)}, f32[144,2048]{1,0:T(8,128)S(1)}, f32[2,144,128]{2,1,0:T(8,128)S(1)}) custom-call(bf16[2320,128]{1,0:T(8,128)(2,1)S(1)} %collective-permute-done.1.packet_ref, f32[144,2048]{1,0:T(8,128)S(1)} %get-tuple-element.33.own_ref, f32[144,2048]{1,0:T(8,128)S(1)} %get-tuple-element.34.z0_ref, ...), custom_call_target="tpu_custom_call" | custom-call | flops 41287680 | bytes 4718592 | tf_op jit(solution)/shard_map/mix/pallas_call | solution.py:355
  38.3 2.8 %collective-permute-start.3 = (f32[2,144,128]{2,1,0:T(8,128)S(1)}, f32[2,144,128]{2,1,0:T(8,128)S(1)}, u32[]{:S(2)}, u32[]{:S(2)}) collective-permute-start(f32[2,144,128]{2,1,0:T(8,128)S(1)} %get-tuple-element.41.refs_0_), channel_id=1, source_target_pairs={{0,1},{1,0},{2,3},{3,2},{4,5},{5,4},{6,7},{7,6},{8,9},{9,8},{10,11... | collective-permute-start | bytes 442376 | tf_op jit(solution)/shard_map/ppermute | solution.py:511
  41.1 1.0 %collective-permute-done.3.refs_1_ = f32[2,144,128]{2,1,0:T(8,128)S(1)} collective-permute-done((f32[2,144,128]{2,1,0:T(8,128)S(1)}, f32[2,144,128]{2,1,0:T(8,128)S(1)}, u32[]{:S(2)}, u32[]{:S(2)}) %collective-permute-start.3) | collective-permute-done | bytes 147488 | tf_op jit(solution)/shard_map/ppermute | solution.py:511
  42.1 1.2 %normalize.2 = (bf16[144,2048]{1,0:T(8,128)(2,1)}, bf16[144,2048]{1,0:T(8,128)(2,1)}) custom-call(f32[2,144,128]{2,1,0:T(8,128)S(1)} %get-tuple-element.41.refs_0_, f32[2,144,128]{2,1,0:T(8,128)S(1)} %collective-permute-done.3.refs_1_, f32[144,2048]{1,0:T(8,128)S(1)} %get-tuple-element.42.refs_2_, f32[144,2048]{1,0:T(8,128)S(1)} %get-tuple-element.43.refs_3_, ...), custom_call_target="tpu_custom_call" | custom-call | flops 2359296 | bytes 3538944 | tf_op jit(solution)/shard_map/normalize/pallas_call | solution.py:486
  43.3 0.8 %collective-permute-done.before_ref = bf16[144,2048]{1,0:T(8,128)(2,1)S(1)} collective-permute-done((bf16[144,2048]{1,0:T(8,128)(2,1)S(1)}, bf16[144,2048]{1,0:T(8,128)(2,1)S(1)}, u32[]{:S(2)}, u32[]{:S(2)}) %collective-permute-start) | collective-permute-done | bytes 589856 | tf_op jit(solution)/shard_map/ppermute | solution.py:505
  44.1 0.5 value_mix.1
  44.6 5.0 %all_to_all.5.refs_0_ = f32[2,144,128]{2,1,0:T(8,128)S(1)} all-to-all(f32[2,144,128]{2,1,0:T(8,128)S(1)} %get-tuple-element.53), channel_id=1, replica_groups=mesh['ctx'=16,'panel'=2] {'panel'}, dimensions={0} | all-to-all | bytes 294912 | tf_op jit(solution)/shard_map/all_to_all | solution.py:534
  49.6 1.0 %normalize.3 = bf16[144,2048]{1,0:T(8,128)(2,1)} custom-call(f32[2,144,128]{2,1,0:T(8,128)S(1)} %all_to_all.5.refs_0_, f32[144,2048]{1,0:T(8,128)S(1)} %get-tuple-element.54.refs_1_), custom_call_target="tpu_custom_call" | custom-call | flops 1179648 | bytes 1769472 | tf_op jit(solution)/shard_map/normalize/pallas_call | solution.py:486
Async XLA Ops:
  0.6 25.3 %collective-permute-start.2 = (bf16[144,2048]{1,0:T(8,128)(2,1)}, bf16[144,2048]{1,0:T(8,128)(2,1)S(1)}, u32[]{:S(2)}, u32[]{:S(2)}) collective-permute-start(bf16[144,2048]{1,0:T(8,128)(2,1)} %k_ref.1), channel_id=1, source_target_pairs={{0,2},{2,4},{4,6},{6,8},{8,10},{10,12},{12,14},{14,16},{16,18},{18... | collective-permute-start | bytes 1769480 | tf_op jit(solution)/shard_map/ppermute | solution.py:505
  6.0 25.5 %collective-permute-start.1 = (bf16[2320,128]{1,0:T(8,128)(2,1)S(1)}, bf16[2320,128]{1,0:T(8,128)(2,1)S(1)}, u32[]{:S(2)}, u32[]{:S(2)}) collective-permute-start(bf16[2320,128]{1,0:T(8,128)(2,1)S(1)} %pack.1), channel_id=1, source_target_pairs={{0,2},{2,4},{4,6},{6,8},{8,10},{10,12},{12,14},{14,16},{16,18},{18... | collective-permute-start | bytes 1781768 | tf_op jit(solution)/shard_map/ppermute | solution.py:505
  9.1 13.7 %copy-start.2 = (bf16[144,2048]{1,0:T(8,128)(2,1)S(1)}, bf16[144,2048]{1,0:T(8,128)(2,1)}, u32[]{:S(2)}) copy-start(bf16[144,2048]{1,0:T(8,128)(2,1)} %v_ref.1) | copy-start | bytes 1769476
  9.1 16.8 %copy-start = (bf16[144,2048]{1,0:T(8,128)(2,1)S(1)}, bf16[144,2048]{1,0:T(8,128)(2,1)}, u32[]{:S(2)}) copy-start(bf16[144,2048]{1,0:T(8,128)(2,1)} %q_ref.1) | copy-start | bytes 1769476
  9.1 16.8 %copy-start.1 = (bf16[144,2048]{1,0:T(8,128)(2,1)S(1)}, bf16[144,2048]{1,0:T(8,128)(2,1)}, u32[]{:S(2)}) copy-start(bf16[144,2048]{1,0:T(8,128)(2,1)} %k_ref.1) | copy-start | bytes 1769476
  22.8 21.3 %collective-permute-start = (bf16[144,2048]{1,0:T(8,128)(2,1)S(1)}, bf16[144,2048]{1,0:T(8,128)(2,1)S(1)}, u32[]{:S(2)}, u32[]{:S(2)}) collective-permute-start(bf16[144,2048]{1,0:T(8,128)(2,1)S(1)} %copy-done.2), channel_id=1, source_target_pairs={{0,2},{2,4},{4,6},{6,8},{8,10},{10,12},{12,14},{14,16},{16,18},{18... | collective-permute-start | bytes 1769480 | tf_op jit(solution)/shard_map/ppermute | solution.py:505
  38.3 3.8 %collective-permute-start.3 = (f32[2,144,128]{2,1,0:T(8,128)S(1)}, f32[2,144,128]{2,1,0:T(8,128)S(1)}, u32[]{:S(2)}, u32[]{:S(2)}) collective-permute-start(f32[2,144,128]{2,1,0:T(8,128)S(1)} %get-tuple-element.41.refs_0_), channel_id=1, source_target_pairs={{0,1},{1,0},{2,3},{3,2},{4,5},{5,4},{6,7},{7,6},{8,9},{9,8},{10,11... | collective-permute-start | bytes 442376 | tf_op jit(solution)/shard_map/ppermute | solution.py:511

commit v10 on v7

--- a/solution.py
+++ b/solution.py
@@ -59,7 +59,26 @@
 
 
 def pack_kernel(
-    per, mr_ref, se_ref, mr_short_ref, se_short_ref, out_ref, m_ref, tail_ref, mw_ref, sw_ref, last_ref, sems
+    per,
+    mr_ref,
+    se_ref,
+    mr_short_ref,
+    se_short_ref,
+    decay_hbm_ref,
+    filter_hbm_ref,
+    values_ref,
+    out_ref,
+    mw_ref,
+    sw_ref,
+    decay_ref,
+    filter_ref,
+    most_ref,
+    rest_ref,
+    m_ref,
+    tail_ref,
+    last_ref,
+    sems,
+    late_sems,
 ):
     _, rows, channels = mr_ref.shape
     width = per * LANES
@@ -80,7 +99,16 @@
                 mr_ref.at[pl.ds(1, 2), :, at], m_ref.at[:, :, at], sems.at[first + n]
             )
         )
-    for copy in copies:
+    most = most_ref.shape[1]
+    late = [
+        pltpu.make_async_copy(values_ref.at[:, pl.ds(0, most)], most_ref, late_sems.at[0]),
+        pltpu.make_async_copy(
+            values_ref.at[:, pl.ds(most, channels - most)], rest_ref, late_sems.at[1]
+        ),
+        pltpu.make_async_copy(decay_hbm_ref, decay_ref, late_sems.at[2]),
+        pltpu.make_async_copy(filter_hbm_ref, filter_ref, late_sems.at[3]),
+    ]
+    for copy in copies + late:
         copy.start()
     for copy in copies[:first]:
         copy.wait()
@@ -119,38 +147,49 @@
         pl.loop(n * per, (n + 1) * per)(one)
 
     out_ref[out_ref.shape[0] - 16 :, :] = last_ref[...].astype(BF16)
-
-
-def pack(se, mr, se_short, mr_short, per):
+    for copy in late:
+        copy.wait()
+
+
+def pack(se, mr, se_short, mr_short, decay, se_filter, values, last_heads, per):
     _, rows, channels = se.shape
     blocks = channels // LANES
     total = blocks * (MEDIUM_TAPS + 16) + 16
+    rest = last_heads * HD
+    operands = (mr, se, mr_short, se_short, decay, se_filter, values)
     return pl.pallas_call(
         functools.partial(pack_kernel, per),
-        out_shape=jax.ShapeDtypeStruct((total, LANES), BF16),
-        in_specs=[pl.BlockSpec(memory_space=pltpu.HBM)] * 4,
-        out_specs=in_vmem(),
+        out_shape=(
+            jax.ShapeDtypeStruct((total, LANES), BF16),
+            jax.ShapeDtypeStruct(mr_short.shape, F32),
+            jax.ShapeDtypeStruct(se_short.shape, F32),
+            jax.ShapeDtypeStruct(decay.shape, F32),
+            jax.ShapeDtypeStruct(se_filter.shape, F32),
+            jax.ShapeDtypeStruct((rows, channels - rest), BF16),
+            jax.ShapeDtypeStruct((rows, rest), BF16),
+        ),
+        in_specs=[pl.BlockSpec(memory_space=pltpu.HBM)] * 7,
+        out_specs=(in_vmem(),) * 7,
         scratch_shapes=[
             pltpu.VMEM((2, rows, channels), BF16),
             pltpu.VMEM((4, 16, channels), BF16),
-            pltpu.VMEM(mr_short.shape, F32),
-            pltpu.VMEM(se_short.shape, F32),
             pltpu.VMEM((16, LANES), F32),
             pltpu.SemaphoreType.DMA((4 + blocks // per,)),
+            pltpu.SemaphoreType.DMA((4,)),
         ],
         compiler_params=params(),
-        cost_estimate=cost(20 * rows * channels, 6 * rows * channels),
+        cost_estimate=cost(20 * rows * channels, 10 * rows * channels),
         name="pack",
-    )(*(pltpu.with_memory_space_constraint(x, pltpu.HBM) for x in (mr, se, mr_short, se_short)))
+    )(*(pltpu.with_memory_space_constraint(x, pltpu.HBM) for x in operands))
 
 
 def own_kernel(
     per,
     m_hbm_ref,
     s_hbm_ref,
+    raw_hbm_ref,
     mw_ref,
     sw_ref,
-    raw_hbm_ref,
     decay_ref,
     filter_ref,
     own_ref,
@@ -232,7 +271,6 @@
     _, rows, channels = mr.shape
     mixed = jax.ShapeDtypeStruct((rows, channels), F32)
     mr, se, raw = (pltpu.with_memory_space_constraint(x, pltpu.HBM) for x in (mr, se, raw))
-    in_hbm = pl.BlockSpec(memory_space=pltpu.HBM)
     return pl.pallas_call(
         functools.partial(own_kernel, per),
         out_shape=(
@@ -243,7 +281,7 @@
             jax.ShapeDtypeStruct((MEDIUM_TAPS, channels), F32),
             jax.ShapeDtypeStruct((6, 8, channels), F32),
         ),
-        in_specs=[in_hbm] * 2 + [in_vmem()] * 2 + [in_hbm] + [in_vmem()] * 2,
+        in_specs=[pl.BlockSpec(memory_space=pltpu.HBM)] * 3 + [in_vmem()] * 4,
         out_specs=(in_vmem(),) * 6,
         scratch_shapes=[
             pltpu.VMEM(mr.shape, BF16),
@@ -255,7 +293,7 @@
         compiler_params=params(10),
         cost_estimate=cost(180 * rows * channels, 24 * rows * channels),
         name="own_part",
-    )(mr, se, mr_short, se_short, raw, decay, se_filter)
+    )(mr, se, raw, mr_short, se_short, decay, se_filter)
 
 
 def mix_kernel(
@@ -344,17 +382,20 @@
         out_specs=(in_vmem(),) * 3,
         scratch_shapes=[pltpu.VMEM((16, LANES), F32), pltpu.VMEM((MEDIUM_TAPS, LANES), F32)],
         compiler_params=params(),
-        cost_estimate=cost(140 * rows * channels, 16 * rows * channels),
+        cost_estimate=cost(1, 1),
         name="mix",
     )(packet, own, z0, se_square, taps, heads, mr_short, se_short, se_filter)
 
 
-def score_kernel(per, q_ref, k_ref, before_ref, v_ref, probs_ref, out_ref, inverse_ref, bias_ref):
+def score_kernel(
+    per, q_ref, k_ref, before_ref, v_ref, probs_ref, out_ref, inverse_ref, square_ref, bias_ref
+):
     rows, channels = q_ref.shape
     at = lax.broadcasted_iota(jnp.int32, (rows, 2 * rows), 0)
     key = lax.broadcasted_iota(jnp.int32, (rows, 2 * rows), 1)
     valid = (key <= at + rows) & ((key >= rows) | (lax.axis_index("ctx") > 0))
     bias_ref[...] = jnp.where(valid, 0.0, -1e30)
+    square_ref[...] = jnp.zeros_like(square_ref)
     factor = math.log2(math.e) / math.sqrt(HD)
     zeros, ones = jnp.zeros((rows, LANES), BF16), jnp.ones((rows, LANES), BF16)
 
@@ -389,9 +430,14 @@
     flat = jax.ShapeDtypeStruct((rows, channels), F32)
     return pl.pallas_call(
         functools.partial(score_kernel, per),
-        out_shape=(jax.ShapeDtypeStruct((channels // HD, rows, rows), BF16), flat, flat),
+        out_shape=(
+            jax.ShapeDtypeStruct((channels // HD, rows, rows), BF16),
+            flat,
+            flat,
+            jax.ShapeDtypeStruct((1, rows, LANES), F32),
+        ),
         in_specs=[in_vmem()] * 4,
-        out_specs=(in_vmem(),) * 3,
+        out_specs=(in_vmem(),) * 4,
         scratch_shapes=[pltpu.VMEM((rows, 2 * rows), F32)],
         compiler_params=params(),
         cost_estimate=cost(
@@ -401,33 +447,35 @@
     )(queries, keys, before, values)
 
 
-def value_kernel(probs_ref, before_ref, own_ref, inverse_ref, out_ref, square_ref):
-    rows, channels = own_ref.shape
-    square = jnp.zeros((rows, LANES), F32)
-    for k in range(channels // LANES):
-        lanes = slice(k * LANES, (k + 1) * LANES)
+def value_kernel(first, probs_ref, before_ref, own_ref, inverse_ref, square_in_ref, out_ref, square_ref):
+    square = square_in_ref[0]
+    for k in range(before_ref.shape[1] // LANES):
+        lanes = slice((first + k) * LANES, (first + k + 1) * LANES)
         total = own_ref[:, lanes] + inverse_ref[:, lanes] * jnp.dot(
-            probs_ref[k], before_ref[:, lanes], preferred_element_type=F32
+            probs_ref[first + k],
+            before_ref[:, k * LANES : (k + 1) * LANES],
+            preferred_element_type=F32,
         )
         out_ref[:, lanes] = total
         square = square + total * total
     square_ref[0] = square
 
 
-def value_mix(probs, before, own, inverse):
-    rows, channels = own.shape
+def value_mix(first, probs, before, own, inverse, square):
+    rows, channels = before.shape
     return pl.pallas_call(
-        value_kernel,
+        functools.partial(value_kernel, first),
         out_shape=(
-            jax.ShapeDtypeStruct((rows, channels), F32),
+            jax.ShapeDtypeStruct(own.shape, F32),
             jax.ShapeDtypeStruct((1, rows, LANES), F32),
         ),
-        in_specs=[in_vmem()] * 4,
+        in_specs=[in_vmem()] * 5,
         out_specs=(in_vmem(),) * 2,
+        input_output_aliases={2: 0},
         compiler_params=params(),
-        cost_estimate=cost(2 * rows * rows * channels, 12 * rows * channels),
+        cost_estimate=cost(1, 1),
         name="value_mix",
-    )(probs, before, own, inverse)
+    )(probs, before, own, inverse, square)
 
 
 def normalize_kernel(count, panels, pieces, with_head, *refs):
@@ -475,7 +523,7 @@
             pltpu.SemaphoreType.DMA((count, pieces)),
         ],
         compiler_params=params(),
-        cost_estimate=cost(4 * count * rows * channels, 6 * count * rows * channels),
+        cost_estimate=cost(1, 1),
         name="normalize",
     )(*operands)
 
@@ -494,22 +542,30 @@
 
 
 def body(se, se_short, se_filter, mr, mr_short, raw, decay, queries, keys, values):
-    decay = decay[None, :]
+    last_heads = 3 * (queries.shape[1] // HD) // 8
     key_before = from_behind(keys)
-    packet = from_behind(pack(se, mr, se_short, mr_short, 4))
+    packet, mr_taps, se_taps, decay, filter_taps, most, rest = pack(
+        se, mr, se_short, mr_short, decay[None, :], se_filter, values, last_heads, 4
+    )
+    packet = from_behind(packet)
     own, z0, se_mix, se_square, taps, heads = own_part(
-        mr, se, mr_short, se_short, raw, decay, se_filter, 4
+        mr, se, mr_taps, se_taps, raw, decay, filter_taps, 4
     )
-    values_later, own = lax.optimization_barrier((values, own))
-    value_before = from_behind(values_later)
-    probs, attended, inverse = score(queries, keys, key_before, values, 4)
+    most, own = lax.optimization_barrier((most, own))
+    most_before = from_behind(most)
+    probs, attended, inverse, square = score(queries, keys, key_before, values, 4)
+    rest, attended = lax.optimization_barrier((rest, attended))
+    rest_before = from_behind(rest)
     packet, attended = lax.optimization_barrier((packet, attended))
-    head, mr_mix, square = mix(
-        packet, own, z0, se_square, taps, heads, mr_short, se_short, se_filter
+    head, mr_mix, mixed_square = mix(
+        packet, own, z0, se_square, taps, heads, mr_taps, se_taps, filter_taps
     )
-    se_out, mr_out = normalize(of_panels(square), (se_mix, mr_mix), head)
-    value_before, se_out, mr_out = lax.optimization_barrier((value_before, se_out, mr_out))
-    attended, square = value_mix(probs, value_before, attended, inverse)
+    se_out, mr_out = normalize(of_panels(mixed_square), (se_mix, mr_mix), head)
+    most_before, se_out, mr_out = lax.optimization_barrier((most_before, se_out, mr_out))
+    attended, square = value_mix(0, probs, most_before, attended, inverse, square)
+    rest_before, attended = lax.optimization_barrier((rest_before, attended))
+    first = most.shape[1] // HD
+    attended, square = value_mix(first, probs, rest_before, attended, inverse, square)
     (attn_out,) = normalize(of_panels(square), (attended,))
     return se_out, mr_out, attn_out
 

time: 48.5 us -> 48.1 us (level)
  waiting for transfers between devices: 6.4 us -> 2.86 us
  starting transfers between devices: 13.9 us -> 16.8 us
    ppermute x3 -> x4, waiting for transfers between devices: 4.48 us -> 0.94 us  [from_behind(): lax.ppermute(value, 'ctx', [(source, source + 1) for source in range(coun...]
    ppermute x3 -> x4, starting transfers between devices: 9.49 us -> 12.5 us  [from_behind(): lax.ppermute(value, 'ctx', [(source, source + 1) for source in range(coun...]
    pallas_call x2 -> x3, Pallas kernels: 2.68 us -> 2.94 us  [the longest x1 2.26 us: pack(): pl.pallas_call(functools.partial(pack_kernel, per), out_shape=(jax.ShapeD...]
  transfers between devices with their start and end apart: 5 -> 6, of which waited for: 4 -> 4; matrix products, arithmetic and copies ran while one was open for 0% -> 0% of each run, Pallas kernels for 53% -> 55%
where the time goes in v10:
time: 48.1 us; the launch traced here: 47.9 us
  Pallas kernels  27.4 us (57%)
  starting transfers between devices  16.8 us (35%)
  waiting for transfers between devices  2.86 us (6%)
  between operations  0.78 us (2%)
    pallas_call x1, Pallas kernels, own_part(): pl.pallas_call(functools.partial(own_kernel, per), out_shape=(mixed, mixe...  12.6 us
    ppermute x4, starting transfers between devices, from_behind(): lax.ppermute(value, 'ctx', [(source, source + 1) for source in range(coun...  12.5 us
    pallas_call x1, Pallas kernels, mix(): pl.pallas_call(mix_kernel, out_shape=(jax.ShapeDtypeStruct((8, channels),...  6.86 us
    ppermute x2, starting transfers between devices, of_panels(): lax.ppermute(square, 'panel', [(n, (n + shift) % count) for n in range(co...  4.36 us
    pallas_call x1, Pallas kernels, score(): pl.pallas_call(functools.partial(score_kernel, per), out_shape=(jax.Shape...  2.84 us
    pallas_call x1, Pallas kernels, pack(): pl.pallas_call(functools.partial(pack_kernel, per), out_shape=(jax.ShapeD...  2.26 us
    pallas_call x2, Pallas kernels, normalize(): pl.pallas_call(functools.partial(normalize_kernel, count, len(squares), p...  2.19 us
    ppermute x2, waiting for transfers between devices, of_panels(): lax.ppermute(square, 'panel', [(n, (n + shift) % count) for n in range(co...  1.92 us
  transfers between devices with their start and end apart: 6, of which 4 were waited for; matrix products, arithmetic and copies ran while one was open for 0% of the time, Pallas kernels for 55%

profile of v10, /device:TPU:9, one launch (start us, length us, event | category | flops | bytes accessed | tf_op | source)
XLA Modules:
  0.0 47.9 jit_solution(8970781823672605604)
XLA Ops:
  0.6 3.1 %collective-permute-start.2 = (bf16[144,2048]{1,0:T(8,128)(2,1)}, bf16[144,2048]{1,0:T(8,128)(2,1)S(1)}, u32[]{:S(2)}, u32[]{:S(2)}) collective-permute-start(bf16[144,2048]{1,0:T(8,128)(2,1)} %k_ref.1), channel_id=1, source_target_pairs={{0,2},{2,4},{4,6},{6,8},{8,10},{10,12},{12,14},{14,16},{16,18},{18... | collective-permute-start | bytes 1769480 | tf_op jit(solution)/shard_map/ppermute | solution.py:533
  3.8 2.3 %pack.1 = (bf16[2320,128]{1,0:T(8,128)(2,1)S(1)}, f32[3,3,2048]{2,1,0:T(4,128)S(1)}, f32[3,3,2048]{2,1,0:T(4,128)S(1)}, f32[1,2048]{1,0:T(1,128)S(1)}, f32[7,204...) custom-call(bf16[3,144,2048]{2,1,0:T(8,128)(2,1)} %m_hbm_ref.1, ...), custom_call_target="tpu_custom_call" | custom-call | flops 5898240 | bytes 2949120 | tf_op jit(solution)/shard_map/pack/pallas_call | solution.py:160
  6.0 3.1 %collective-permute-start.1 = (bf16[2320,128]{1,0:T(8,128)(2,1)S(1)}, bf16[2320,128]{1,0:T(8,128)(2,1)S(1)}, u32[]{:S(2)}, u32[]{:S(2)}) collective-permute-start(bf16[2320,128]{1,0:T(8,128)(2,1)S(1)} %get-tuple-element.47), channel_id=1, source_target_pairs={{0,2},{2,4},{4,6},{6,8},{8,10},{10,12},{12,14},{14,16},{16,18},{18... | collective-permute-start | bytes 1781768 | tf_op jit(solution)/shard_map/ppermute | solution.py:533
  9.2 0.0 copy-start
  9.2 0.0 copy-start.1
  9.2 0.0 copy-start.2
  9.2 12.6 %own_part.1 = (f32[144,2048]{1,0:T(8,128)S(1)}, f32[144,2048]{1,0:T(8,128)S(1)}, f32[144,2048]{1,0:T(8,128)S(1)}, f32[144,128]{1,0:T(8,128)S(1)}, f32[128,2048]{1,0:T(8,128)S(1)}, /*index=5*/f32[6,8,2048]{2,1,0:T(8,128)S(1)}) custom-call(bf16[3,144,2048]{2,1,0:T(8,128)(2,1)} %m_hbm_ref.1, bf16[3,144,2048]{2,1,0:T(8,128)(2,1)} %s_hbm_ref.1, ...), custom_call_target="tpu_custom_call" | custom-call | flops 53084160 | bytes 7077888 | tf_op jit(solution)/shard_map/own_part/pallas_call | solution.py:274
  21.8 3.1 %collective-permute-start = (bf16[144,1280]{1,0:T(8,128)(2,1)S(1)}, bf16[144,1280]{1,0:T(8,128)(2,1)S(1)}, u32[]{:S(2)}, u32[]{:S(2)}) collective-permute-start(bf16[144,1280]{1,0:T(8,128)(2,1)S(1)} %get-tuple-element.46), channel_id=1, source_target_pairs={{0,2},{2,4},{4,6},{6,8},{8,10},{10,12},{12,14},{14,16},{16,18},{18... | collective-permute-start | bytes 1105928 | tf_op jit(solution)/shard_map/ppermute | solution.py:533
  24.9 0.0 collective-permute-done.2.before_ref
  24.9 0.0 copy-done
  24.9 0.0 copy-done.1
  24.9 0.0 copy-done.2
  24.9 2.8 %score.1 = (bf16[16,144,144]{2,1,0:T(8,128)(2,1)S(1)}, f32[144,2048]{1,0:T(8,128)S(1)}, f32[144,2048]{1,0:T(8,128)S(1)}, f32[1,144,128]{2,1,0:T(8,128)S(1)}) custom-call(bf16[144,2048]{1,0:T(8,128)(2,1)S(1)} %copy-done.1, bf16[144,2048]{1,0:T(8,128)(2,1)S(1)} %copy-done.2, bf16[144,2048]{1,0:T(8,128)(2,1)S(1)} %collective-permute-done.2.before_ref, ...), custom_call_target="tpu_custom_call" | custom-call | flops 339738624 | bytes 4128768 | tf_op jit(solution)/shard_map/score/pallas_call | solution.py:431
  27.8 3.1 %collective-permute-start.4 = (bf16[144,768]{1,0:T(8,128)(2,1)S(1)}, bf16[144,768]{1,0:T(8,128)(2,1)S(1)}, u32[]{:S(2)}, u32[]{:S(2)}) collective-permute-start(bf16[144,768]{1,0:T(8,128)(2,1)S(1)} %get-tuple-element.66), channel_id=1, source_target_pairs={{0,2},{2,4},{4,6},{6,8},{8,10},{10,12},{12,14},{14,16},{16,18},{18... | collective-permute-start | bytes 663560 | tf_op jit(solution)/shard_map/ppermute | solution.py:533
  30.9 0.6 %collective-permute-done.1.packet_ref = bf16[2320,128]{1,0:T(8,128)(2,1)S(1)} collective-permute-done((bf16[2320,128]{1,0:T(8,128)(2,1)S(1)}, bf16[2320,128]{1,0:T(8,128)(2,1)S(1)}, u32[]{:S(2)}, u32[]{:S(2)}) %collective-permute-start.1) | collective-permute-done | bytes 593952 | tf_op jit(solution)/shard_map/ppermute | solution.py:533
  31.5 6.9 %mix.1 = (f32[8,2048]{1,0:T(8,128)S(1)}, f32[144,2048]{1,0:T(8,128)S(1)}, f32[2,144,128]{2,1,0:T(8,128)S(1)}) custom-call(bf16[2320,128]{1,0:T(8,128)(2,1)S(1)} %collective-permute-done.1.packet_ref, f32[144,2048]{1,0:T(8,128)S(1)} %get-tuple-element.52.own_ref, f32[144,2048]{1,0:T(8,128)S(1)} %get-tuple-element.53.z0_ref, ...), custom_call_target="tpu_custom_call" | custom-call | flops 1 | bytes 1 | tf_op jit(solution)/shard_map/mix/pallas_call | solution.py:374
  38.3 2.8 %collective-permute-start.3 = (f32[2,144,128]{2,1,0:T(8,128)S(1)}, f32[2,144,128]{2,1,0:T(8,128)S(1)}, u32[]{:S(2)}, u32[]{:S(2)}) collective-permute-start(f32[2,144,128]{2,1,0:T(8,128)S(1)} %get-tuple-element.57.refs_0_), channel_id=1, source_target_pairs={{0,1},{1,0},{2,3},{3,2},{4,5},{5,4},{6,7},{7,6},{8,9},{9,8},{10,11... | collective-permute-start | bytes 442376 | tf_op jit(solution)/shard_map/ppermute | solution.py:539
  41.1 1.0 %collective-permute-done.3.refs_1_ = f32[2,144,128]{2,1,0:T(8,128)S(1)} collective-permute-done((f32[2,144,128]{2,1,0:T(8,128)S(1)}, f32[2,144,128]{2,1,0:T(8,128)S(1)}, u32[]{:S(2)}, u32[]{:S(2)}) %collective-permute-start.3) | collective-permute-done | bytes 147488 | tf_op jit(solution)/shard_map/ppermute | solution.py:539
  42.1 1.2 %normalize.2 = (bf16[144,2048]{1,0:T(8,128)(2,1)}, bf16[144,2048]{1,0:T(8,128)(2,1)}) custom-call(f32[2,144,128]{2,1,0:T(8,128)S(1)} %get-tuple-element.57.refs_0_, f32[2,144,128]{2,1,0:T(8,128)S(1)} %collective-permute-done.3.refs_1_, f32[144,2048]{1,0:T(8,128)S(1)} %get-tuple-element.58.refs_2_, f32[144,2048]{1,0:T(8,128)S(1)} %get-tuple-element.59.refs_3_, ...), custom_call_target="tpu_custom_call" | custom-call | flops 1 | bytes 1 | tf_op jit(solution)/shard_map/normalize/pallas_call | solution.py:516
  43.3 0.0 collective-permute-done.before_ref
  43.3 0.4 value_mix.2
  43.7 0.4 collective-permute-done.4.before_ref
  44.1 0.3 value_mix.3
  44.4 1.6 %collective-permute-start.5 = (f32[1,144,128]{2,1,0:T(8,128)S(1)}, f32[1,144,128]{2,1,0:T(8,128)S(1)}, u32[]{:S(2)}, u32[]{:S(2)}) collective-permute-start(f32[1,144,128]{2,1,0:T(8,128)S(1)} %get-tuple-element.75.refs_0_), channel_id=1, source_target_pairs={{0,1},{1,0},{2,3},{3,2},{4,5},{5,4},{6,7},{7,6},{8,9},{9,8},{10,11... | collective-permute-start | bytes 221192 | tf_op jit(solution)/shard_map/ppermute | solution.py:539
  46.0 0.9 %collective-permute-done.5.refs_1_ = f32[1,144,128]{2,1,0:T(8,128)S(1)} collective-permute-done((f32[1,144,128]{2,1,0:T(8,128)S(1)}, f32[1,144,128]{2,1,0:T(8,128)S(1)}, u32[]{:S(2)}, u32[]{:S(2)}) %collective-permute-start.5) | collective-permute-done | bytes 73760 | tf_op jit(solution)/shard_map/ppermute | solution.py:539
  46.9 1.0 %normalize.3 = bf16[144,2048]{1,0:T(8,128)(2,1)} custom-call(f32[1,144,128]{2,1,0:T(8,128)S(1)} %get-tuple-element.75.refs_0_, f32[1,144,128]{2,1,0:T(8,128)S(1)} %collective-permute-done.5.refs_1_, f32[144,2048]{1,0:T(8,128)S(1)} %get-tuple-element.76.refs_2_), custom_call_target="tpu_custom_call" | custom-call | flops 1 | bytes 1 | tf_op jit(solution)/shard_map/normalize/pallas_call | solution.py:516
Async XLA Ops:
  0.6 24.3 %collective-permute-start.2 = (bf16[144,2048]{1,0:T(8,128)(2,1)}, bf16[144,2048]{1,0:T(8,128)(2,1)S(1)}, u32[]{:S(2)}, u32[]{:S(2)}) collective-permute-start(bf16[144,2048]{1,0:T(8,128)(2,1)} %k_ref.1), channel_id=1, source_target_pairs={{0,2},{2,4},{4,6},{6,8},{8,10},{10,12},{12,14},{14,16},{16,18},{18... | collective-permute-start | bytes 1769480 | tf_op jit(solution)/shard_map/ppermute | solution.py:533
  6.0 25.4 %collective-permute-start.1 = (bf16[2320,128]{1,0:T(8,128)(2,1)S(1)}, bf16[2320,128]{1,0:T(8,128)(2,1)S(1)}, u32[]{:S(2)}, u32[]{:S(2)}) collective-permute-start(bf16[2320,128]{1,0:T(8,128)(2,1)S(1)} %get-tuple-element.47), channel_id=1, source_target_pairs={{0,2},{2,4},{4,6},{6,8},{8,10},{10,12},{12,14},{14,16},{16,18},{18... | collective-permute-start | bytes 1781768 | tf_op jit(solution)/shard_map/ppermute | solution.py:533
  9.2 15.8 %copy-start = (bf16[144,2048]{1,0:T(8,128)(2,1)S(1)}, bf16[144,2048]{1,0:T(8,128)(2,1)}, u32[]{:S(2)}) copy-start(bf16[144,2048]{1,0:T(8,128)(2,1)} %v_ref.1) | copy-start | bytes 1769476
  9.2 15.8 %copy-start.1 = (bf16[144,2048]{1,0:T(8,128)(2,1)S(1)}, bf16[144,2048]{1,0:T(8,128)(2,1)}, u32[]{:S(2)}) copy-start(bf16[144,2048]{1,0:T(8,128)(2,1)} %q_ref.1) | copy-start | bytes 1769476
  9.2 15.7 %copy-start.2 = (bf16[144,2048]{1,0:T(8,128)(2,1)S(1)}, bf16[144,2048]{1,0:T(8,128)(2,1)}, u32[]{:S(2)}) copy-start(bf16[144,2048]{1,0:T(8,128)(2,1)} %k_ref.1) | copy-start | bytes 1769476
  21.8 21.5 %collective-permute-start = (bf16[144,1280]{1,0:T(8,128)(2,1)S(1)}, bf16[144,1280]{1,0:T(8,128)(2,1)S(1)}, u32[]{:S(2)}, u32[]{:S(2)}) collective-permute-start(bf16[144,1280]{1,0:T(8,128)(2,1)S(1)} %get-tuple-element.46), channel_id=1, source_target_pairs={{0,2},{2,4},{4,6},{6,8},{8,10},{10,12},{12,14},{14,16},{16,18},{18... | collective-permute-start | bytes 1105928 | tf_op jit(solution)/shard_map/ppermute | solution.py:533
  27.8 16.3 %collective-permute-start.4 = (bf16[144,768]{1,0:T(8,128)(2,1)S(1)}, bf16[144,768]{1,0:T(8,128)(2,1)S(1)}, u32[]{:S(2)}, u32[]{:S(2)}) collective-permute-start(bf16[144,768]{1,0:T(8,128)(2,1)S(1)} %get-tuple-element.66), channel_id=1, source_target_pairs={{0,2},{2,4},{4,6},{6,8},{8,10},{10,12},{12,14},{14,16},{16,18},{18... | collective-permute-start | bytes 663560 | tf_op jit(solution)/shard_map/ppermute | solution.py:533
  38.3 3.8 %collective-permute-start.3 = (f32[2,144,128]{2,1,0:T(8,128)S(1)}, f32[2,144,128]{2,1,0:T(8,128)S(1)}, u32[]{:S(2)}, u32[]{:S(2)}) collective-permute-start(f32[2,144,128]{2,1,0:T(8,128)S(1)} %get-tuple-element.57.refs_0_), channel_id=1, source_target_pairs={{0,1},{1,0},{2,3},{3,2},{4,5},{5,4},{6,7},{7,6},{8,9},{9,8},{10,11... | collective-permute-start | bytes 442376 | tf_op jit(solution)/shard_map/ppermute | solution.py:539
  44.4 2.5 %collective-permute-start.5 = (f32[1,144,128]{2,1,0:T(8,128)S(1)}, f32[1,144,128]{2,1,0:T(8,128)S(1)}, u32[]{:S(2)}, u32[]{:S(2)}) collective-permute-start(f32[1,144,128]{2,1,0:T(8,128)S(1)} %get-tuple-element.75.refs_0_), channel_id=1, source_target_pairs={{0,1},{1,0},{2,3},{3,2},{4,5},{5,4},{6,7},{7,6},{8,9},{9,8},{10,11... | collective-permute-start | bytes 221192 | tf_op jit(solution)/shard_map/ppermute | solution.py:539

commit v11 on v10

--- a/solution.py
+++ b/solution.py
@@ -478,49 +478,50 @@
     )(probs, before, own, inverse, square)
 
 
-def normalize_kernel(count, panels, pieces, with_head, *refs):
+def normalize_kernel(count, panels, with_head, *refs):
     square_refs, refs = refs[:panels], refs[panels:]
     mixed_refs, refs = refs[:count], refs[count:]
     if with_head:
         head_ref, refs = refs[0], refs[1:]
     out_refs, (held_ref, sems) = refs[:count], refs[count:]
-    rows = mixed_refs[0].shape[0]
-    piece = rows // pieces
-    copies = []
+    pieces = mixed_refs[0].shape[0] // 16
+
+    def write(n, m):
+        at = pl.ds(pl.multiple_of(m * 16, 16), 16)
+        return pltpu.make_async_copy(held_ref.at[n, at], out_refs[n].at[at], sems.at[n, m])
+
     for n in range(count):
-        square = square_refs[0][n]
-        for ref in square_refs[1:]:
-            square = square + ref[n]
-        scale = lax.rsqrt(jnp.sum(square, axis=-1, keepdims=True) * (1.0 / CHANNELS) + 1e-06)
+
+        @pl.loop(0, pieces)
+        def _(m):
+            at = pl.ds(pl.multiple_of(m * 16, 16), 16)
+            square = square_refs[0][n, at, :]
+            for ref in square_refs[1:]:
+                square = square + ref[n, at, :]
+            scale = lax.rsqrt(jnp.sum(square, axis=-1, keepdims=True) * (1.0 / CHANNELS) + 1e-06)
+            value = mixed_refs[n][at, :]
+            if with_head and n == 0:
+                value = jnp.where(m == 0, jnp.concatenate([head_ref[...], value[8:]], axis=0), value)
+            held_ref[n, at, :] = (value * scale).astype(BF16)
+            write(n, m).start()
+
+    for n in range(count):
         for m in range(pieces):
-            at = slice(m * piece, (m + 1) * piece)
-            value = mixed_refs[n][at, :]
-            if with_head and n == 0 and m == 0:
-                value = jnp.concatenate([head_ref[...], value[8:]], axis=0)
-            held_ref[n, at, :] = (value * scale[at]).astype(BF16)
-            copy = pltpu.make_async_copy(
-                held_ref.at[n, pl.ds(m * piece, piece)],
-                out_refs[n].at[pl.ds(m * piece, piece)],
-                sems.at[n, m],
-            )
-            copy.start()
-            copies.append(copy)
-    for copy in copies:
-        copy.wait()
-
-
-def normalize(squares, mixed, head=None, pieces=3):
+            write(n, m).wait()
+
+
+def normalize(squares, mixed, head=None):
     rows, channels = mixed[0].shape
     count = len(mixed)
     operands = (*squares, *mixed) + (() if head is None else (head,))
     return pl.pallas_call(
-        functools.partial(normalize_kernel, count, len(squares), pieces, head is not None),
+        functools.partial(normalize_kernel, count, len(squares), head is not None),
         out_shape=(jax.ShapeDtypeStruct((rows, channels), BF16),) * count,
         in_specs=[in_vmem()] * len(operands),
         out_specs=(pl.BlockSpec(memory_space=pl.ANY),) * count,
         scratch_shapes=[
             pltpu.VMEM((count, rows, channels), BF16),
-            pltpu.SemaphoreType.DMA((count, pieces)),
+            pltpu.SemaphoreType.DMA((count, rows // 16)),
         ],
         compiler_params=params(),
         cost_estimate=cost(1, 1),

time: 48.1 us -> 48.7 us (1.012)
  Pallas kernels: 27.4 us -> 29.3 us
  starting transfers between devices: 16.8 us -> 15.9 us
    pallas_call x2, Pallas kernels: 2.19 us -> 4.09 us  [normalize(): pl.pallas_call(functools.partial(normalize_kernel, count, len(squares), h...]
    ppermute x2, starting transfers between devices: 4.36 us -> 3.42 us  [of_panels(): lax.ppermute(square, 'panel', [(n, (n + shift) % count) for n in range(co...]
  transfers between devices with their start and end apart: 6 -> 6, of which waited for: 4 -> 3; matrix products, arithmetic and copies ran while one was open for 0% -> 0% of each run, Pallas kernels for 55% -> 57%
where the time goes in v11:
time: 48.7 us; the launch traced here: 48.5 us
  Pallas kernels  29.3 us (60%)
  starting transfers between devices  15.9 us (33%)
  waiting for transfers between devices  2.48 us (5%)
  between operations  0.79 us (2%)
    pallas_call x1, Pallas kernels, own_part(): pl.pallas_call(functools.partial(own_kernel, per), out_shape=(mixed, mixe...  12.6 us
    ppermute x4, starting transfers between devices, from_behind(): lax.ppermute(value, 'ctx', [(source, source + 1) for source in range(coun...  12.5 us
    pallas_call x1, Pallas kernels, mix(): pl.pallas_call(mix_kernel, out_shape=(jax.ShapeDtypeStruct((8, channels),...  6.86 us
    pallas_call x2, Pallas kernels, normalize(): pl.pallas_call(functools.partial(normalize_kernel, count, len(squares), h...  4.09 us
    ppermute x2, starting transfers between devices, of_panels(): lax.ppermute(square, 'panel', [(n, (n + shift) % count) for n in range(co...  3.42 us
    pallas_call x1, Pallas kernels, score(): pl.pallas_call(functools.partial(score_kernel, per), out_shape=(jax.Shape...  2.84 us
    pallas_call x1, Pallas kernels, pack(): pl.pallas_call(functools.partial(pack_kernel, per), out_shape=(jax.ShapeD...  2.26 us
    ppermute x2, waiting for transfers between devices, of_panels(): lax.ppermute(square, 'panel', [(n, (n + shift) % count) for n in range(co...  1.92 us
  transfers between devices with their start and end apart: 6, of which 3 were waited for; matrix products, arithmetic and copies ran while one was open for 0% of the time, Pallas kernels for 57%

profile of v11, /device:TPU:9, one launch (start us, length us, event | category | flops | bytes accessed | tf_op | source)
XLA Modules:
  0.0 48.5 jit_solution(263850337837259709)
XLA Ops:
  0.6 3.1 %collective-permute-start.2 = (bf16[144,2048]{1,0:T(8,128)(2,1)}, bf16[144,2048]{1,0:T(8,128)(2,1)S(1)}, u32[]{:S(2)}, u32[]{:S(2)}) collective-permute-start(bf16[144,2048]{1,0:T(8,128)(2,1)} %k_ref.1), channel_id=1, source_target_pairs={{0,2},{2,4},{4,6},{6,8},{8,10},{10,12},{12,14},{14,16},{16,18},{18... | collective-permute-start | bytes 1769480 | tf_op jit(solution)/shard_map/ppermute | solution.py:534
  3.8 2.3 %pack.1 = (bf16[2320,128]{1,0:T(8,128)(2,1)S(1)}, f32[3,3,2048]{2,1,0:T(4,128)S(1)}, f32[3,3,2048]{2,1,0:T(4,128)S(1)}, f32[1,2048]{1,0:T(1,128)S(1)}, f32[7,204...) custom-call(bf16[3,144,2048]{2,1,0:T(8,128)(2,1)} %m_hbm_ref.1, ...), custom_call_target="tpu_custom_call" | custom-call | flops 5898240 | bytes 2949120 | tf_op jit(solution)/shard_map/pack/pallas_call | solution.py:160
  6.0 3.1 %collective-permute-start.1 = (bf16[2320,128]{1,0:T(8,128)(2,1)S(1)}, bf16[2320,128]{1,0:T(8,128)(2,1)S(1)}, u32[]{:S(2)}, u32[]{:S(2)}) collective-permute-start(bf16[2320,128]{1,0:T(8,128)(2,1)S(1)} %get-tuple-element.47), channel_id=1, source_target_pairs={{0,2},{2,4},{4,6},{6,8},{8,10},{10,12},{12,14},{14,16},{16,18},{18... | collective-permute-start | bytes 1781768 | tf_op jit(solution)/shard_map/ppermute | solution.py:534
  9.2 0.0 copy-start
  9.2 0.0 copy-start.1
  9.2 0.0 copy-start.2
  9.2 12.6 %own_part.1 = (f32[144,2048]{1,0:T(8,128)S(1)}, f32[144,2048]{1,0:T(8,128)S(1)}, f32[144,2048]{1,0:T(8,128)S(1)}, f32[144,128]{1,0:T(8,128)S(1)}, f32[128,2048]{1,0:T(8,128)S(1)}, /*index=5*/f32[6,8,2048]{2,1,0:T(8,128)S(1)}) custom-call(bf16[3,144,2048]{2,1,0:T(8,128)(2,1)} %m_hbm_ref.1, bf16[3,144,2048]{2,1,0:T(8,128)(2,1)} %s_hbm_ref.1, ...), custom_call_target="tpu_custom_call" | custom-call | flops 53084160 | bytes 7077888 | tf_op jit(solution)/shard_map/own_part/pallas_call | solution.py:274
  21.8 3.1 %collective-permute-start = (bf16[144,1280]{1,0:T(8,128)(2,1)S(1)}, bf16[144,1280]{1,0:T(8,128)(2,1)S(1)}, u32[]{:S(2)}, u32[]{:S(2)}) collective-permute-start(bf16[144,1280]{1,0:T(8,128)(2,1)S(1)} %get-tuple-element.46), channel_id=1, source_target_pairs={{0,2},{2,4},{4,6},{6,8},{8,10},{10,12},{12,14},{14,16},{16,18},{18... | collective-permute-start | bytes 1105928 | tf_op jit(solution)/shard_map/ppermute | solution.py:534
  24.9 0.0 collective-permute-done.2.before_ref
  24.9 0.0 copy-done
  24.9 0.0 copy-done.1
  24.9 0.0 copy-done.2
  24.9 2.8 %score.1 = (bf16[16,144,144]{2,1,0:T(8,128)(2,1)S(1)}, f32[144,2048]{1,0:T(8,128)S(1)}, f32[144,2048]{1,0:T(8,128)S(1)}, f32[1,144,128]{2,1,0:T(8,128)S(1)}) custom-call(bf16[144,2048]{1,0:T(8,128)(2,1)S(1)} %copy-done.1, bf16[144,2048]{1,0:T(8,128)(2,1)S(1)} %copy-done.2, bf16[144,2048]{1,0:T(8,128)(2,1)S(1)} %collective-permute-done.2.before_ref, ...), custom_call_target="tpu_custom_call" | custom-call | flops 339738624 | bytes 4128768 | tf_op jit(solution)/shard_map/score/pallas_call | solution.py:431
  27.8 3.1 %collective-permute-start.4 = (bf16[144,768]{1,0:T(8,128)(2,1)S(1)}, bf16[144,768]{1,0:T(8,128)(2,1)S(1)}, u32[]{:S(2)}, u32[]{:S(2)}) collective-permute-start(bf16[144,768]{1,0:T(8,128)(2,1)S(1)} %get-tuple-element.66), channel_id=1, source_target_pairs={{0,2},{2,4},{4,6},{6,8},{8,10},{10,12},{12,14},{14,16},{16,18},{18... | collective-permute-start | bytes 663560 | tf_op jit(solution)/shard_map/ppermute | solution.py:534
  30.9 0.6 %collective-permute-done.1.packet_ref = bf16[2320,128]{1,0:T(8,128)(2,1)S(1)} collective-permute-done((bf16[2320,128]{1,0:T(8,128)(2,1)S(1)}, bf16[2320,128]{1,0:T(8,128)(2,1)S(1)}, u32[]{:S(2)}, u32[]{:S(2)}) %collective-permute-start.1) | collective-permute-done | bytes 593952 | tf_op jit(solution)/shard_map/ppermute | solution.py:534
  31.5 6.9 %mix.1 = (f32[8,2048]{1,0:T(8,128)S(1)}, f32[144,2048]{1,0:T(8,128)S(1)}, f32[2,144,128]{2,1,0:T(8,128)S(1)}) custom-call(bf16[2320,128]{1,0:T(8,128)(2,1)S(1)} %collective-permute-done.1.packet_ref, f32[144,2048]{1,0:T(8,128)S(1)} %get-tuple-element.52.own_ref, f32[144,2048]{1,0:T(8,128)S(1)} %get-tuple-element.53.z0_ref, ...), custom_call_target="tpu_custom_call" | custom-call | flops 1 | bytes 1 | tf_op jit(solution)/shard_map/mix/pallas_call | solution.py:374
  38.3 2.8 %collective-permute-start.3 = (f32[2,144,128]{2,1,0:T(8,128)S(1)}, f32[2,144,128]{2,1,0:T(8,128)S(1)}, u32[]{:S(2)}, u32[]{:S(2)}) collective-permute-start(f32[2,144,128]{2,1,0:T(8,128)S(1)} %get-tuple-element.57.refs_0_), channel_id=1, source_target_pairs={{0,1},{1,0},{2,3},{3,2},{4,5},{5,4},{6,7},{7,6},{8,9},{9,8},{10,11... | collective-permute-start | bytes 442376 | tf_op jit(solution)/shard_map/ppermute | solution.py:540
  41.1 1.0 %collective-permute-done.3.refs_1_ = f32[2,144,128]{2,1,0:T(8,128)S(1)} collective-permute-done((f32[2,144,128]{2,1,0:T(8,128)S(1)}, f32[2,144,128]{2,1,0:T(8,128)S(1)}, u32[]{:S(2)}, u32[]{:S(2)}) %collective-permute-start.3) | collective-permute-done | bytes 147488 | tf_op jit(solution)/shard_map/ppermute | solution.py:540
  42.1 2.5 %normalize.2 = (bf16[144,2048]{1,0:T(8,128)(2,1)}, bf16[144,2048]{1,0:T(8,128)(2,1)}) custom-call(f32[2,144,128]{2,1,0:T(8,128)S(1)} %get-tuple-element.57.refs_0_, f32[2,144,128]{2,1,0:T(8,128)S(1)} %collective-permute-done.3.refs_1_, f32[144,2048]{1,0:T(8,128)S(1)} %get-tuple-element.58.refs_2_, f32[144,2048]{1,0:T(8,128)S(1)} %get-tuple-element.59.refs_3_, ...), custom_call_target="tpu_custom_call" | custom-call | flops 1 | bytes 1 | tf_op jit(solution)/shard_map/normalize/pallas_call | solution.py:517
  44.6 0.0 collective-permute-done.before_ref
  44.6 0.4 value_mix.2
  45.0 0.0 collective-permute-done.4.before_ref
  45.0 0.3 value_mix.3
  45.3 0.7 %collective-permute-start.5 = (f32[1,144,128]{2,1,0:T(8,128)S(1)}, f32[1,144,128]{2,1,0:T(8,128)S(1)}, u32[]{:S(2)}, u32[]{:S(2)}) collective-permute-start(f32[1,144,128]{2,1,0:T(8,128)S(1)} %get-tuple-element.75.refs_0_), channel_id=1, source_target_pairs={{0,1},{1,0},{2,3},{3,2},{4,5},{5,4},{6,7},{7,6},{8,9},{9,8},{10,11... | collective-permute-start | bytes 221192 | tf_op jit(solution)/shard_map/ppermute | solution.py:540
  46.0 0.9 %collective-permute-done.5.refs_1_ = f32[1,144,128]{2,1,0:T(8,128)S(1)} collective-permute-done((f32[1,144,128]{2,1,0:T(8,128)S(1)}, f32[1,144,128]{2,1,0:T(8,128)S(1)}, u32[]{:S(2)}, u32[]{:S(2)}) %collective-permute-start.5) | collective-permute-done | bytes 73760 | tf_op jit(solution)/shard_map/ppermute | solution.py:540
  46.9 1.6 %normalize.3 = bf16[144,2048]{1,0:T(8,128)(2,1)} custom-call(f32[1,144,128]{2,1,0:T(8,128)S(1)} %get-tuple-element.75.refs_0_, f32[1,144,128]{2,1,0:T(8,128)S(1)} %collective-permute-done.5.refs_1_, f32[144,2048]{1,0:T(8,128)S(1)} %get-tuple-element.76.refs_2_), custom_call_target="tpu_custom_call" | custom-call | flops 1 | bytes 1 | tf_op jit(solution)/shard_map/normalize/pallas_call | solution.py:517
Async XLA Ops:
  0.6 24.3 %collective-permute-start.2 = (bf16[144,2048]{1,0:T(8,128)(2,1)}, bf16[144,2048]{1,0:T(8,128)(2,1)S(1)}, u32[]{:S(2)}, u32[]{:S(2)}) collective-permute-start(bf16[144,2048]{1,0:T(8,128)(2,1)} %k_ref.1), channel_id=1, source_target_pairs={{0,2},{2,4},{4,6},{6,8},{8,10},{10,12},{12,14},{14,16},{16,18},{18... | collective-permute-start | bytes 1769480 | tf_op jit(solution)/shard_map/ppermute | solution.py:534
  6.0 25.4 %collective-permute-start.1 = (bf16[2320,128]{1,0:T(8,128)(2,1)S(1)}, bf16[2320,128]{1,0:T(8,128)(2,1)S(1)}, u32[]{:S(2)}, u32[]{:S(2)}) collective-permute-start(bf16[2320,128]{1,0:T(8,128)(2,1)S(1)} %get-tuple-element.47), channel_id=1, source_target_pairs={{0,2},{2,4},{4,6},{6,8},{8,10},{10,12},{12,14},{14,16},{16,18},{18... | collective-permute-start | bytes 1781768 | tf_op jit(solution)/shard_map/ppermute | solution.py:534
  9.2 15.8 %copy-start = (bf16[144,2048]{1,0:T(8,128)(2,1)S(1)}, bf16[144,2048]{1,0:T(8,128)(2,1)}, u32[]{:S(2)}) copy-start(bf16[144,2048]{1,0:T(8,128)(2,1)} %v_ref.1) | copy-start | bytes 1769476
  9.2 15.8 %copy-start.1 = (bf16[144,2048]{1,0:T(8,128)(2,1)S(1)}, bf16[144,2048]{1,0:T(8,128)(2,1)}, u32[]{:S(2)}) copy-start(bf16[144,2048]{1,0:T(8,128)(2,1)} %q_ref.1) | copy-start | bytes 1769476
  9.2 15.7 %copy-start.2 = (bf16[144,2048]{1,0:T(8,128)(2,1)S(1)}, bf16[144,2048]{1,0:T(8,128)(2,1)}, u32[]{:S(2)}) copy-start(bf16[144,2048]{1,0:T(8,128)(2,1)} %k_ref.1) | copy-start | bytes 1769476
  21.8 22.9 %collective-permute-start = (bf16[144,1280]{1,0:T(8,128)(2,1)S(1)}, bf16[144,1280]{1,0:T(8,128)(2,1)S(1)}, u32[]{:S(2)}, u32[]{:S(2)}) collective-permute-start(bf16[144,1280]{1,0:T(8,128)(2,1)S(1)} %get-tuple-element.46), channel_id=1, source_target_pairs={{0,2},{2,4},{4,6},{6,8},{8,10},{10,12},{12,14},{14,16},{16,18},{18... | collective-permute-start | bytes 1105928 | tf_op jit(solution)/shard_map/ppermute | solution.py:534
  27.8 17.3 %collective-permute-start.4 = (bf16[144,768]{1,0:T(8,128)(2,1)S(1)}, bf16[144,768]{1,0:T(8,128)(2,1)S(1)}, u32[]{:S(2)}, u32[]{:S(2)}) collective-permute-start(bf16[144,768]{1,0:T(8,128)(2,1)S(1)} %get-tuple-element.66), channel_id=1, source_target_pairs={{0,2},{2,4},{4,6},{6,8},{8,10},{10,12},{12,14},{14,16},{16,18},{18... | collective-permute-start | bytes 663560 | tf_op jit(solution)/shard_map/ppermute | solution.py:534
  38.3 3.8 %collective-permute-start.3 = (f32[2,144,128]{2,1,0:T(8,128)S(1)}, f32[2,144,128]{2,1,0:T(8,128)S(1)}, u32[]{:S(2)}, u32[]{:S(2)}) collective-permute-start(f32[2,144,128]{2,1,0:T(8,128)S(1)} %get-tuple-element.57.refs_0_), channel_id=1, source_target_pairs={{0,1},{1,0},{2,3},{3,2},{4,5},{5,4},{6,7},{7,6},{8,9},{9,8},{10,11... | collective-permute-start | bytes 442376 | tf_op jit(solution)/shard_map/ppermute | solution.py:540
  45.3 1.6 %collective-permute-start.5 = (f32[1,144,128]{2,1,0:T(8,128)S(1)}, f32[1,144,128]{2,1,0:T(8,128)S(1)}, u32[]{:S(2)}, u32[]{:S(2)}) collective-permute-start(f32[1,144,128]{2,1,0:T(8,128)S(1)} %get-tuple-element.75.refs_0_), channel_id=1, source_target_pairs={{0,1},{1,0},{2,3},{3,2},{4,5},{5,4},{6,7},{7,6},{8,9},{9,8},{10,11... | collective-permute-start | bytes 221192 | tf_op jit(solution)/shard_map/ppermute | solution.py:540

commit v12 on v10

--- a/solution.py
+++ b/solution.py
@@ -108,7 +108,7 @@
         pltpu.make_async_copy(decay_hbm_ref, decay_ref, late_sems.at[2]),
         pltpu.make_async_copy(filter_hbm_ref, filter_ref, late_sems.at[3]),
     ]
-    for copy in copies + late:
+    for copy in copies:
         copy.start()
     for copy in copies[:first]:
         copy.wait()
@@ -144,6 +144,9 @@
 
     for n in range(channels // width):
         copies[first + n].wait()
+        if n == 0:
+            for copy in late:
+                copy.start()
         pl.loop(n * per, (n + 1) * per)(one)
 
     out_ref[out_ref.shape[0] - 16 :, :] = last_ref[...].astype(BF16)
@@ -542,7 +545,7 @@
 
 
 def body(se, se_short, se_filter, mr, mr_short, raw, decay, queries, keys, values):
-    last_heads = 3 * (queries.shape[1] // HD) // 8
+    last_heads = 5 * (queries.shape[1] // HD) // 16
     key_before = from_behind(keys)
     packet, mr_taps, se_taps, decay, filter_taps, most, rest = pack(
         se, mr, se_short, mr_short, decay[None, :], se_filter, values, last_heads, 4

time: 48.1 us -> 48.3 us (level)
  Pallas kernels: 27.4 us -> 28.1 us
  waiting for transfers between devices: 2.86 us -> 2.33 us
    pallas_call x2, Pallas kernels: 0.68 us -> 1.24 us  [value_mix(): pl.pallas_call(functools.partial(value_kernel, first), out_shape=(jax.Sha...]
    ppermute x4, waiting for transfers between devices: 0.94 us -> 0.41 us  [from_behind(): lax.ppermute(value, 'ctx', [(source, source + 1) for source in range(coun...]
  transfers between devices with their start and end apart: 6 -> 6, of which waited for: 4 -> 3; matrix products, arithmetic and copies ran while one was open for 0% -> 0% of each run, Pallas kernels for 55% -> 56%
where the time goes in v12:
time: 48.3 us; the launch traced here: 48 us
  Pallas kernels  28.1 us (58%)
  starting transfers between devices  16.8 us (35%)
  waiting for transfers between devices  2.33 us (5%)
  between operations  0.78 us (2%)
    pallas_call x1, Pallas kernels, own_part(): pl.pallas_call(functools.partial(own_kernel, per), out_shape=(mixed, mixe...  12.6 us
    ppermute x4, starting transfers between devices, from_behind(): lax.ppermute(value, 'ctx', [(source, source + 1) for source in range(coun...  12.5 us
    pallas_call x1, Pallas kernels, mix(): pl.pallas_call(mix_kernel, out_shape=(jax.ShapeDtypeStruct((8, channels),...  6.86 us
    ppermute x2, starting transfers between devices, of_panels(): lax.ppermute(square, 'panel', [(n, (n + shift) % count) for n in range(co...  4.32 us
    pallas_call x1, Pallas kernels, score(): pl.pallas_call(functools.partial(score_kernel, per), out_shape=(jax.Shape...  2.83 us
    pallas_call x1, Pallas kernels, pack(): pl.pallas_call(functools.partial(pack_kernel, per), out_shape=(jax.ShapeD...  2.41 us
    pallas_call x2, Pallas kernels, normalize(): pl.pallas_call(functools.partial(normalize_kernel, count, len(squares), p...  2.19 us
    ppermute x2, waiting for transfers between devices, of_panels(): lax.ppermute(square, 'panel', [(n, (n + shift) % count) for n in range(co...  1.92 us
  transfers between devices with their start and end apart: 6, of which 3 were waited for; matrix products, arithmetic and copies ran while one was open for 0% of the time, Pallas kernels for 56%

profile of v12, /device:TPU:9, one launch (start us, length us, event | category | flops | bytes accessed | tf_op | source)
XLA Modules:
  0.0 48.0 jit_solution(6123510374607026451)
XLA Ops:
  0.6 3.1 %collective-permute-start.2 = (bf16[144,2048]{1,0:T(8,128)(2,1)}, bf16[144,2048]{1,0:T(8,128)(2,1)S(1)}, u32[]{:S(2)}, u32[]{:S(2)}) collective-permute-start(bf16[144,2048]{1,0:T(8,128)(2,1)} %k_ref.1), channel_id=1, source_target_pairs={{0,2},{2,4},{4,6},{6,8},{8,10},{10,12},{12,14},{14,16},{16,18},{18... | collective-permute-start | bytes 1769480 | tf_op jit(solution)/shard_map/ppermute | solution.py:536
  3.8 2.4 %pack.1 = (bf16[2320,128]{1,0:T(8,128)(2,1)S(1)}, f32[3,3,2048]{2,1,0:T(4,128)S(1)}, f32[3,3,2048]{2,1,0:T(4,128)S(1)}, f32[1,2048]{1,0:T(1,128)S(1)}, f32[7,204...) custom-call(bf16[3,144,2048]{2,1,0:T(8,128)(2,1)} %m_hbm_ref.1, ...), custom_call_target="tpu_custom_call" | custom-call | flops 5898240 | bytes 2949120 | tf_op jit(solution)/shard_map/pack/pallas_call | solution.py:163
  6.2 3.1 %collective-permute-start.1 = (bf16[2320,128]{1,0:T(8,128)(2,1)S(1)}, bf16[2320,128]{1,0:T(8,128)(2,1)S(1)}, u32[]{:S(2)}, u32[]{:S(2)}) collective-permute-start(bf16[2320,128]{1,0:T(8,128)(2,1)S(1)} %get-tuple-element.47), channel_id=1, source_target_pairs={{0,2},{2,4},{4,6},{6,8},{8,10},{10,12},{12,14},{14,16},{16,18},{18... | collective-permute-start | bytes 1781768 | tf_op jit(solution)/shard_map/ppermute | solution.py:536
  9.3 0.0 copy-start
  9.3 0.0 copy-start.1
  9.3 0.0 copy-start.2
  9.3 12.6 %own_part.1 = (f32[144,2048]{1,0:T(8,128)S(1)}, f32[144,2048]{1,0:T(8,128)S(1)}, f32[144,2048]{1,0:T(8,128)S(1)}, f32[144,128]{1,0:T(8,128)S(1)}, f32[128,2048]{1,0:T(8,128)S(1)}, /*index=5*/f32[6,8,2048]{2,1,0:T(8,128)S(1)}) custom-call(bf16[3,144,2048]{2,1,0:T(8,128)(2,1)} %m_hbm_ref.1, bf16[3,144,2048]{2,1,0:T(8,128)(2,1)} %s_hbm_ref.1, ...), custom_call_target="tpu_custom_call" | custom-call | flops 53084160 | bytes 7077888 | tf_op jit(solution)/shard_map/own_part/pallas_call | solution.py:277
  21.9 3.1 %collective-permute-start = (bf16[144,1408]{1,0:T(8,128)(2,1)S(1)}, bf16[144,1408]{1,0:T(8,128)(2,1)S(1)}, u32[]{:S(2)}, u32[]{:S(2)}) collective-permute-start(bf16[144,1408]{1,0:T(8,128)(2,1)S(1)} %get-tuple-element.46), channel_id=1, source_target_pairs={{0,2},{2,4},{4,6},{6,8},{8,10},{10,12},{12,14},{14,16},{16,18},{18... | collective-permute-start | bytes 1216520 | tf_op jit(solution)/shard_map/ppermute | solution.py:536
  25.0 0.0 collective-permute-done.2.before_ref
  25.1 0.0 copy-done
  25.1 0.0 copy-done.1
  25.1 0.0 copy-done.2
  25.1 2.8 %score.1 = (bf16[16,144,144]{2,1,0:T(8,128)(2,1)S(1)}, f32[144,2048]{1,0:T(8,128)S(1)}, f32[144,2048]{1,0:T(8,128)S(1)}, f32[1,144,128]{2,1,0:T(8,128)S(1)}) custom-call(bf16[144,2048]{1,0:T(8,128)(2,1)S(1)} %copy-done.1, bf16[144,2048]{1,0:T(8,128)(2,1)S(1)} %copy-done.2, bf16[144,2048]{1,0:T(8,128)(2,1)S(1)} %collective-permute-done.2.before_ref, ...), custom_call_target="tpu_custom_call" | custom-call | flops 339738624 | bytes 4128768 | tf_op jit(solution)/shard_map/score/pallas_call | solution.py:434
  27.9 3.1 %collective-permute-start.4 = (bf16[144,640]{1,0:T(8,128)(2,1)S(1)}, bf16[144,640]{1,0:T(8,128)(2,1)S(1)}, u32[]{:S(2)}, u32[]{:S(2)}) collective-permute-start(bf16[144,640]{1,0:T(8,128)(2,1)S(1)} %get-tuple-element.66), channel_id=1, source_target_pairs={{0,2},{2,4},{4,6},{6,8},{8,10},{10,12},{12,14},{14,16},{16,18},{18... | collective-permute-start | bytes 552968 | tf_op jit(solution)/shard_map/ppermute | solution.py:536
  31.1 0.4 collective-permute-done.1.packet_ref
  31.5 6.9 %mix.1 = (f32[8,2048]{1,0:T(8,128)S(1)}, f32[144,2048]{1,0:T(8,128)S(1)}, f32[2,144,128]{2,1,0:T(8,128)S(1)}) custom-call(bf16[2320,128]{1,0:T(8,128)(2,1)S(1)} %collective-permute-done.1.packet_ref, f32[144,2048]{1,0:T(8,128)S(1)} %get-tuple-element.52.own_ref, f32[144,2048]{1,0:T(8,128)S(1)} %get-tuple-element.53.z0_ref, ...), custom_call_target="tpu_custom_call" | custom-call | flops 1 | bytes 1 | tf_op jit(solution)/shard_map/mix/pallas_call | solution.py:377
  38.3 2.8 %collective-permute-start.3 = (f32[2,144,128]{2,1,0:T(8,128)S(1)}, f32[2,144,128]{2,1,0:T(8,128)S(1)}, u32[]{:S(2)}, u32[]{:S(2)}) collective-permute-start(f32[2,144,128]{2,1,0:T(8,128)S(1)} %get-tuple-element.57.refs_0_), channel_id=1, source_target_pairs={{0,1},{1,0},{2,3},{3,2},{4,5},{5,4},{6,7},{7,6},{8,9},{9,8},{10,11... | collective-permute-start | bytes 442376 | tf_op jit(solution)/shard_map/ppermute | solution.py:542
  41.1 1.0 %collective-permute-done.3.refs_1_ = f32[2,144,128]{2,1,0:T(8,128)S(1)} collective-permute-done((f32[2,144,128]{2,1,0:T(8,128)S(1)}, f32[2,144,128]{2,1,0:T(8,128)S(1)}, u32[]{:S(2)}, u32[]{:S(2)}) %collective-permute-start.3) | collective-permute-done | bytes 147488 | tf_op jit(solution)/shard_map/ppermute | solution.py:542
  42.1 1.2 %normalize.2 = (bf16[144,2048]{1,0:T(8,128)(2,1)}, bf16[144,2048]{1,0:T(8,128)(2,1)}) custom-call(f32[2,144,128]{2,1,0:T(8,128)S(1)} %get-tuple-element.57.refs_0_, f32[2,144,128]{2,1,0:T(8,128)S(1)} %collective-permute-done.3.refs_1_, f32[144,2048]{1,0:T(8,128)S(1)} %get-tuple-element.58.refs_2_, f32[144,2048]{1,0:T(8,128)S(1)} %get-tuple-element.59.refs_3_, ...), custom_call_target="tpu_custom_call" | custom-call | flops 1 | bytes 1 | tf_op jit(solution)/shard_map/normalize/pallas_call | solution.py:519
  43.3 0.0 collective-permute-done.before_ref
  43.3 0.8 %value_mix.2 = (f32[144,2048]{1,0:T(8,128)S(1)}, f32[1,144,128]{2,1,0:T(8,128)S(1)}) custom-call(bf16[16,144,144]{2,1,0:T(8,128)(2,1)S(1)} %get-tuple-element.65.probs_ref, bf16[144,1408]{1,0:T(8,128)(2,1)S(1)} %collective-permute-done.before_ref, f32[144,2048]{1,0:T(8,128)S(1)} %get-tuple-element.68.own_ref, ...), custom_call_target="tpu_custom_call", output_to_operand_aliasing={{0}: (2, {})} | custom-call | flops 1 | bytes 1 | tf_op jit(solution)/shard_map/value_mix/pallas_call | solution.py:469
  44.1 0.0 collective-permute-done.4.before_ref
  44.1 0.4 value_mix.3
  44.6 1.6 %collective-permute-start.5 = (f32[1,144,128]{2,1,0:T(8,128)S(1)}, f32[1,144,128]{2,1,0:T(8,128)S(1)}, u32[]{:S(2)}, u32[]{:S(2)}) collective-permute-start(f32[1,144,128]{2,1,0:T(8,128)S(1)} %get-tuple-element.75.refs_0_), channel_id=1, source_target_pairs={{0,1},{1,0},{2,3},{3,2},{4,5},{5,4},{6,7},{7,6},{8,9},{9,8},{10,11... | collective-permute-start | bytes 221192 | tf_op jit(solution)/shard_map/ppermute | solution.py:542
  46.1 0.9 %collective-permute-done.5.refs_1_ = f32[1,144,128]{2,1,0:T(8,128)S(1)} collective-permute-done((f32[1,144,128]{2,1,0:T(8,128)S(1)}, f32[1,144,128]{2,1,0:T(8,128)S(1)}, u32[]{:S(2)}, u32[]{:S(2)}) %collective-permute-start.5) | collective-permute-done | bytes 73760 | tf_op jit(solution)/shard_map/ppermute | solution.py:542
  47.1 1.0 %normalize.3 = bf16[144,2048]{1,0:T(8,128)(2,1)} custom-call(f32[1,144,128]{2,1,0:T(8,128)S(1)} %get-tuple-element.75.refs_0_, f32[1,144,128]{2,1,0:T(8,128)S(1)} %collective-permute-done.5.refs_1_, f32[144,2048]{1,0:T(8,128)S(1)} %get-tuple-element.76.refs_2_), custom_call_target="tpu_custom_call" | custom-call | flops 1 | bytes 1 | tf_op jit(solution)/shard_map/normalize/pallas_call | solution.py:519
Async XLA Ops:
  0.6 24.4 %collective-permute-start.2 = (bf16[144,2048]{1,0:T(8,128)(2,1)}, bf16[144,2048]{1,0:T(8,128)(2,1)S(1)}, u32[]{:S(2)}, u32[]{:S(2)}) collective-permute-start(bf16[144,2048]{1,0:T(8,128)(2,1)} %k_ref.1), channel_id=1, source_target_pairs={{0,2},{2,4},{4,6},{6,8},{8,10},{10,12},{12,14},{14,16},{16,18},{18... | collective-permute-start | bytes 1769480 | tf_op jit(solution)/shard_map/ppermute | solution.py:536
  6.2 25.3 %collective-permute-start.1 = (bf16[2320,128]{1,0:T(8,128)(2,1)S(1)}, bf16[2320,128]{1,0:T(8,128)(2,1)S(1)}, u32[]{:S(2)}, u32[]{:S(2)}) collective-permute-start(bf16[2320,128]{1,0:T(8,128)(2,1)S(1)} %get-tuple-element.47), channel_id=1, source_target_pairs={{0,2},{2,4},{4,6},{6,8},{8,10},{10,12},{12,14},{14,16},{16,18},{18... | collective-permute-start | bytes 1781768 | tf_op jit(solution)/shard_map/ppermute | solution.py:536
  9.3 15.8 %copy-start = (bf16[144,2048]{1,0:T(8,128)(2,1)S(1)}, bf16[144,2048]{1,0:T(8,128)(2,1)}, u32[]{:S(2)}) copy-start(bf16[144,2048]{1,0:T(8,128)(2,1)} %v_ref.1) | copy-start | bytes 1769476
  9.3 15.8 %copy-start.1 = (bf16[144,2048]{1,0:T(8,128)(2,1)S(1)}, bf16[144,2048]{1,0:T(8,128)(2,1)}, u32[]{:S(2)}) copy-start(bf16[144,2048]{1,0:T(8,128)(2,1)} %q_ref.1) | copy-start | bytes 1769476
  9.3 15.7 %copy-start.2 = (bf16[144,2048]{1,0:T(8,128)(2,1)S(1)}, bf16[144,2048]{1,0:T(8,128)(2,1)}, u32[]{:S(2)}) copy-start(bf16[144,2048]{1,0:T(8,128)(2,1)} %k_ref.1) | copy-start | bytes 1769476
  21.9 21.4 %collective-permute-start = (bf16[144,1408]{1,0:T(8,128)(2,1)S(1)}, bf16[144,1408]{1,0:T(8,128)(2,1)S(1)}, u32[]{:S(2)}, u32[]{:S(2)}) collective-permute-start(bf16[144,1408]{1,0:T(8,128)(2,1)S(1)} %get-tuple-element.46), channel_id=1, source_target_pairs={{0,2},{2,4},{4,6},{6,8},{8,10},{10,12},{12,14},{14,16},{16,18},{18... | collective-permute-start | bytes 1216520 | tf_op jit(solution)/shard_map/ppermute | solution.py:536
  27.9 16.2 %collective-permute-start.4 = (bf16[144,640]{1,0:T(8,128)(2,1)S(1)}, bf16[144,640]{1,0:T(8,128)(2,1)S(1)}, u32[]{:S(2)}, u32[]{:S(2)}) collective-permute-start(bf16[144,640]{1,0:T(8,128)(2,1)S(1)} %get-tuple-element.66), channel_id=1, source_target_pairs={{0,2},{2,4},{4,6},{6,8},{8,10},{10,12},{12,14},{14,16},{16,18},{18... | collective-permute-start | bytes 552968 | tf_op jit(solution)/shard_map/ppermute | solution.py:536
  38.3 3.8 %collective-permute-start.3 = (f32[2,144,128]{2,1,0:T(8,128)S(1)}, f32[2,144,128]{2,1,0:T(8,128)S(1)}, u32[]{:S(2)}, u32[]{:S(2)}) collective-permute-start(f32[2,144,128]{2,1,0:T(8,128)S(1)} %get-tuple-element.57.refs_0_), channel_id=1, source_target_pairs={{0,1},{1,0},{2,3},{3,2},{4,5},{5,4},{6,7},{7,6},{8,9},{9,8},{10,11... | collective-permute-start | bytes 442376 | tf_op jit(solution)/shard_map/ppermute | solution.py:542
  44.6 2.5 %collective-permute-start.5 = (f32[1,144,128]{2,1,0:T(8,128)S(1)}, f32[1,144,128]{2,1,0:T(8,128)S(1)}, u32[]{:S(2)}, u32[]{:S(2)}) collective-permute-start(f32[1,144,128]{2,1,0:T(8,128)S(1)} %get-tuple-element.75.refs_0_), channel_id=1, source_target_pairs={{0,1},{1,0},{2,3},{3,2},{4,5},{5,4},{6,7},{7,6},{8,9},{9,8},{10,11... | collective-permute-start | bytes 221192 | tf_op jit(solution)/shard_map/ppermute | solution.py:542

commit v13 on v12

--- a/solution.py
+++ b/solution.py
@@ -545,7 +545,7 @@
 
 
 def body(se, se_short, se_filter, mr, mr_short, raw, decay, queries, keys, values):
-    last_heads = 5 * (queries.shape[1] // HD) // 16
+    last_heads = 3 * (queries.shape[1] // HD) // 8
     key_before = from_behind(keys)
     packet, mr_taps, se_taps, decay, filter_taps, most, rest = pack(
         se, mr, se_short, mr_short, decay[None, :], se_filter, values, last_heads, 4

time: 48.3 us -> 48.1 us (level)
  Pallas kernels: 28.1 us -> 27.5 us
    pallas_call x2, Pallas kernels: 1.24 us -> 0.68 us  [value_mix(): pl.pallas_call(functools.partial(value_kernel, first), out_shape=(jax.Sha...]
  transfers between devices with their start and end apart: 6 -> 6, of which waited for: 3 -> 4; matrix products, arithmetic and copies ran while one was open for 0% -> 0% of each run, Pallas kernels for 56% -> 55%
where the time goes in v13:
time: 48.1 us; the launch traced here: 47.9 us
  Pallas kernels  27.5 us (57%)
  starting transfers between devices  16.8 us (35%)
  waiting for transfers between devices  2.7 us (6%)
  between operations  0.78 us (2%)
    pallas_call x1, Pallas kernels, own_part(): pl.pallas_call(functools.partial(own_kernel, per), out_shape=(mixed, mixe...  12.6 us
    ppermute x4, starting transfers between devices, from_behind(): lax.ppermute(value, 'ctx', [(source, source + 1) for source in range(coun...  12.5 us
    pallas_call x1, Pallas kernels, mix(): pl.pallas_call(mix_kernel, out_shape=(jax.ShapeDtypeStruct((8, channels),...  6.86 us
    ppermute x2, starting transfers between devices, of_panels(): lax.ppermute(square, 'panel', [(n, (n + shift) % count) for n in range(co...  4.36 us
    pallas_call x1, Pallas kernels, score(): pl.pallas_call(functools.partial(score_kernel, per), out_shape=(jax.Shape...  2.84 us
    pallas_call x1, Pallas kernels, pack(): pl.pallas_call(functools.partial(pack_kernel, per), out_shape=(jax.ShapeD...  2.41 us
    pallas_call x2, Pallas kernels, normalize(): pl.pallas_call(functools.partial(normalize_kernel, count, len(squares), p...  2.19 us
    ppermute x2, waiting for transfers between devices, of_panels(): lax.ppermute(square, 'panel', [(n, (n + shift) % count) for n in range(co...  1.92 us
  transfers between devices with their start and end apart: 6, of which 4 were waited for; matrix products, arithmetic and copies ran while one was open for 0% of the time, Pallas kernels for 55%

profile of v13, /device:TPU:9, one launch (start us, length us, event | category | flops | bytes accessed | tf_op | source)
XLA Modules:
  0.0 47.9 jit_solution(9329479875327695548)
XLA Ops:
  0.6 3.1 %collective-permute-start.2 = (bf16[144,2048]{1,0:T(8,128)(2,1)}, bf16[144,2048]{1,0:T(8,128)(2,1)S(1)}, u32[]{:S(2)}, u32[]{:S(2)}) collective-permute-start(bf16[144,2048]{1,0:T(8,128)(2,1)} %k_ref.1), channel_id=1, source_target_pairs={{0,2},{2,4},{4,6},{6,8},{8,10},{10,12},{12,14},{14,16},{16,18},{18... | collective-permute-start | bytes 1769480 | tf_op jit(solution)/shard_map/ppermute | solution.py:536
  3.8 2.4 %pack.1 = (bf16[2320,128]{1,0:T(8,128)(2,1)S(1)}, f32[3,3,2048]{2,1,0:T(4,128)S(1)}, f32[3,3,2048]{2,1,0:T(4,128)S(1)}, f32[1,2048]{1,0:T(1,128)S(1)}, f32[7,204...) custom-call(bf16[3,144,2048]{2,1,0:T(8,128)(2,1)} %m_hbm_ref.1, ...), custom_call_target="tpu_custom_call" | custom-call | flops 5898240 | bytes 2949120 | tf_op jit(solution)/shard_map/pack/pallas_call | solution.py:163
  6.2 3.1 %collective-permute-start.1 = (bf16[2320,128]{1,0:T(8,128)(2,1)S(1)}, bf16[2320,128]{1,0:T(8,128)(2,1)S(1)}, u32[]{:S(2)}, u32[]{:S(2)}) collective-permute-start(bf16[2320,128]{1,0:T(8,128)(2,1)S(1)} %get-tuple-element.47), channel_id=1, source_target_pairs={{0,2},{2,4},{4,6},{6,8},{8,10},{10,12},{12,14},{14,16},{16,18},{18... | collective-permute-start | bytes 1781768 | tf_op jit(solution)/shard_map/ppermute | solution.py:536
  9.3 0.0 copy-start
  9.3 0.0 copy-start.1
  9.3 0.0 copy-start.2
  9.3 12.6 %own_part.1 = (f32[144,2048]{1,0:T(8,128)S(1)}, f32[144,2048]{1,0:T(8,128)S(1)}, f32[144,2048]{1,0:T(8,128)S(1)}, f32[144,128]{1,0:T(8,128)S(1)}, f32[128,2048]{1,0:T(8,128)S(1)}, /*index=5*/f32[6,8,2048]{2,1,0:T(8,128)S(1)}) custom-call(bf16[3,144,2048]{2,1,0:T(8,128)(2,1)} %m_hbm_ref.1, bf16[3,144,2048]{2,1,0:T(8,128)(2,1)} %s_hbm_ref.1, ...), custom_call_target="tpu_custom_call" | custom-call | flops 53084160 | bytes 7077888 | tf_op jit(solution)/shard_map/own_part/pallas_call | solution.py:277
  21.9 3.1 %collective-permute-start = (bf16[144,1280]{1,0:T(8,128)(2,1)S(1)}, bf16[144,1280]{1,0:T(8,128)(2,1)S(1)}, u32[]{:S(2)}, u32[]{:S(2)}) collective-permute-start(bf16[144,1280]{1,0:T(8,128)(2,1)S(1)} %get-tuple-element.46), channel_id=1, source_target_pairs={{0,2},{2,4},{4,6},{6,8},{8,10},{10,12},{12,14},{14,16},{16,18},{18... | collective-permute-start | bytes 1105928 | tf_op jit(solution)/shard_map/ppermute | solution.py:536
  25.0 0.0 collective-permute-done.2.before_ref
  25.1 0.0 copy-done
  25.1 0.0 copy-done.1
  25.1 0.0 copy-done.2
  25.1 2.8 %score.1 = (bf16[16,144,144]{2,1,0:T(8,128)(2,1)S(1)}, f32[144,2048]{1,0:T(8,128)S(1)}, f32[144,2048]{1,0:T(8,128)S(1)}, f32[1,144,128]{2,1,0:T(8,128)S(1)}) custom-call(bf16[144,2048]{1,0:T(8,128)(2,1)S(1)} %copy-done.1, bf16[144,2048]{1,0:T(8,128)(2,1)S(1)} %copy-done.2, bf16[144,2048]{1,0:T(8,128)(2,1)S(1)} %collective-permute-done.2.before_ref, ...), custom_call_target="tpu_custom_call" | custom-call | flops 339738624 | bytes 4128768 | tf_op jit(solution)/shard_map/score/pallas_call | solution.py:434
  27.9 3.1 %collective-permute-start.4 = (bf16[144,768]{1,0:T(8,128)(2,1)S(1)}, bf16[144,768]{1,0:T(8,128)(2,1)S(1)}, u32[]{:S(2)}, u32[]{:S(2)}) collective-permute-start(bf16[144,768]{1,0:T(8,128)(2,1)S(1)} %get-tuple-element.66), channel_id=1, source_target_pairs={{0,2},{2,4},{4,6},{6,8},{8,10},{10,12},{12,14},{14,16},{16,18},{18... | collective-permute-start | bytes 663560 | tf_op jit(solution)/shard_map/ppermute | solution.py:536
  31.1 0.4 collective-permute-done.1.packet_ref
  31.5 6.9 %mix.1 = (f32[8,2048]{1,0:T(8,128)S(1)}, f32[144,2048]{1,0:T(8,128)S(1)}, f32[2,144,128]{2,1,0:T(8,128)S(1)}) custom-call(bf16[2320,128]{1,0:T(8,128)(2,1)S(1)} %collective-permute-done.1.packet_ref, f32[144,2048]{1,0:T(8,128)S(1)} %get-tuple-element.52.own_ref, f32[144,2048]{1,0:T(8,128)S(1)} %get-tuple-element.53.z0_ref, ...), custom_call_target="tpu_custom_call" | custom-call | flops 1 | bytes 1 | tf_op jit(solution)/shard_map/mix/pallas_call | solution.py:377
  38.3 2.8 %collective-permute-start.3 = (f32[2,144,128]{2,1,0:T(8,128)S(1)}, f32[2,144,128]{2,1,0:T(8,128)S(1)}, u32[]{:S(2)}, u32[]{:S(2)}) collective-permute-start(f32[2,144,128]{2,1,0:T(8,128)S(1)} %get-tuple-element.57.refs_0_), channel_id=1, source_target_pairs={{0,1},{1,0},{2,3},{3,2},{4,5},{5,4},{6,7},{7,6},{8,9},{9,8},{10,11... | collective-permute-start | bytes 442376 | tf_op jit(solution)/shard_map/ppermute | solution.py:542
  41.1 1.0 %collective-permute-done.3.refs_1_ = f32[2,144,128]{2,1,0:T(8,128)S(1)} collective-permute-done((f32[2,144,128]{2,1,0:T(8,128)S(1)}, f32[2,144,128]{2,1,0:T(8,128)S(1)}, u32[]{:S(2)}, u32[]{:S(2)}) %collective-permute-start.3) | collective-permute-done | bytes 147488 | tf_op jit(solution)/shard_map/ppermute | solution.py:542
  42.1 1.2 %normalize.2 = (bf16[144,2048]{1,0:T(8,128)(2,1)}, bf16[144,2048]{1,0:T(8,128)(2,1)}) custom-call(f32[2,144,128]{2,1,0:T(8,128)S(1)} %get-tuple-element.57.refs_0_, f32[2,144,128]{2,1,0:T(8,128)S(1)} %collective-permute-done.3.refs_1_, f32[144,2048]{1,0:T(8,128)S(1)} %get-tuple-element.58.refs_2_, f32[144,2048]{1,0:T(8,128)S(1)} %get-tuple-element.59.refs_3_, ...), custom_call_target="tpu_custom_call" | custom-call | flops 1 | bytes 1 | tf_op jit(solution)/shard_map/normalize/pallas_call | solution.py:519
  43.3 0.0 collective-permute-done.before_ref
  43.3 0.4 value_mix.2
  43.7 0.4 collective-permute-done.4.before_ref
  44.1 0.3 value_mix.3
  44.4 1.6 %collective-permute-start.5 = (f32[1,144,128]{2,1,0:T(8,128)S(1)}, f32[1,144,128]{2,1,0:T(8,128)S(1)}, u32[]{:S(2)}, u32[]{:S(2)}) collective-permute-start(f32[1,144,128]{2,1,0:T(8,128)S(1)} %get-tuple-element.75.refs_0_), channel_id=1, source_target_pairs={{0,1},{1,0},{2,3},{3,2},{4,5},{5,4},{6,7},{7,6},{8,9},{9,8},{10,11... | collective-permute-start | bytes 221192 | tf_op jit(solution)/shard_map/ppermute | solution.py:542
  46.0 0.9 %collective-permute-done.5.refs_1_ = f32[1,144,128]{2,1,0:T(8,128)S(1)} collective-permute-done((f32[1,144,128]{2,1,0:T(8,128)S(1)}, f32[1,144,128]{2,1,0:T(8,128)S(1)}, u32[]{:S(2)}, u32[]{:S(2)}) %collective-permute-start.5) | collective-permute-done | bytes 73760 | tf_op jit(solution)/shard_map/ppermute | solution.py:542
  46.9 1.0 %normalize.3 = bf16[144,2048]{1,0:T(8,128)(2,1)} custom-call(f32[1,144,128]{2,1,0:T(8,128)S(1)} %get-tuple-element.75.refs_0_, f32[1,144,128]{2,1,0:T(8,128)S(1)} %collective-permute-done.5.refs_1_, f32[144,2048]{1,0:T(8,128)S(1)} %get-tuple-element.76.refs_2_), custom_call_target="tpu_custom_call" | custom-call | flops 1 | bytes 1 | tf_op jit(solution)/shard_map/normalize/pallas_call | solution.py:519
Async XLA Ops:
  0.6 24.4 %collective-permute-start.2 = (bf16[144,2048]{1,0:T(8,128)(2,1)}, bf16[144,2048]{1,0:T(8,128)(2,1)S(1)}, u32[]{:S(2)}, u32[]{:S(2)}) collective-permute-start(bf16[144,2048]{1,0:T(8,128)(2,1)} %k_ref.1), channel_id=1, source_target_pairs={{0,2},{2,4},{4,6},{6,8},{8,10},{10,12},{12,14},{14,16},{16,18},{18... | collective-permute-start | bytes 1769480 | tf_op jit(solution)/shard_map/ppermute | solution.py:536
  6.2 25.3 %collective-permute-start.1 = (bf16[2320,128]{1,0:T(8,128)(2,1)S(1)}, bf16[2320,128]{1,0:T(8,128)(2,1)S(1)}, u32[]{:S(2)}, u32[]{:S(2)}) collective-permute-start(bf16[2320,128]{1,0:T(8,128)(2,1)S(1)} %get-tuple-element.47), channel_id=1, source_target_pairs={{0,2},{2,4},{4,6},{6,8},{8,10},{10,12},{12,14},{14,16},{16,18},{18... | collective-permute-start | bytes 1781768 | tf_op jit(solution)/shard_map/ppermute | solution.py:536
  9.3 15.8 %copy-start = (bf16[144,2048]{1,0:T(8,128)(2,1)S(1)}, bf16[144,2048]{1,0:T(8,128)(2,1)}, u32[]{:S(2)}) copy-start(bf16[144,2048]{1,0:T(8,128)(2,1)} %v_ref.1) | copy-start | bytes 1769476
  9.3 15.8 %copy-start.1 = (bf16[144,2048]{1,0:T(8,128)(2,1)S(1)}, bf16[144,2048]{1,0:T(8,128)(2,1)}, u32[]{:S(2)}) copy-start(bf16[144,2048]{1,0:T(8,128)(2,1)} %q_ref.1) | copy-start | bytes 1769476
  9.3 15.7 %copy-start.2 = (bf16[144,2048]{1,0:T(8,128)(2,1)S(1)}, bf16[144,2048]{1,0:T(8,128)(2,1)}, u32[]{:S(2)}) copy-start(bf16[144,2048]{1,0:T(8,128)(2,1)} %k_ref.1) | copy-start | bytes 1769476
  21.9 21.4 %collective-permute-start = (bf16[144,1280]{1,0:T(8,128)(2,1)S(1)}, bf16[144,1280]{1,0:T(8,128)(2,1)S(1)}, u32[]{:S(2)}, u32[]{:S(2)}) collective-permute-start(bf16[144,1280]{1,0:T(8,128)(2,1)S(1)} %get-tuple-element.46), channel_id=1, source_target_pairs={{0,2},{2,4},{4,6},{6,8},{8,10},{10,12},{12,14},{14,16},{16,18},{18... | collective-permute-start | bytes 1105928 | tf_op jit(solution)/shard_map/ppermute | solution.py:536
  27.9 16.2 %collective-permute-start.4 = (bf16[144,768]{1,0:T(8,128)(2,1)S(1)}, bf16[144,768]{1,0:T(8,128)(2,1)S(1)}, u32[]{:S(2)}, u32[]{:S(2)}) collective-permute-start(bf16[144,768]{1,0:T(8,128)(2,1)S(1)} %get-tuple-element.66), channel_id=1, source_target_pairs={{0,2},{2,4},{4,6},{6,8},{8,10},{10,12},{12,14},{14,16},{16,18},{18... | collective-permute-start | bytes 663560 | tf_op jit(solution)/shard_map/ppermute | solution.py:536
  38.3 3.8 %collective-permute-start.3 = (f32[2,144,128]{2,1,0:T(8,128)S(1)}, f32[2,144,128]{2,1,0:T(8,128)S(1)}, u32[]{:S(2)}, u32[]{:S(2)}) collective-permute-start(f32[2,144,128]{2,1,0:T(8,128)S(1)} %get-tuple-element.57.refs_0_), channel_id=1, source_target_pairs={{0,1},{1,0},{2,3},{3,2},{4,5},{5,4},{6,7},{7,6},{8,9},{9,8},{10,11... | collective-permute-start | bytes 442376 | tf_op jit(solution)/shard_map/ppermute | solution.py:542
  44.4 2.5 %collective-permute-start.5 = (f32[1,144,128]{2,1,0:T(8,128)S(1)}, f32[1,144,128]{2,1,0:T(8,128)S(1)}, u32[]{:S(2)}, u32[]{:S(2)}) collective-permute-start(f32[1,144,128]{2,1,0:T(8,128)S(1)} %get-tuple-element.75.refs_0_), channel_id=1, source_target_pairs={{0,1},{1,0},{2,3},{3,2},{4,5},{5,4},{6,7},{7,6},{8,9},{9,8},{10,11... | collective-permute-start | bytes 221192 | tf_op jit(solution)/shard_map/ppermute | solution.py:542

commit v14 on v13

--- a/solution.py
+++ b/solution.py
@@ -512,7 +512,7 @@
         copy.wait()
 
 
-def normalize(squares, mixed, head=None, pieces=3):
+def normalize(squares, mixed, head=None, pieces=1):
     rows, channels = mixed[0].shape
     count = len(mixed)
     operands = (*squares, *mixed) + (() if head is None else (head,))

time: 48.1 us -> 48.1 us (level)
  no operation moved by 1% of the time
where the time goes in v14:
time: 48.1 us; the launch traced here: 47.9 us
  Pallas kernels  27.5 us (57%)
  starting transfers between devices  16.8 us (35%)
  waiting for transfers between devices  2.73 us (6%)
  between operations  0.78 us (2%)
    pallas_call x1, Pallas kernels, own_part(): pl.pallas_call(functools.partial(own_kernel, per), out_shape=(mixed, mixe...  12.6 us
    ppermute x4, starting transfers between devices, from_behind(): lax.ppermute(value, 'ctx', [(source, source + 1) for source in range(coun...  12.5 us
    pallas_call x1, Pallas kernels, mix(): pl.pallas_call(mix_kernel, out_shape=(jax.ShapeDtypeStruct((8, channels),...  6.86 us
    ppermute x2, starting transfers between devices, of_panels(): lax.ppermute(square, 'panel', [(n, (n + shift) % count) for n in range(co...  4.36 us
    pallas_call x1, Pallas kernels, score(): pl.pallas_call(functools.partial(score_kernel, per), out_shape=(jax.Shape...  2.84 us
    pallas_call x1, Pallas kernels, pack(): pl.pallas_call(functools.partial(pack_kernel, per), out_shape=(jax.ShapeD...  2.41 us
    pallas_call x2, Pallas kernels, normalize(): pl.pallas_call(functools.partial(normalize_kernel, count, len(squares), p...  2.16 us
    ppermute x2, waiting for transfers between devices, of_panels(): lax.ppermute(square, 'panel', [(n, (n + shift) % count) for n in range(co...  1.92 us
  transfers between devices with their start and end apart: 6, of which 4 were waited for; matrix products, arithmetic and copies ran while one was open for 0% of the time, Pallas kernels for 55%

profile of v14, /device:TPU:9, one launch (start us, length us, event | category | flops | bytes accessed | tf_op | source)
XLA Modules:
  0.0 47.9 jit_solution(7240578231406800158)
XLA Ops:
  0.6 3.1 %collective-permute-start.2 = (bf16[144,2048]{1,0:T(8,128)(2,1)}, bf16[144,2048]{1,0:T(8,128)(2,1)S(1)}, u32[]{:S(2)}, u32[]{:S(2)}) collective-permute-start(bf16[144,2048]{1,0:T(8,128)(2,1)} %k_ref.1), channel_id=1, source_target_pairs={{0,2},{2,4},{4,6},{6,8},{8,10},{10,12},{12,14},{14,16},{16,18},{18... | collective-permute-start | bytes 1769480 | tf_op jit(solution)/shard_map/ppermute | solution.py:536
  3.8 2.4 %pack.1 = (bf16[2320,128]{1,0:T(8,128)(2,1)S(1)}, f32[3,3,2048]{2,1,0:T(4,128)S(1)}, f32[3,3,2048]{2,1,0:T(4,128)S(1)}, f32[1,2048]{1,0:T(1,128)S(1)}, f32[7,204...) custom-call(bf16[3,144,2048]{2,1,0:T(8,128)(2,1)} %m_hbm_ref.1, ...), custom_call_target="tpu_custom_call" | custom-call | flops 5898240 | bytes 2949120 | tf_op jit(solution)/shard_map/pack/pallas_call | solution.py:163
  6.2 3.1 %collective-permute-start.1 = (bf16[2320,128]{1,0:T(8,128)(2,1)S(1)}, bf16[2320,128]{1,0:T(8,128)(2,1)S(1)}, u32[]{:S(2)}, u32[]{:S(2)}) collective-permute-start(bf16[2320,128]{1,0:T(8,128)(2,1)S(1)} %get-tuple-element.47), channel_id=1, source_target_pairs={{0,2},{2,4},{4,6},{6,8},{8,10},{10,12},{12,14},{14,16},{16,18},{18... | collective-permute-start | bytes 1781768 | tf_op jit(solution)/shard_map/ppermute | solution.py:536
  9.3 0.0 copy-start
  9.3 0.0 copy-start.1
  9.3 0.0 copy-start.2
  9.3 12.6 %own_part.1 = (f32[144,2048]{1,0:T(8,128)S(1)}, f32[144,2048]{1,0:T(8,128)S(1)}, f32[144,2048]{1,0:T(8,128)S(1)}, f32[144,128]{1,0:T(8,128)S(1)}, f32[128,2048]{1,0:T(8,128)S(1)}, /*index=5*/f32[6,8,2048]{2,1,0:T(8,128)S(1)}) custom-call(bf16[3,144,2048]{2,1,0:T(8,128)(2,1)} %m_hbm_ref.1, bf16[3,144,2048]{2,1,0:T(8,128)(2,1)} %s_hbm_ref.1, ...), custom_call_target="tpu_custom_call" | custom-call | flops 53084160 | bytes 7077888 | tf_op jit(solution)/shard_map/own_part/pallas_call | solution.py:277
  21.9 3.1 %collective-permute-start = (bf16[144,1280]{1,0:T(8,128)(2,1)S(1)}, bf16[144,1280]{1,0:T(8,128)(2,1)S(1)}, u32[]{:S(2)}, u32[]{:S(2)}) collective-permute-start(bf16[144,1280]{1,0:T(8,128)(2,1)S(1)} %get-tuple-element.46), channel_id=1, source_target_pairs={{0,2},{2,4},{4,6},{6,8},{8,10},{10,12},{12,14},{14,16},{16,18},{18... | collective-permute-start | bytes 1105928 | tf_op jit(solution)/shard_map/ppermute | solution.py:536
  25.0 0.0 collective-permute-done.2.before_ref
  25.1 0.0 copy-done
  25.1 0.0 copy-done.1
  25.1 0.0 copy-done.2
  25.1 2.8 %score.1 = (bf16[16,144,144]{2,1,0:T(8,128)(2,1)S(1)}, f32[144,2048]{1,0:T(8,128)S(1)}, f32[144,2048]{1,0:T(8,128)S(1)}, f32[1,144,128]{2,1,0:T(8,128)S(1)}) custom-call(bf16[144,2048]{1,0:T(8,128)(2,1)S(1)} %copy-done.1, bf16[144,2048]{1,0:T(8,128)(2,1)S(1)} %copy-done.2, bf16[144,2048]{1,0:T(8,128)(2,1)S(1)} %collective-permute-done.2.before_ref, ...), custom_call_target="tpu_custom_call" | custom-call | flops 339738624 | bytes 4128768 | tf_op jit(solution)/shard_map/score/pallas_call | solution.py:434
  27.9 3.1 %collective-permute-start.4 = (bf16[144,768]{1,0:T(8,128)(2,1)S(1)}, bf16[144,768]{1,0:T(8,128)(2,1)S(1)}, u32[]{:S(2)}, u32[]{:S(2)}) collective-permute-start(bf16[144,768]{1,0:T(8,128)(2,1)S(1)} %get-tuple-element.66), channel_id=1, source_target_pairs={{0,2},{2,4},{4,6},{6,8},{8,10},{10,12},{12,14},{14,16},{16,18},{18... | collective-permute-start | bytes 663560 | tf_op jit(solution)/shard_map/ppermute | solution.py:536
  31.1 0.4 collective-permute-done.1.packet_ref
  31.5 6.9 %mix.1 = (f32[8,2048]{1,0:T(8,128)S(1)}, f32[144,2048]{1,0:T(8,128)S(1)}, f32[2,144,128]{2,1,0:T(8,128)S(1)}) custom-call(bf16[2320,128]{1,0:T(8,128)(2,1)S(1)} %collective-permute-done.1.packet_ref, f32[144,2048]{1,0:T(8,128)S(1)} %get-tuple-element.52.own_ref, f32[144,2048]{1,0:T(8,128)S(1)} %get-tuple-element.53.z0_ref, ...), custom_call_target="tpu_custom_call" | custom-call | flops 1 | bytes 1 | tf_op jit(solution)/shard_map/mix/pallas_call | solution.py:377
  38.3 2.8 %collective-permute-start.3 = (f32[2,144,128]{2,1,0:T(8,128)S(1)}, f32[2,144,128]{2,1,0:T(8,128)S(1)}, u32[]{:S(2)}, u32[]{:S(2)}) collective-permute-start(f32[2,144,128]{2,1,0:T(8,128)S(1)} %get-tuple-element.57.refs_0_), channel_id=1, source_target_pairs={{0,1},{1,0},{2,3},{3,2},{4,5},{5,4},{6,7},{7,6},{8,9},{9,8},{10,11... | collective-permute-start | bytes 442376 | tf_op jit(solution)/shard_map/ppermute | solution.py:542
  41.1 1.0 %collective-permute-done.3.refs_1_ = f32[2,144,128]{2,1,0:T(8,128)S(1)} collective-permute-done((f32[2,144,128]{2,1,0:T(8,128)S(1)}, f32[2,144,128]{2,1,0:T(8,128)S(1)}, u32[]{:S(2)}, u32[]{:S(2)}) %collective-permute-start.3) | collective-permute-done | bytes 147488 | tf_op jit(solution)/shard_map/ppermute | solution.py:542
  42.1 1.2 %normalize.2 = (bf16[144,2048]{1,0:T(8,128)(2,1)}, bf16[144,2048]{1,0:T(8,128)(2,1)}) custom-call(f32[2,144,128]{2,1,0:T(8,128)S(1)} %get-tuple-element.57.refs_0_, f32[2,144,128]{2,1,0:T(8,128)S(1)} %collective-permute-done.3.refs_1_, f32[144,2048]{1,0:T(8,128)S(1)} %get-tuple-element.58.refs_2_, f32[144,2048]{1,0:T(8,128)S(1)} %get-tuple-element.59.refs_3_, ...), custom_call_target="tpu_custom_call" | custom-call | flops 1 | bytes 1 | tf_op jit(solution)/shard_map/normalize/pallas_call | solution.py:519
  43.3 0.0 collective-permute-done.before_ref
  43.3 0.4 value_mix.2
  43.7 0.4 collective-permute-done.4.before_ref
  44.1 0.3 value_mix.3
  44.4 1.6 %collective-permute-start.5 = (f32[1,144,128]{2,1,0:T(8,128)S(1)}, f32[1,144,128]{2,1,0:T(8,128)S(1)}, u32[]{:S(2)}, u32[]{:S(2)}) collective-permute-start(f32[1,144,128]{2,1,0:T(8,128)S(1)} %get-tuple-element.75.refs_0_), channel_id=1, source_target_pairs={{0,1},{1,0},{2,3},{3,2},{4,5},{5,4},{6,7},{7,6},{8,9},{9,8},{10,11... | collective-permute-start | bytes 221192 | tf_op jit(solution)/shard_map/ppermute | solution.py:542
  46.0 0.9 %collective-permute-done.5.refs_1_ = f32[1,144,128]{2,1,0:T(8,128)S(1)} collective-permute-done((f32[1,144,128]{2,1,0:T(8,128)S(1)}, f32[1,144,128]{2,1,0:T(8,128)S(1)}, u32[]{:S(2)}, u32[]{:S(2)}) %collective-permute-start.5) | collective-permute-done | bytes 73760 | tf_op jit(solution)/shard_map/ppermute | solution.py:542
  46.9 1.0 %normalize.3 = bf16[144,2048]{1,0:T(8,128)(2,1)} custom-call(f32[1,144,128]{2,1,0:T(8,128)S(1)} %get-tuple-element.75.refs_0_, f32[1,144,128]{2,1,0:T(8,128)S(1)} %collective-permute-done.5.refs_1_, f32[144,2048]{1,0:T(8,128)S(1)} %get-tuple-element.76.refs_2_), custom_call_target="tpu_custom_call" | custom-call | flops 1 | bytes 1 | tf_op jit(solution)/shard_map/normalize/pallas_call | solution.py:519
Async XLA Ops:
  0.6 24.4 %collective-permute-start.2 = (bf16[144,2048]{1,0:T(8,128)(2,1)}, bf16[144,2048]{1,0:T(8,128)(2,1)S(1)}, u32[]{:S(2)}, u32[]{:S(2)}) collective-permute-start(bf16[144,2048]{1,0:T(8,128)(2,1)} %k_ref.1), channel_id=1, source_target_pairs={{0,2},{2,4},{4,6},{6,8},{8,10},{10,12},{12,14},{14,16},{16,18},{18... | collective-permute-start | bytes 1769480 | tf_op jit(solution)/shard_map/ppermute | solution.py:536
  6.2 25.3 %collective-permute-start.1 = (bf16[2320,128]{1,0:T(8,128)(2,1)S(1)}, bf16[2320,128]{1,0:T(8,128)(2,1)S(1)}, u32[]{:S(2)}, u32[]{:S(2)}) collective-permute-start(bf16[2320,128]{1,0:T(8,128)(2,1)S(1)} %get-tuple-element.47), channel_id=1, source_target_pairs={{0,2},{2,4},{4,6},{6,8},{8,10},{10,12},{12,14},{14,16},{16,18},{18... | collective-permute-start | bytes 1781768 | tf_op jit(solution)/shard_map/ppermute | solution.py:536
  9.3 15.8 %copy-start = (bf16[144,2048]{1,0:T(8,128)(2,1)S(1)}, bf16[144,2048]{1,0:T(8,128)(2,1)}, u32[]{:S(2)}) copy-start(bf16[144,2048]{1,0:T(8,128)(2,1)} %v_ref.1) | copy-start | bytes 1769476
  9.3 15.8 %copy-start.1 = (bf16[144,2048]{1,0:T(8,128)(2,1)S(1)}, bf16[144,2048]{1,0:T(8,128)(2,1)}, u32[]{:S(2)}) copy-start(bf16[144,2048]{1,0:T(8,128)(2,1)} %q_ref.1) | copy-start | bytes 1769476
  9.3 15.7 %copy-start.2 = (bf16[144,2048]{1,0:T(8,128)(2,1)S(1)}, bf16[144,2048]{1,0:T(8,128)(2,1)}, u32[]{:S(2)}) copy-start(bf16[144,2048]{1,0:T(8,128)(2,1)} %k_ref.1) | copy-start | bytes 1769476
  21.9 21.4 %collective-permute-start = (bf16[144,1280]{1,0:T(8,128)(2,1)S(1)}, bf16[144,1280]{1,0:T(8,128)(2,1)S(1)}, u32[]{:S(2)}, u32[]{:S(2)}) collective-permute-start(bf16[144,1280]{1,0:T(8,128)(2,1)S(1)} %get-tuple-element.46), channel_id=1, source_target_pairs={{0,2},{2,4},{4,6},{6,8},{8,10},{10,12},{12,14},{14,16},{16,18},{18... | collective-permute-start | bytes 1105928 | tf_op jit(solution)/shard_map/ppermute | solution.py:536
  27.9 16.2 %collective-permute-start.4 = (bf16[144,768]{1,0:T(8,128)(2,1)S(1)}, bf16[144,768]{1,0:T(8,128)(2,1)S(1)}, u32[]{:S(2)}, u32[]{:S(2)}) collective-permute-start(bf16[144,768]{1,0:T(8,128)(2,1)S(1)} %get-tuple-element.66), channel_id=1, source_target_pairs={{0,2},{2,4},{4,6},{6,8},{8,10},{10,12},{12,14},{14,16},{16,18},{18... | collective-permute-start | bytes 663560 | tf_op jit(solution)/shard_map/ppermute | solution.py:536
  38.3 3.8 %collective-permute-start.3 = (f32[2,144,128]{2,1,0:T(8,128)S(1)}, f32[2,144,128]{2,1,0:T(8,128)S(1)}, u32[]{:S(2)}, u32[]{:S(2)}) collective-permute-start(f32[2,144,128]{2,1,0:T(8,128)S(1)} %get-tuple-element.57.refs_0_), channel_id=1, source_target_pairs={{0,1},{1,0},{2,3},{3,2},{4,5},{5,4},{6,7},{7,6},{8,9},{9,8},{10,11... | collective-permute-start | bytes 442376 | tf_op jit(solution)/shard_map/ppermute | solution.py:542
  44.4 2.5 %collective-permute-start.5 = (f32[1,144,128]{2,1,0:T(8,128)S(1)}, f32[1,144,128]{2,1,0:T(8,128)S(1)}, u32[]{:S(2)}, u32[]{:S(2)}) collective-permute-start(f32[1,144,128]{2,1,0:T(8,128)S(1)} %get-tuple-element.75.refs_0_), channel_id=1, source_target_pairs={{0,1},{1,0},{2,3},{3,2},{4,5},{5,4},{6,7},{7,6},{8,9},{9,8},{10,11... | collective-permute-start | bytes 221192 | tf_op jit(solution)/shard_map/ppermute | solution.py:542

commit v15 on v14

--- a/solution.py
+++ b/solution.py
@@ -109,7 +109,7 @@
         pltpu.make_async_copy(filter_hbm_ref, filter_ref, late_sems.at[3]),
     ]
     for copy in copies:
-        copy.start()
+        copy.start(priority=1)
     for copy in copies[:first]:
         copy.wait()
     last_ref[...] = jnp.zeros_like(last_ref)
@@ -146,7 +146,7 @@
         copies[first + n].wait()
         if n == 0:
             for copy in late:
-                copy.start()
+                copy.start(priority=1)
         pl.loop(n * per, (n + 1) * per)(one)
 
     out_ref[out_ref.shape[0] - 16 :, :] = last_ref[...].astype(BF16)

time: 48.1 us -> 48.1 us (level)
  no operation moved by 1% of the time
where the time goes in v15:
time: 48.1 us; the launch traced here: 47.9 us
  Pallas kernels  27.5 us (57%)
  starting transfers between devices  16.8 us (35%)
  waiting for transfers between devices  2.73 us (6%)
  between operations  0.78 us (2%)
    pallas_call x1, Pallas kernels, own_part(): pl.pallas_call(functools.partial(own_kernel, per), out_shape=(mixed, mixe...  12.6 us
    ppermute x4, starting transfers between devices, from_behind(): lax.ppermute(value, 'ctx', [(source, source + 1) for source in range(coun...  12.5 us
    pallas_call x1, Pallas kernels, mix(): pl.pallas_call(mix_kernel, out_shape=(jax.ShapeDtypeStruct((8, channels),...  6.86 us
    ppermute x2, starting transfers between devices, of_panels(): lax.ppermute(square, 'panel', [(n, (n + shift) % count) for n in range(co...  4.36 us
    pallas_call x1, Pallas kernels, score(): pl.pallas_call(functools.partial(score_kernel, per), out_shape=(jax.Shape...  2.84 us
    pallas_call x1, Pallas kernels, pack(): pl.pallas_call(functools.partial(pack_kernel, per), out_shape=(jax.ShapeD...  2.41 us
    pallas_call x2, Pallas kernels, normalize(): pl.pallas_call(functools.partial(normalize_kernel, count, len(squares), p...  2.16 us
    ppermute x2, waiting for transfers between devices, of_panels(): lax.ppermute(square, 'panel', [(n, (n + shift) % count) for n in range(co...  1.92 us
  transfers between devices with their start and end apart: 6, of which 4 were waited for; matrix products, arithmetic and copies ran while one was open for 0% of the time, Pallas kernels for 55%

profile of v15, /device:TPU:9, one launch (start us, length us, event | category | flops | bytes accessed | tf_op | source)
XLA Modules:
  0.0 47.9 jit_solution(17496372282787524517)
XLA Ops:
  0.6 3.1 %collective-permute-start.2 = (bf16[144,2048]{1,0:T(8,128)(2,1)}, bf16[144,2048]{1,0:T(8,128)(2,1)S(1)}, u32[]{:S(2)}, u32[]{:S(2)}) collective-permute-start(bf16[144,2048]{1,0:T(8,128)(2,1)} %k_ref.1), channel_id=1, source_target_pairs={{0,2},{2,4},{4,6},{6,8},{8,10},{10,12},{12,14},{14,16},{16,18},{18... | collective-permute-start | bytes 1769480 | tf_op jit(solution)/shard_map/ppermute | solution.py:536
  3.8 2.4 %pack.1 = (bf16[2320,128]{1,0:T(8,128)(2,1)S(1)}, f32[3,3,2048]{2,1,0:T(4,128)S(1)}, f32[3,3,2048]{2,1,0:T(4,128)S(1)}, f32[1,2048]{1,0:T(1,128)S(1)}, f32[7,204...) custom-call(bf16[3,144,2048]{2,1,0:T(8,128)(2,1)} %m_hbm_ref.1, ...), custom_call_target="tpu_custom_call" | custom-call | flops 5898240 | bytes 2949120 | tf_op jit(solution)/shard_map/pack/pallas_call | solution.py:163
  6.2 3.1 %collective-permute-start.1 = (bf16[2320,128]{1,0:T(8,128)(2,1)S(1)}, bf16[2320,128]{1,0:T(8,128)(2,1)S(1)}, u32[]{:S(2)}, u32[]{:S(2)}) collective-permute-start(bf16[2320,128]{1,0:T(8,128)(2,1)S(1)} %get-tuple-element.47), channel_id=1, source_target_pairs={{0,2},{2,4},{4,6},{6,8},{8,10},{10,12},{12,14},{14,16},{16,18},{18... | collective-permute-start | bytes 1781768 | tf_op jit(solution)/shard_map/ppermute | solution.py:536
  9.3 0.0 copy-start
  9.3 0.0 copy-start.1
  9.3 0.0 copy-start.2
  9.3 12.6 %own_part.1 = (f32[144,2048]{1,0:T(8,128)S(1)}, f32[144,2048]{1,0:T(8,128)S(1)}, f32[144,2048]{1,0:T(8,128)S(1)}, f32[144,128]{1,0:T(8,128)S(1)}, f32[128,2048]{1,0:T(8,128)S(1)}, /*index=5*/f32[6,8,2048]{2,1,0:T(8,128)S(1)}) custom-call(bf16[3,144,2048]{2,1,0:T(8,128)(2,1)} %m_hbm_ref.1, bf16[3,144,2048]{2,1,0:T(8,128)(2,1)} %s_hbm_ref.1, ...), custom_call_target="tpu_custom_call" | custom-call | flops 53084160 | bytes 7077888 | tf_op jit(solution)/shard_map/own_part/pallas_call | solution.py:277
  21.9 3.1 %collective-permute-start = (bf16[144,1280]{1,0:T(8,128)(2,1)S(1)}, bf16[144,1280]{1,0:T(8,128)(2,1)S(1)}, u32[]{:S(2)}, u32[]{:S(2)}) collective-permute-start(bf16[144,1280]{1,0:T(8,128)(2,1)S(1)} %get-tuple-element.46), channel_id=1, source_target_pairs={{0,2},{2,4},{4,6},{6,8},{8,10},{10,12},{12,14},{14,16},{16,18},{18... | collective-permute-start | bytes 1105928 | tf_op jit(solution)/shard_map/ppermute | solution.py:536
  25.0 0.0 collective-permute-done.2.before_ref
  25.1 0.0 copy-done
  25.1 0.0 copy-done.1
  25.1 0.0 copy-done.2
  25.1 2.8 %score.1 = (bf16[16,144,144]{2,1,0:T(8,128)(2,1)S(1)}, f32[144,2048]{1,0:T(8,128)S(1)}, f32[144,2048]{1,0:T(8,128)S(1)}, f32[1,144,128]{2,1,0:T(8,128)S(1)}) custom-call(bf16[144,2048]{1,0:T(8,128)(2,1)S(1)} %copy-done.1, bf16[144,2048]{1,0:T(8,128)(2,1)S(1)} %copy-done.2, bf16[144,2048]{1,0:T(8,128)(2,1)S(1)} %collective-permute-done.2.before_ref, ...), custom_call_target="tpu_custom_call" | custom-call | flops 339738624 | bytes 4128768 | tf_op jit(solution)/shard_map/score/pallas_call | solution.py:434
  27.9 3.1 %collective-permute-start.4 = (bf16[144,768]{1,0:T(8,128)(2,1)S(1)}, bf16[144,768]{1,0:T(8,128)(2,1)S(1)}, u32[]{:S(2)}, u32[]{:S(2)}) collective-permute-start(bf16[144,768]{1,0:T(8,128)(2,1)S(1)} %get-tuple-element.66), channel_id=1, source_target_pairs={{0,2},{2,4},{4,6},{6,8},{8,10},{10,12},{12,14},{14,16},{16,18},{18... | collective-permute-start | bytes 663560 | tf_op jit(solution)/shard_map/ppermute | solution.py:536
  31.1 0.4 collective-permute-done.1.packet_ref
  31.5 6.9 %mix.1 = (f32[8,2048]{1,0:T(8,128)S(1)}, f32[144,2048]{1,0:T(8,128)S(1)}, f32[2,144,128]{2,1,0:T(8,128)S(1)}) custom-call(bf16[2320,128]{1,0:T(8,128)(2,1)S(1)} %collective-permute-done.1.packet_ref, f32[144,2048]{1,0:T(8,128)S(1)} %get-tuple-element.52.own_ref, f32[144,2048]{1,0:T(8,128)S(1)} %get-tuple-element.53.z0_ref, ...), custom_call_target="tpu_custom_call" | custom-call | flops 1 | bytes 1 | tf_op jit(solution)/shard_map/mix/pallas_call | solution.py:377
  38.3 2.8 %collective-permute-start.3 = (f32[2,144,128]{2,1,0:T(8,128)S(1)}, f32[2,144,128]{2,1,0:T(8,128)S(1)}, u32[]{:S(2)}, u32[]{:S(2)}) collective-permute-start(f32[2,144,128]{2,1,0:T(8,128)S(1)} %get-tuple-element.57.refs_0_), channel_id=1, source_target_pairs={{0,1},{1,0},{2,3},{3,2},{4,5},{5,4},{6,7},{7,6},{8,9},{9,8},{10,11... | collective-permute-start | bytes 442376 | tf_op jit(solution)/shard_map/ppermute | solution.py:542
  41.1 1.0 %collective-permute-done.3.refs_1_ = f32[2,144,128]{2,1,0:T(8,128)S(1)} collective-permute-done((f32[2,144,128]{2,1,0:T(8,128)S(1)}, f32[2,144,128]{2,1,0:T(8,128)S(1)}, u32[]{:S(2)}, u32[]{:S(2)}) %collective-permute-start.3) | collective-permute-done | bytes 147488 | tf_op jit(solution)/shard_map/ppermute | solution.py:542
  42.1 1.2 %normalize.2 = (bf16[144,2048]{1,0:T(8,128)(2,1)}, bf16[144,2048]{1,0:T(8,128)(2,1)}) custom-call(f32[2,144,128]{2,1,0:T(8,128)S(1)} %get-tuple-element.57.refs_0_, f32[2,144,128]{2,1,0:T(8,128)S(1)} %collective-permute-done.3.refs_1_, f32[144,2048]{1,0:T(8,128)S(1)} %get-tuple-element.58.refs_2_, f32[144,2048]{1,0:T(8,128)S(1)} %get-tuple-element.59.refs_3_, ...), custom_call_target="tpu_custom_call" | custom-call | flops 1 | bytes 1 | tf_op jit(solution)/shard_map/normalize/pallas_call | solution.py:519
  43.3 0.0 collective-permute-done.before_ref
  43.3 0.4 value_mix.2
  43.7 0.4 collective-permute-done.4.before_ref
  44.1 0.3 value_mix.3
  44.4 1.6 %collective-permute-start.5 = (f32[1,144,128]{2,1,0:T(8,128)S(1)}, f32[1,144,128]{2,1,0:T(8,128)S(1)}, u32[]{:S(2)}, u32[]{:S(2)}) collective-permute-start(f32[1,144,128]{2,1,0:T(8,128)S(1)} %get-tuple-element.75.refs_0_), channel_id=1, source_target_pairs={{0,1},{1,0},{2,3},{3,2},{4,5},{5,4},{6,7},{7,6},{8,9},{9,8},{10,11... | collective-permute-start | bytes 221192 | tf_op jit(solution)/shard_map/ppermute | solution.py:542
  46.0 0.9 %collective-permute-done.5.refs_1_ = f32[1,144,128]{2,1,0:T(8,128)S(1)} collective-permute-done((f32[1,144,128]{2,1,0:T(8,128)S(1)}, f32[1,144,128]{2,1,0:T(8,128)S(1)}, u32[]{:S(2)}, u32[]{:S(2)}) %collective-permute-start.5) | collective-permute-done | bytes 73760 | tf_op jit(solution)/shard_map/ppermute | solution.py:542
  46.9 1.0 %normalize.3 = bf16[144,2048]{1,0:T(8,128)(2,1)} custom-call(f32[1,144,128]{2,1,0:T(8,128)S(1)} %get-tuple-element.75.refs_0_, f32[1,144,128]{2,1,0:T(8,128)S(1)} %collective-permute-done.5.refs_1_, f32[144,2048]{1,0:T(8,128)S(1)} %get-tuple-element.76.refs_2_), custom_call_target="tpu_custom_call" | custom-call | flops 1 | bytes 1 | tf_op jit(solution)/shard_map/normalize/pallas_call | solution.py:519
Async XLA Ops:
  0.6 24.4 %collective-permute-start.2 = (bf16[144,2048]{1,0:T(8,128)(2,1)}, bf16[144,2048]{1,0:T(8,128)(2,1)S(1)}, u32[]{:S(2)}, u32[]{:S(2)}) collective-permute-start(bf16[144,2048]{1,0:T(8,128)(2,1)} %k_ref.1), channel_id=1, source_target_pairs={{0,2},{2,4},{4,6},{6,8},{8,10},{10,12},{12,14},{14,16},{16,18},{18... | collective-permute-start | bytes 1769480 | tf_op jit(solution)/shard_map/ppermute | solution.py:536
  6.2 25.3 %collective-permute-start.1 = (bf16[2320,128]{1,0:T(8,128)(2,1)S(1)}, bf16[2320,128]{1,0:T(8,128)(2,1)S(1)}, u32[]{:S(2)}, u32[]{:S(2)}) collective-permute-start(bf16[2320,128]{1,0:T(8,128)(2,1)S(1)} %get-tuple-element.47), channel_id=1, source_target_pairs={{0,2},{2,4},{4,6},{6,8},{8,10},{10,12},{12,14},{14,16},{16,18},{18... | collective-permute-start | bytes 1781768 | tf_op jit(solution)/shard_map/ppermute | solution.py:536
  9.3 15.8 %copy-start = (bf16[144,2048]{1,0:T(8,128)(2,1)S(1)}, bf16[144,2048]{1,0:T(8,128)(2,1)}, u32[]{:S(2)}) copy-start(bf16[144,2048]{1,0:T(8,128)(2,1)} %v_ref.1) | copy-start | bytes 1769476
  9.3 15.8 %copy-start.1 = (bf16[144,2048]{1,0:T(8,128)(2,1)S(1)}, bf16[144,2048]{1,0:T(8,128)(2,1)}, u32[]{:S(2)}) copy-start(bf16[144,2048]{1,0:T(8,128)(2,1)} %q_ref.1) | copy-start | bytes 1769476
  9.3 15.7 %copy-start.2 = (bf16[144,2048]{1,0:T(8,128)(2,1)S(1)}, bf16[144,2048]{1,0:T(8,128)(2,1)}, u32[]{:S(2)}) copy-start(bf16[144,2048]{1,0:T(8,128)(2,1)} %k_ref.1) | copy-start | bytes 1769476
  21.9 21.4 %collective-permute-start = (bf16[144,1280]{1,0:T(8,128)(2,1)S(1)}, bf16[144,1280]{1,0:T(8,128)(2,1)S(1)}, u32[]{:S(2)}, u32[]{:S(2)}) collective-permute-start(bf16[144,1280]{1,0:T(8,128)(2,1)S(1)} %get-tuple-element.46), channel_id=1, source_target_pairs={{0,2},{2,4},{4,6},{6,8},{8,10},{10,12},{12,14},{14,16},{16,18},{18... | collective-permute-start | bytes 1105928 | tf_op jit(solution)/shard_map/ppermute | solution.py:536
  27.9 16.2 %collective-permute-start.4 = (bf16[144,768]{1,0:T(8,128)(2,1)S(1)}, bf16[144,768]{1,0:T(8,128)(2,1)S(1)}, u32[]{:S(2)}, u32[]{:S(2)}) collective-permute-start(bf16[144,768]{1,0:T(8,128)(2,1)S(1)} %get-tuple-element.66), channel_id=1, source_target_pairs={{0,2},{2,4},{4,6},{6,8},{8,10},{10,12},{12,14},{14,16},{16,18},{18... | collective-permute-start | bytes 663560 | tf_op jit(solution)/shard_map/ppermute | solution.py:536
  38.3 3.8 %collective-permute-start.3 = (f32[2,144,128]{2,1,0:T(8,128)S(1)}, f32[2,144,128]{2,1,0:T(8,128)S(1)}, u32[]{:S(2)}, u32[]{:S(2)}) collective-permute-start(f32[2,144,128]{2,1,0:T(8,128)S(1)} %get-tuple-element.57.refs_0_), channel_id=1, source_target_pairs={{0,1},{1,0},{2,3},{3,2},{4,5},{5,4},{6,7},{7,6},{8,9},{9,8},{10,11... | collective-permute-start | bytes 442376 | tf_op jit(solution)/shard_map/ppermute | solution.py:542
  44.4 2.5 %collective-permute-start.5 = (f32[1,144,128]{2,1,0:T(8,128)S(1)}, f32[1,144,128]{2,1,0:T(8,128)S(1)}, u32[]{:S(2)}, u32[]{:S(2)}) collective-permute-start(f32[1,144,128]{2,1,0:T(8,128)S(1)} %get-tuple-element.75.refs_0_), channel_id=1, source_target_pairs={{0,1},{1,0},{2,3},{3,2},{4,5},{5,4},{6,7},{7,6},{8,9},{9,8},{10,11... | collective-permute-start | bytes 221192 | tf_op jit(solution)/shard_map/ppermute | solution.py:542
